TPU v7x, 512 devices: a whole 4x8x8 slice. The times are simulated.
512 devices in a mesh: dp: 32 (over x_hi, z, core), fsdp: 16 (over x_lo, y).
Axes of the slice: x: 4 (x_hi: 2, x_lo: 2; x = x_hi * 2 + x_lo), y: 8, z: 8, core: 2. Of those that a mesh axis runs over, the one named last changes fastest.
Arguments:
- states: bfloat16 [512, 2, 128, 64], P(('dp', 'fsdp')), may hold values from -6 to 6
- adjoint: float32 [512, 128, 64], P(('dp', 'fsdp')), may hold values from -6 to 6
- grid_step_index: int32 [512], P(('dp', 'fsdp')), may hold values from 3 to 26
- input_weight: bfloat16 [64, 1536], replicated, may hold values from -0.75 to 0.75
- timestep_weight: bfloat16 [256, 4608], P('fsdp'), may hold values from -0.375 to 0.375
- query_key_value_weight: bfloat16 [1536, 2304], P('fsdp'), may hold values from -0.15625 to 0.15625
- projection_weight: bfloat16 [768, 1536], P('fsdp'), may hold values from -0.21875 to 0.21875
- down_factor: bfloat16 [768, 64], P('fsdp'), may hold values from -0.21875 to 0.21875
- up_factor: bfloat16 [64, 1536], P('fsdp'), may hold values from -0.75 to 0.75
- query_norm_gain: float32 [64], replicated, may hold values from 0.5 to 1.5
- key_norm_gain: float32 [64], replicated, may hold values from 0.5 to 1.5
- final_norm_gain: float32 [1536], replicated, may hold values from 0.1 to 1.9
- output_weight: bfloat16 [1536, 64], replicated, may hold values from -0.15625 to 0.15625
Outputs:
- adjoint_out: float32 [512, 128, 64], P(('dp', 'fsdp'))
- down_factor_gradient: float32 [768, 64], P('fsdp')
- up_factor_gradient: float32 [64, 1536], P('fsdp')
Inputs may be any that keep to these rules, and one draw needn't show every extreme that they name: `grid_step_index`: each sample's adjoint stands at grid time (k + 1) / 28.
All inputs are finite; a program needn't handle non-finite values.
Results may differ from a plain program's by a relative error of at most 0.019.
Values may be sent and summed in bfloat16 or wider, within the bound.
No kernel may reach another device: no remote copies, remote signals or barrier semaphores. Data moves between devices by JAX's collectives and lax.ppermute only.
A program may use at most 64 MiB of HBM per device.

v0:
```python
from functools import partial
import math

import jax
import jax.numpy as jnp
from jax import lax
from jax.sharding import PartitionSpec as P

HEADS = 12
HEAD_DIM = 64
TIME_FEAT = 256
STEPS = 28


def normalize(values):
    return values * lax.rsqrt(jnp.mean(values * values, axis=-1, keepdims=True) + 1e-06)


def time_features(upper_time):
    halves = TIME_FEAT // 2
    frequency = jnp.exp(-math.log(10000.0) * jnp.arange(halves, dtype=jnp.float32) / halves)
    angles = 1000.0 * upper_time * frequency
    return jnp.concatenate([jnp.cos(angles), jnp.sin(angles)]).astype(jnp.bfloat16)


def modulation(upper_time, timestep_weight, width):
    mod_all = jnp.dot(
        time_features(upper_time)[None, :], timestep_weight, preferred_element_type=jnp.float32
    )[0]
    return (mod_all[:width], mod_all[width : 2 * width], mod_all[2 * width :])


def prelude(latent, input_weight, shift_vec, scale_vec):
    hidden_state = jnp.dot(
        latent.astype(jnp.bfloat16), input_weight, preferred_element_type=jnp.float32
    )
    normed = (normalize(hidden_state) * (1.0 + scale_vec) + shift_vec).astype(jnp.bfloat16)
    return (hidden_state, normed)


def mixing(query_key_value_rows, query_norm_gain, key_norm_gain, inner_width):
    tokens_here = query_key_value_rows.shape[0]
    shaped = (tokens_here, HEADS, HEAD_DIM)
    queries = (
        normalize(query_key_value_rows[:, :inner_width].reshape(shaped)) * query_norm_gain
    ).astype(jnp.bfloat16)
    keyset = (
        normalize(query_key_value_rows[:, inner_width : 2 * inner_width].reshape(shaped))
        * key_norm_gain
    ).astype(jnp.bfloat16)
    valueset = query_key_value_rows[:, 2 * inner_width :].reshape(shaped).astype(jnp.bfloat16)
    scores = jnp.einsum(
        "qhd,khd->hqk", queries, keyset, preferred_element_type=jnp.float32
    ) / math.sqrt(HEAD_DIM)
    expscore = jnp.exp(scores)
    attention = (expscore / jnp.sum(expscore, axis=-1, keepdims=True)).astype(jnp.bfloat16)
    blended_mix = jnp.einsum(
        "hqk,khd->qhd", attention, valueset, preferred_element_type=jnp.float32
    )
    return blended_mix.reshape(tokens_here, inner_width).astype(jnp.bfloat16)


def finish(projected, hidden_state, gate_vector, final_norm_gain, output_weight):
    normed = (normalize(hidden_state + gate_vector * projected) * final_norm_gain).astype(
        jnp.bfloat16
    )
    return jnp.dot(normed, output_weight, preferred_element_type=jnp.float32)


def advance_step(
    query_key_value_rows,
    hidden_state,
    backward_preamble,
    current_adjoint,
    upper_time,
    gate_vector,
    query_key_value_weight,
    projection_weight,
    down_factor,
    up_factor,
    query_norm_gain,
    key_norm_gain,
    final_norm_gain,
    output_weight,
    sample_batch,
):
    inner_width = projection_weight.shape[0]
    blended_mix, back_mix = jax.vjp(
        partial(
            mixing,
            query_norm_gain=query_norm_gain,
            key_norm_gain=key_norm_gain,
            inner_width=inner_width,
        ),
        query_key_value_rows,
    )
    base_projection = jnp.dot(blended_mix, projection_weight, preferred_element_type=jnp.float32)
    lowrank_update = jnp.dot(blended_mix, down_factor, preferred_element_type=jnp.float32).astype(
        jnp.bfloat16
    )
    adjusted_projection = base_projection + jnp.dot(
        lowrank_update, up_factor, preferred_element_type=jnp.float32
    )
    tail = partial(
        finish,
        gate_vector=gate_vector,
        final_norm_gain=final_norm_gain,
        output_weight=output_weight,
    )
    base_vel, back_base = jax.vjp(tail, base_projection, hidden_state)
    adjusted_vel, back_adjusted = jax.vjp(
        lambda projected: tail(projected, hidden_state), adjusted_projection
    )
    sigma = jnp.sqrt(2.0 * (1.0 - upper_time) / upper_time)
    residual = 2.0 / sigma * (adjusted_vel - base_vel) + sigma * current_adjoint
    adjusted_gradient = back_adjusted(4.0 * residual / (sigma * sample_batch))[0].astype(
        jnp.bfloat16
    )
    up_factor_gradient = jnp.dot(
        lowrank_update.T, adjusted_gradient, preferred_element_type=jnp.float32
    )
    lowrank_gradient = jnp.dot(
        adjusted_gradient, up_factor.T, preferred_element_type=jnp.float32
    ).astype(jnp.bfloat16)
    down_factor_gradient = jnp.dot(
        blended_mix.T, lowrank_gradient, preferred_element_type=jnp.float32
    )
    proj_grad, hidden_grad = back_base(current_adjoint)
    blend_grad = jnp.dot(
        proj_grad.astype(jnp.bfloat16), projection_weight.T, preferred_element_type=jnp.float32
    ).astype(jnp.bfloat16)
    qkv_grad = back_mix(blend_grad)[0]
    normed_grad = jnp.dot(
        qkv_grad.astype(jnp.bfloat16), query_key_value_weight.T, preferred_element_type=jnp.float32
    ).astype(jnp.bfloat16)
    latent_grad = backward_preamble((hidden_grad, normed_grad))[0]
    adjoint_next = current_adjoint + (2.0 * latent_grad - current_adjoint / upper_time) / STEPS
    return (adjoint_next, down_factor_gradient, up_factor_gradient)


def per_device(
    states,
    adjoint,
    grid_step_index,
    input_weight,
    timestep_weight,
    query_key_value_weight,
    projection_weight,
    down_factor,
    up_factor,
    query_norm_gain,
    key_norm_gain,
    final_norm_gain,
    output_weight,
):
    sample_batch = lax.axis_size("dp") * lax.axis_size("fsdp") * states.shape[0]
    sample_step = grid_step_index[0]
    tokens_here = states.shape[2]
    width = input_weight.shape[1]
    time_full, proj_full, down_full, up_full = (
        lax.all_gather(timestep_weight, "fsdp", axis=0, tiled=True),
        lax.all_gather(projection_weight, "fsdp", axis=0, tiled=True),
        lax.all_gather(down_factor, "fsdp", axis=0, tiled=True),
        lax.all_gather(up_factor, "fsdp", axis=0, tiled=True),
    )
    times = [(sample_step + 1 - turn_index).astype(jnp.float32) / STEPS for turn_index in range(2)]
    gates = []
    hiddens = []
    backs = []
    normeds = []
    for turn_index in range(2):
        shift_vec, scale_vec, gate_vector = modulation(times[turn_index], time_full, width)
        forward_output, backward_preamble = jax.vjp(
            partial(prelude, input_weight=input_weight, shift_vec=shift_vec, scale_vec=scale_vec),
            states[0, turn_index].astype(jnp.float32),
        )
        gates.append(gate_vector)
        hiddens.append(forward_output[0])
        normeds.append(forward_output[1])
        backs.append(backward_preamble)
    normed_both = jnp.concatenate(normeds, axis=0)
    row_block = lax.all_gather(query_key_value_weight, "fsdp", axis=0, tiled=True)
    total = jnp.dot(normed_both, row_block, preferred_element_type=jnp.float32)
    current_adjoint = adjoint[0]
    down_total = jnp.zeros(down_full.shape, jnp.float32)
    up_total = jnp.zeros(up_full.shape, jnp.float32)
    for turn_index in range(2):
        query_key_value_rows = total[turn_index * tokens_here : (turn_index + 1) * tokens_here]
        current_adjoint, down_factor_gradient, up_factor_gradient = advance_step(
            query_key_value_rows,
            hiddens[turn_index],
            backs[turn_index],
            current_adjoint,
            times[turn_index],
            gates[turn_index],
            row_block,
            proj_full,
            down_full,
            up_full,
            query_norm_gain,
            key_norm_gain,
            final_norm_gain,
            output_weight,
            sample_batch,
        )
        down_total = down_total + down_factor_gradient
        up_total = up_total + up_factor_gradient
    part_down, part_up = (
        lax.psum_scatter(
            down_total.astype(jnp.bfloat16), "fsdp", scatter_dimension=0, tiled=True
        ).astype(jnp.float32),
        lax.psum_scatter(
            up_total.astype(jnp.bfloat16), "fsdp", scatter_dimension=0, tiled=True
        ).astype(jnp.float32),
    )
    part_down, part_up = (
        lax.psum(part_down.astype(jnp.bfloat16), "dp").astype(jnp.float32),
        lax.psum(part_up.astype(jnp.bfloat16), "dp").astype(jnp.float32),
    )
    return (current_adjoint[None], part_down, part_up)


def solution(mesh):
    in_specs = (
        P(("dp", "fsdp"), None, None, None),
        P(("dp", "fsdp"), None, None),
        P(("dp", "fsdp")),
        P(),
        P("fsdp", None),
        P("fsdp", None),
        P("fsdp", None),
        P("fsdp", None),
        P("fsdp", None),
        P(),
        P(),
        P(),
        P(),
    )
    out_specs = (P(("dp", "fsdp"), None, None), P("fsdp", None), P("fsdp", None))
    return jax.shard_map(
        per_device, mesh=mesh, in_specs=in_specs, out_specs=out_specs, check_vma=False
    )
```

profile of v0, /device:TPU:1, one launch (start us, length us, event | category | flops | bytes accessed | tf_op | source)
XLA Modules:
  0.0 675.3 jit_solution(6327461827655405221)
XLA Ops:
  7.2 0.7 all-gather.5.cloned.1.call-update
  8.0 0.7 all-gather.7.cloned.1.call-update
  8.7 0.7 all-gather.9.cloned.1.call-update
  9.5 1.3 multiply_reduce_fusion.13
  10.8 1.6 multiply_reduce_fusion.12
  13.5 31.4 %all_gather.18 = bf16[768,64]{1,0:T(8,128)(2,1)} all-gather(bf16[48,64]{1,0:T(8,128)(2,1)S(1)} %copy-done.70), channel_id=1, replica_groups=mesh['dp'=32,'fsdp'=16] {'fsdp'}, dimensions={0}, use_global_device_ids=true | all-gather | bytes 104448 | tf_op jit(solution)/shard_map/all_gather | solution.py:163
  44.9 26.3 %all-gather = bf16[16,4,1536]{2,1,0:T(4,128)(2,1)S(1)} all-gather(bf16[1,4,1536]{2,1,0:T(4,128)(2,1)S(1)} %bitcast.170), channel_id=1, replica_groups=mesh['dp'=32,'fsdp'=16] {'fsdp'}, dimensions={0}, use_global_device_ids=true | all-gather | bytes 208896 | tf_op jit(solution)/shard_map/all_gather | solution.py:164
  71.2 1.3 dynamic-slice
  73.1 9.5 %all-gather.5.cloned.1.call-done = bf16[256,4608]{1,0:T(8,128)(2,1)} async-done(((bf16[16,4608]{1,0:T(8,128)(2,1)}), bf16[256,4608]{1,0:T(8,128)(2,1)}) %all-gather.5.cloned.1.call-update) | async-done | bytes 2359312 | tf_op jit(solution)/shard_map/all_gather | solution.py:161
  82.6 2.2 convolution_reduce_fusion.1
  84.9 0.6 fusion.129
  86.3 94.4 %all-gather.7.cloned.1.call-done = bf16[1536,2304]{1,0:T(8,128)(2,1)} async-done(((bf16[96,2304]{1,0:T(8,128)(2,1)}), bf16[1536,2304]{1,0:T(8,128)(2,1)}) %all-gather.7.cloned.1.call-update) | async-done | bytes 7077904 | tf_op jit(solution)/shard_map/all_gather | solution.py:182
  180.7 6.0 fusion.130
  186.7 1.0 fusion.126
  188.1 1.9 fusion.127
  190.8 0.7 multiply_divide_fusion.1
  191.7 55.2 %all-gather.9.cloned.1.call-done = bf16[768,1536]{1,0:T(8,128)(2,1)} async-done(((bf16[48,1536]{1,0:T(8,128)(2,1)}), bf16[768,1536]{1,0:T(8,128)(2,1)}) %all-gather.9.cloned.1.call-update) | async-done | bytes 2359312 | tf_op jit(solution)/shard_map/all_gather | solution.py:162
  247.0 2.2 fusion.135
  250.2 0.9 copy-done.8
  251.4 1.6 convolution_convert_fusion.12
  253.0 1.7 copy.62
  254.8 1.8 multiply_reduce_fusion.9
  256.7 1.8 multiply_reduce_fusion.18
  260.9 3.4 multiply_reduce_fusion.8
  264.8 1.9 copy.67
  266.7 1.9 copy.68
  268.6 1.0 multiply_reduce_fusion.16
  270.3 1.0 multiply_reduce_fusion.17
  271.9 2.4 fusion.132
  274.3 0.6 copy-done.65
  274.9 0.6 multiply_divide_fusion
  275.6 1.8 copy.66
  277.3 2.4 fusion.52
  280.6 0.9 copy-done.16
  282.0 0.8 copy-done.6
  283.2 1.6 convolution_convert_fusion.9
  284.8 1.9 copy.70
  286.7 1.7 multiply_reduce_fusion.5
  288.4 2.4 multiply_reduce_fusion.14
  290.8 1.8 multiply_reduce_fusion.15
  292.6 1.1 convolution_convert_fusion.8
  294.1 0.8 convolution_convert_fusion.21
  296.6 0.9 fusion.70
  297.5 3.0 multiply_reduce_fusion.2
  300.5 0.7 multiply_multiply_fusion.7
  301.2 1.4 fusion.55
  302.7 2.3 fusion.53
  304.9 1.7 fusion.137
  306.6 0.7 multiply_multiply_fusion.2
  307.3 0.7 multiply_multiply_fusion.3
  308.1 1.1 add_add_fusion.8
  309.3 6.4 multiply_reduce_fusion.4
  317.8 2.3 multiply_reduce_fusion
  320.2 0.8 multiply_multiply_fusion.6
  320.9 2.1 fusion.57
  323.0 2.4 fusion.21
  325.4 2.0 fusion.16
  327.6 2.4 fusion.47
  330.0 129.9 %all-reduce.10.cloned.1.call-done = bf16[64,1536]{1,0:T(8,128)(2,1)} async-done(((bf16[64,1536]{1,0:T(8,128)(2,1)}), bf16[64,1536]{1,0:T(8,128)(2,1)}) %all-reduce.10.cloned.1.call-update) | async-done | bytes 196624
  459.9 0.7 constant_dynamic-slice_fusion
  460.6 70.8 %reduce-scatter.2.cloned.1.call-done = bf16[48,64]{1,0:T(8,128)(2,1)} async-done(((bf16[768,64]{1,0:T(8,128)(2,1)}), bf16[48,64]{1,0:T(8,128)(2,1)}) %reduce-scatter.2.cloned.1.call-update) | async-done | bytes 6160 | tf_op jit(solution)/shard_map/reduce_scatter | solution.py:209
  531.4 136.1 %all-reduce.7 = (bf16[48,64]{1,0:T(8,128)(2,1)S(1)}, bf16[4,1536]{1,0:T(4,128)(2,1)S(1)}) all-reduce(bf16[48,64]{1,0:T(8,128)(2,1)} %reduce-scatter.2.cloned.1.call-done, bf16[4,1536]{1,0:T(4,128)(2,1)S(1)} %constant_dynamic-slice_fusion), channel_id=1, replica_groups=mesh['dp'=32,'fsdp'=16] {'dp'}, use_global_device_ids=true, to_apply=%region_25.0 | all-reduce | flops 9216 | bytes 36864 | tf_op jit(solution)/shard_map/psum | solution.py:217
  667.6 0.6 convert_element_type.307
  668.2 0.6 convert_element_type.309
  (245 shorter events, 13.5 us)
Async XLA Ops:
  7.2 242.1 %copy-start = (bf16[1536,64]{0,1:T(8,128)(2,1)S(1)}, bf16[1536,64]{0,1:T(8,128)(2,1)}, u32[]{:S(2)}) copy-start(bf16[1536,64]{0,1:T(8,128)(2,1)} %param.25) | copy-start | bytes 589828
  7.2 6.3 copy-start.70
  7.2 37.7 %copy-start.71 = (bf16[4,1536]{1,0:T(4,128)(2,1)S(1)}, bf16[4,1536]{1,0:T(4,128)(2,1)}, u32[]{:S(2)}) copy-start(bf16[4,1536]{1,0:T(4,128)(2,1)} %param.21) | copy-start | bytes 36868
  7.2 75.4 %all-gather.5.cloned.1.call-start = ((), (), s32[]{:S(2)}) async-start(), calls=%async_computation.1 | async-start | bytes 2506752 | tf_op jit(solution)/shard_map/all_gather | solution.py:161
  7.9 172.7 %all-gather.7.cloned.1.call-start = ((), (), s32[]{:S(2)}) async-start(), calls=%async_computation.2 | async-start | bytes 7520256 | tf_op jit(solution)/shard_map/all_gather | solution.py:182
  8.7 238.3 %all-gather.9.cloned.1.call-start = ((), (), s32[]{:S(2)}) async-start(), calls=%async_computation.3 | async-start | bytes 2506752 | tf_op jit(solution)/shard_map/all_gather | solution.py:162
  9.4 450.5 %all-reduce.10.cloned.1.call-start = ((), (), s32[]{:S(2)}) async-start(), calls=%async_computation.5 | async-start | bytes 393216
  10.8 34.1 %copy-start.91 = (f32[128]{0:T(128)}, f32[128]{0:T(128)S(1)}, u32[]{:S(2)}) copy-start(f32[128]{0:T(128)S(1)} %get-tuple-element.29) | copy-start | bytes 1540
  10.8 75.3 %copy-start.2 = (f32[128,1536]{1,0:T(8,128)}, f32[128,1536]{1,0:T(8,128)S(1)}, u32[]{:S(2)}) copy-start(f32[128,1536]{1,0:T(8,128)S(1)} %get-tuple-element.30) | copy-start | bytes 2359300
  12.4 32.5 %copy-start.89 = (f32[128]{0:T(128)}, f32[128]{0:T(128)S(1)}, u32[]{:S(2)}) copy-start(f32[128]{0:T(128)S(1)} %get-tuple-element.27) | copy-start | bytes 1540
  13.5 72.5 %copy-start.87 = (f32[128]{0:T(128)}, f32[128]{0:T(128)S(1)}, u32[]{:S(2)}) copy-start(f32[128]{0:T(128)S(1)} %fusion.113) | copy-start | bytes 1540
  13.5 72.6 %copy-start.88 = (f32[128]{0:T(128)}, f32[128]{0:T(128)S(1)}, u32[]{:S(2)}) copy-start(f32[128]{0:T(128)S(1)} %fusion.112) | copy-start | bytes 1540
  82.6 2.8 copy-start.10
  85.9 100.8 %copy-start.61 = (f32[1536]{0:T(1024)}, f32[1536]{0:T(1024)S(1)}, u32[]{:S(2)}) copy-start(f32[1536]{0:T(1024)S(1)} %get-tuple-element.19) | copy-start | bytes 18436
  187.7 2.6 copy-start.81
  187.7 2.6 copy-start.84
  187.9 3.8 copy-start.22
  188.1 3.6 copy-start.20
  190.7 56.3 %copy-start.26 = (f32[12,128,128]{1,2,0:T(8,128)}, f32[12,128,128]{1,2,0:T(8,128)S(1)}, u32[]{:S(2)}) copy-start(f32[12,128,128]{1,2,0:T(8,128)S(1)} %get-tuple-element.34) | copy-start | bytes 2359300
  190.7 56.3 %copy-start.68 = (f32[12,128]{1,0:T(8,128)}, f32[12,128]{1,0:T(8,128)S(1)}, u32[]{:S(2)}) copy-start(f32[12,128]{1,0:T(8,128)S(1)} %get-tuple-element.33) | copy-start | bytes 18436
  191.7 55.3 %copy-start.28 = (bf16[12,64,128]{2,1,0:T(8,128)(2,1)}, bf16[12,64,128]{2,1,0:T(8,128)(2,1)S(1)}, u32[]{:S(2)}) copy-start(bf16[12,64,128]{2,1,0:T(8,128)(2,1)S(1)} %convolution_convert_fusion.13) | copy-start | bytes 589828
  191.7 57.6 %copy-start.41 = (f32[1536]{0:T(1024)S(1)}, f32[1536]{0:T(1024)}, u32[]{:S(2)}) copy-start(f32[1536]{0:T(1024)} %param.24) | copy-start | bytes 18436
  247.0 2.3 copy-start.3
  247.0 2.3 copy-start.40
  247.0 2.3 copy-start.42
  249.3 2.2 copy-start.1
  254.8 5.6 slice-start
  256.6 1.9 copy-start.21
  256.6 1.9 copy-start.23
  256.6 1.9 copy-start.27
  256.6 1.9 copy-start.54
  258.5 1.9 slice-start.1
  260.9 3.4 copy-start.92
  269.7 2.2 copy-start.47
  271.9 2.4 copy-start.49
  277.3 2.5 copy-start.24
  277.3 2.5 copy-start.34
  277.3 2.5 copy-start.66
  280.0 1.9 copy-start.31
  284.8 3.6 copy-start.18
  284.8 3.6 copy-start.19
  284.8 3.6 copy-start.25
  288.4 2.5 copy-start.50
  288.4 2.4 copy-start.67
  288.4 2.4 copy-start.83
  288.4 2.4 copy-start.86
  292.6 2.4 copy-start.5
  292.6 2.4 copy-start.15
  292.6 2.4 copy-start.43
  293.7 3.8 copy-start.9
  301.2 7.9 %copy-start.39 = (f32[128,12,64]{0,2,1:T(8,128)S(1)}, f32[128,12,64]{0,2,1:T(8,128)}, u32[]{:S(2)}) copy-start(f32[128,12,64]{0,2,1:T(8,128)} %get-tuple-element.52) | copy-start | bytes 1179652
  302.6 6.5 copy-start.48
  302.6 6.6 copy-start.44
  302.6 6.6 copy-start.62
  309.3 6.4 copy-start.90
  309.3 6.9 %copy-start.17 = (f32[128,1536]{1,0:T(8,128)S(1)}, f32[128,1536]{1,0:T(8,128)}, u32[]{:S(2)}) copy-start(f32[128,1536]{1,0:T(8,128)} %copy-done.16) | copy-start | bytes 2359300
  309.3 6.9 %copy-start.45 = (bf16[128,64]{0,1:T(8,128)(2,1)S(1)}, bf16[128,64]{0,1:T(8,128)(2,1)}, u32[]{:S(2)}) copy-start(bf16[128,64]{0,1:T(8,128)(2,1)} %convolution_convert_fusion.21) | copy-start | bytes 49156
  315.7 2.1 copy-start.7
  315.7 2.1 copy-start.38
  315.7 2.1 copy-start.73
  320.1 7.4 %copy-start.12 = (f32[128,1536]{1,0:T(8,128)S(1)}, f32[128,1536]{1,0:T(8,128)}, u32[]{:S(2)}) copy-start(f32[128,1536]{1,0:T(8,128)} %copy-done.11) | copy-start | bytes 2359300
  320.1 7.4 %copy-start.74 = (f32[128]{0:T(128)S(1)}, f32[128]{0:T(128)}, u32[]{:S(2)}) copy-start(f32[128]{0:T(128)} %copy-done.72) | copy-start | bytes 1540
  320.2 7.4 %copy-start.77 = (f32[128]{0:T(128)S(1)}, f32[128]{0:T(128)}, u32[]{:S(2)}) copy-start(f32[128]{0:T(128)} %copy-done.76) | copy-start | bytes 1540
  327.5 203.9 %reduce-scatter.2.cloned.1.call-start = ((), (), s32[]{:S(2)}) async-start(), calls=%async_computation.4 | async-start | bytes 208896 | tf_op jit(solution)/shard_map/reduce_scatter | solution.py:209
  (38 other events, 41.7 us)
Sparse Core Ops, SparseCore 0:
  10.1 72.4 all-gather.4
  84.7 95.9 all-gather.6
  182.7 64.2 all-gather.8
  327.6 132.2 all-reduce.9
  462.7 68.6 reduce-scatter.1
where the time goes:
time: 680 us; the launch traced here: 675 us
  waiting for transfers between devices  362 us (53%)
  blocking collectives  194 us (29%)
  matrix products  64.5 us (9%)
  local copies, waits for them, and re-layouts  23.8 us (4%)
  between operations  16.5 us (2%)
  other arithmetic  14.6 us (2%)
    psum x1, blocking collectives, per_device(): lax.psum(part_down.astype(jnp.bfloat16), 'dp').astype(jnp.float32)  136 us
    unnamed x6, waiting for transfers between devices  132 us
    all_gather x1, waiting for transfers between devices, per_device(): lax.all_gather(query_key_value_weight, 'fsdp', axis=0, tiled=True)  94.4 us
    reduce_scatter x1, waiting for transfers between devices, per_device(): lax.psum_scatter(down_total.astype(jnp.bfloat16), 'fsdp', scatter_dimensi...  70.8 us
    all_gather x1, waiting for transfers between devices, per_device(): lax.all_gather(projection_weight, 'fsdp', axis=0, tiled=True)  55.2 us
    all_gather x1, blocking collectives, per_device(): lax.all_gather(down_factor, 'fsdp', axis=0, tiled=True)  31.4 us
    all_gather x1, blocking collectives, per_device(): lax.all_gather(up_factor, 'fsdp', axis=0, tiled=True)  26.3 us
  transfers between devices with their start and end apart: 5, of which 5 were waited for; matrix products, arithmetic and copies ran while one was open for 3% of the time, Pallas kernels for 0%

commit v1 on v0

v1 whole, which is shorter than its diff:
```python
import math

import jax
import jax.numpy as jnp
from jax import lax
from jax.experimental import pallas as pl
from jax.experimental.pallas import tpu as pltpu
from jax.sharding import PartitionSpec as P

HEAD_DIM = 64
TIME_FEAT = 256
STEPS = 28
LANES = 128
EPS = 1e-06
BF = jnp.bfloat16
F32 = jnp.float32


def dot_nn(a, b):
    return lax.dot_general(a, b, (((1,), (0,)), ((), ())), preferred_element_type=F32)


def dot_nt(a, b):
    return lax.dot_general(a, b, (((1,), (1,)), ((), ())), preferred_element_type=F32)


def dot_tn(a, b):
    return lax.dot_general(a, b, (((0,), (0,)), ((), ())), preferred_element_type=F32)


def step_pair_kernel(
    core_ref,
    coef_ref,
    own_ref,
    other_ref,
    normed_ref,
    hidden_ref,
    adjoint_ref,
    scale1_ref,
    gate_ref,
    down_ref,
    up_ref,
    qgain_ref,
    kgain_ref,
    fgain_ref,
    wout_ref,
    win_ref,
    adjoint_out_ref,
    down_out_ref,
    up_out_ref,
    weights,
    sems,
    qn,
    qz,
    qr,
    kn,
    kz,
    kr,
    vn,
    att,
    blended,
    base_u,
    adj_u,
    base_vel,
    adj_vel,
    lowrank,
    adj_grad,
    low_grad,
):
    tokens = adjoint_ref.shape[0]
    rows = 2 * tokens
    width = hidden_ref.shape[1]
    half = weights.shape[3]
    shards = weights.shape[1]
    per_qkv = width // shards
    inner = 2 * half
    per_proj = inner // shards
    pairs = half // LANES
    core = core_ref[0]

    copy_own = pltpu.make_async_copy(own_ref, weights.at[core], sems.at[0])
    copy_other = pltpu.make_async_copy(other_ref, weights.at[1 - core], sems.at[1])
    copy_own.start()
    copy_other.start()

    lane = lax.broadcasted_iota(jnp.int32, (1, LANES), 1)
    even_f = (lane < HEAD_DIM).astype(F32)
    even = even_f.astype(BF)
    odd = (1.0 - even_f).astype(BF)
    row_i = lax.broadcasted_iota(jnp.int32, (2 * LANES, LANES), 0) & (LANES - 1)
    col_i = lax.broadcasted_iota(jnp.int32, (2 * LANES, LANES), 1)
    same = ((row_i >= HEAD_DIM) == (col_i >= HEAD_DIM)).astype(F32)
    averager = (same * (1.0 / HEAD_DIM)).astype(BF)

    def head_mean(values):
        high = values.astype(BF)
        low = (values - high.astype(F32)).astype(BF)
        return dot_nn(jnp.concatenate([high, low], axis=1), averager)

    def split_heads(tile):
        return jnp.concatenate([tile * even, tile * odd], axis=0)

    def qkv_block(h, part):
        return weights[h, :, part * per_qkv : (part + 1) * per_qkv, :].reshape(width, half)

    def proj_block(h, b):
        start = 3 * per_qkv + b * per_proj
        return weights[h, :, start : start + per_proj, :].reshape(inner, half)

    copy_own.wait()
    copy_other.wait()

    normed = normed_ref[...]
    for h in range(2):
        for part, gain_ref, n_ref, z_ref, r_ref in (
            (0, qgain_ref, qn, qz, qr),
            (1, kgain_ref, kn, kz, kr),
        ):
            raw = dot_nn(normed, qkv_block(h, part))
            for p in range(pairs):
                x = raw[:, p * LANES : (p + 1) * LANES]
                r = lax.rsqrt(head_mean(x * x) + EPS)
                z = x * r
                z_ref[h * pairs + p] = z
                r_ref[h * pairs + p] = r
                n_ref[h * pairs + p] = (z * gain_ref[...]).astype(BF)
        raw = dot_nn(normed, qkv_block(h, 2)).astype(BF)
        for p in range(pairs):
            vn[h * pairs + p] = raw[:, p * LANES : (p + 1) * LANES]

    for i in range(2 * pairs):
        for j in range(2):
            rs = slice(j * tokens, (j + 1) * tokens)
            score = dot_nt(split_heads(qn[i, rs, :]), kn[i, rs, :]) * (1.0 / math.sqrt(HEAD_DIM))
            e = jnp.exp(score)
            a = e * (1.0 / jnp.sum(e, axis=-1, keepdims=True))
            att[i, j] = a
            ab = a.astype(BF)
            mixed = dot_nn(
                jnp.concatenate([ab[:tokens], ab[tokens:]], axis=1), split_heads(vn[i, rs, :])
            )
            blended[rs, i * LANES : (i + 1) * LANES] = mixed.astype(BF)

    low = dot_nn(blended[...], down_ref[...]).astype(BF)
    lowrank[...] = low
    for h in range(2):
        for b in range(2):
            cols = slice((2 * h + b) * half, (2 * h + b + 1) * half)
            base = dot_nn(blended[...], proj_block(h, b))
            extra = dot_nn(low, up_ref[:, cols])
            for j in range(2):
                rs = slice(j * tokens, (j + 1) * tokens)
                gate = gate_ref[j : j + 1, cols]
                u = hidden_ref[rs, cols] + gate * base[rs]
                base_u[rs, cols] = u
                adj_u[rs, cols] = u + gate * extra[rs]

    def row_norm(u):
        return lax.rsqrt(jnp.mean(u * u, axis=-1, keepdims=True) + EPS)

    fgain = fgain_ref[...]
    for u_ref, vel_ref in ((base_u, base_vel), (adj_u, adj_vel)):
        u = u_ref[...]
        y = (u * row_norm(u) * fgain).astype(BF)
        vel_ref[...] = dot_nn(y, wout_ref[...])

    def tail_back(u, cotangent):
        dz = dot_nt(cotangent.astype(BF), wout_ref[...]) * fgain
        r = row_norm(u)
        z = u * r
        return r * (dz - z * jnp.mean(dz * z, axis=-1, keepdims=True))

    current = adjoint_ref[...]
    for j in range(2):
        rs = slice(j * tokens, (j + 1) * tokens)
        gate = gate_ref[j : j + 1, :]
        residual = coef_ref[j, 0] * (adj_vel[rs, :] - base_vel[rs, :]) + coef_ref[j, 1] * current
        adjusted = (tail_back(adj_u[rs, :], coef_ref[j, 2] * residual) * gate).astype(BF)
        adj_grad[rs, :] = adjusted
        low_grad[rs, :] = dot_nt(adjusted, up_ref[...]).astype(BF)

        hidden_grad = tail_back(base_u[rs, :], current)
        proj_grad = (hidden_grad * gate).astype(BF)
        blend_grad = jnp.zeros((tokens, inner), F32)
        for h in range(2):
            for b in range(2):
                cols = slice((2 * h + b) * half, (2 * h + b + 1) * half)
                blend_grad = blend_grad + dot_nt(proj_grad[:, cols], proj_block(h, b))
        blend_grad = blend_grad.astype(BF)

        normed_grad = jnp.zeros((tokens, width), F32)
        for h in range(2):
            dqs, dks, dvs = [], [], []
            for p in range(pairs):
                i = h * pairs + p
                db = split_heads(blend_grad[:, i * LANES : (i + 1) * LANES])
                a = att[i, j]
                da = dot_nt(db, vn[i, rs, :])
                ds = a * (da - jnp.sum(da * a, axis=-1, keepdims=True))
                ds = (ds * (1.0 / math.sqrt(HEAD_DIM))).astype(BF)
                dvs.append(dot_tn(a.astype(BF), db).astype(BF))
                dq2 = dot_nn(ds, kn[i, rs, :])
                dq = jnp.where(lane < HEAD_DIM, dq2[:tokens], dq2[tokens:])
                dk = dot_tn(ds, split_heads(qn[i, rs, :]))
                for grad, gain_ref, z_ref, r_ref, out in (
                    (dq, qgain_ref, qz, qr, dqs),
                    (dk, kgain_ref, kz, kr, dks),
                ):
                    dz = grad * gain_ref[...]
                    z = z_ref[i, rs, :]
                    out.append((r_ref[i, rs, :] * (dz - z * head_mean(dz * z))).astype(BF))
            for part, pieces in enumerate((dqs, dks, dvs)):
                grad = jnp.concatenate(pieces, axis=1)
                normed_grad = normed_grad + dot_nt(grad, qkv_block(h, part))

        hid = hidden_ref[rs, :]
        rh = row_norm(hid)
        hn = hid * rh
        dhn = normed_grad * scale1_ref[j : j + 1, :]
        total = hidden_grad + rh * (dhn - hn * jnp.mean(dhn * hn, axis=-1, keepdims=True))
        latent_grad = dot_nt(total.astype(BF), win_ref[...])
        current = current + (2.0 * latent_grad - current * coef_ref[j, 3]) * (1.0 / STEPS)

    adjoint_out_ref[...] = current
    down_out_ref[...] = dot_tn(blended[...], low_grad[...]).astype(BF)
    up_out_ref[...] = dot_tn(lowrank[...], adj_grad[...]).astype(BF)


def step_pair(core, coef, own, other, normed, hidden, adjoint, *rest):
    tokens, chan = adjoint.shape
    rows, width = hidden.shape
    shards, packed, half = own.shape
    inner, rank = rest[2].shape
    tiles = inner // LANES
    vmem = pl.BlockSpec(memory_space=pltpu.VMEM)
    smem = pl.BlockSpec(memory_space=pltpu.SMEM)
    hbm = pl.BlockSpec(memory_space=pl.ANY)
    f32_tiles = pltpu.VMEM((tiles, rows, LANES), F32)
    bf_tiles = pltpu.VMEM((tiles, rows, LANES), BF)
    return pl.pallas_call(
        step_pair_kernel,
        out_shape=(
            jax.ShapeDtypeStruct((tokens, chan), F32),
            jax.ShapeDtypeStruct((inner, rank), BF),
            jax.ShapeDtypeStruct((rank, width), BF),
        ),
        in_specs=[smem, smem, hbm, hbm] + [vmem] * (3 + len(rest)),
        out_specs=(vmem, vmem, vmem),
        scratch_shapes=[
            pltpu.VMEM((2, shards, packed, half), BF),
            pltpu.SemaphoreType.DMA((2,)),
            bf_tiles,
            f32_tiles,
            f32_tiles,
            bf_tiles,
            f32_tiles,
            f32_tiles,
            bf_tiles,
            pltpu.VMEM((tiles, 2, 2 * tokens, tokens), F32),
            pltpu.VMEM((rows, inner), BF),
            pltpu.VMEM((rows, width), F32),
            pltpu.VMEM((rows, width), F32),
            pltpu.VMEM((rows, chan), F32),
            pltpu.VMEM((rows, chan), F32),
            pltpu.VMEM((rows, rank), BF),
            pltpu.VMEM((rows, width), BF),
            pltpu.VMEM((rows, rank), BF),
        ],
        compiler_params=pltpu.CompilerParams(vmem_limit_bytes=50 * 1024 * 1024),
    )(core, coef, own, other, normed, hidden, adjoint, *rest)


def time_features(upper_time):
    halves = TIME_FEAT // 2
    frequency = jnp.exp(-math.log(10000.0) * jnp.arange(halves, dtype=F32) / halves)
    angles = 1000.0 * upper_time[..., None] * frequency
    return jnp.concatenate([jnp.cos(angles), jnp.sin(angles)], axis=-1).astype(BF)


def per_device(
    states,
    adjoint,
    grid_step_index,
    input_weight,
    timestep_weight,
    query_key_value_weight,
    projection_weight,
    down_factor,
    up_factor,
    query_norm_gain,
    key_norm_gain,
    final_norm_gain,
    output_weight,
):
    dp, shards = lax.axis_size("dp"), lax.axis_size("fsdp")
    sample_batch = dp * shards * states.shape[0]
    core = lax.axis_index("dp") % 2
    tokens, chan = states.shape[2:]
    width = input_weight.shape[1]
    inner = projection_weight.shape[1] // 2
    half = inner // 2
    rank = down_factor.shape[1]

    pieces = [
        lax.dynamic_slice_in_dim(query_key_value_weight, part * inner + core * half, half, 1)
        for part in range(3)
    ]
    pieces += [
        lax.dynamic_slice_in_dim(projection_weight, core * inner + b * half, half, 1)
        for b in range(2)
    ]
    own = lax.all_gather(jnp.concatenate(pieces, axis=0), "fsdp", axis=0)
    other = lax.ppermute(own, "dp", [(i, i ^ 1) for i in range(dp)])

    mod_cols = 3 * width // shards
    time_rows = timestep_weight.shape[0]
    n_time = time_rows * mod_cols // LANES
    n_down = down_factor.size // LANES
    n_up = up_factor.size // LANES

    def to_all(rows):
        return jnp.broadcast_to(rows[None], (shards,) + rows.shape)

    out = jnp.concatenate(
        [
            timestep_weight.reshape(time_rows, shards, mod_cols)
            .transpose(1, 0, 2)
            .reshape(shards, n_time, LANES),
            to_all(down_factor.reshape(n_down, LANES)),
            to_all(up_factor.reshape(n_up, LANES)),
            to_all(jnp.broadcast_to(grid_step_index.astype(BF)[:, None], (4, LANES))),
        ],
        axis=1,
    )
    got = lax.all_to_all(out, "fsdp", 0, 0, tiled=True)
    time_cols = got[:, :n_time].reshape(shards * time_rows, mod_cols)
    down_full = got[:, n_time : n_time + n_down].reshape(shards * down_factor.shape[0], rank)
    up_full = got[:, n_time + n_down : n_time + n_down + n_up].reshape(rank, width)
    steps = got[:, n_time + n_down + n_up, 0].astype(F32)

    turns = jnp.arange(2, dtype=F32)
    feats = time_features((steps[:, None] + 1.0 - turns) / STEPS)
    mods = jnp.dot(
        feats.reshape(2 * shards, TIME_FEAT), time_cols, preferred_element_type=F32
    ).reshape(shards, 2, mod_cols)
    mods = lax.all_to_all(mods, "fsdp", 0, 0, tiled=True)
    mods = mods.transpose(1, 0, 2).reshape(2, 3 * width)
    shift, scale1, gate = mods[:, :width], 1.0 + mods[:, width : 2 * width], mods[:, 2 * width :]

    hidden = jnp.dot(states[0].reshape(2 * tokens, chan), input_weight, preferred_element_type=F32)
    root = lax.rsqrt(jnp.mean(hidden * hidden, axis=-1, keepdims=True) + EPS)
    normed = (hidden * root).reshape(2, tokens, width) * scale1[:, None] + shift[:, None]
    normed = normed.astype(BF).reshape(2 * tokens, width)

    times = (grid_step_index[0].astype(F32) + 1.0 - turns) / STEPS
    sigma = jnp.sqrt(2.0 * (1.0 - times) / times)
    coef = jnp.stack([2.0 / sigma, sigma, 4.0 / (sigma * sample_batch), 1.0 / times], axis=1)

    adjoint_out, down_grad, up_grad = step_pair(
        core.astype(jnp.int32)[None],
        coef,
        own,
        other,
        normed,
        hidden,
        adjoint[0],
        scale1,
        gate,
        down_full,
        up_full,
        jnp.tile(query_norm_gain, 2)[None],
        jnp.tile(key_norm_gain, 2)[None],
        final_norm_gain[None],
        output_weight,
        input_weight,
    )

    out = jnp.concatenate(
        [down_grad.reshape(shards, n_down, LANES), up_grad.reshape(shards, n_up, LANES)], axis=1
    )
    got = lax.all_to_all(out, "fsdp", 0, 0, tiled=True)
    part = jnp.sum(got.astype(F32), axis=0).astype(BF)
    got = lax.all_to_all(
        jnp.broadcast_to(part[None], (dp,) + part.shape), "dp", 0, 0, tiled=True
    )
    part = jnp.sum(got.astype(F32), axis=0)
    return (
        adjoint_out[None],
        part[:n_down].reshape(down_factor.shape),
        part[n_down:].reshape(up_factor.shape),
    )


def solution(mesh):
    in_specs = (
        P(("dp", "fsdp"), None, None, None),
        P(("dp", "fsdp"), None, None),
        P(("dp", "fsdp")),
        P(),
        P("fsdp", None),
        P("fsdp", None),
        P("fsdp", None),
        P("fsdp", None),
        P("fsdp", None),
        P(),
        P(),
        P(),
        P(),
    )
    out_specs = (P(("dp", "fsdp"), None, None), P("fsdp", None), P("fsdp", None))
    return jax.shard_map(
        per_device, mesh=mesh, in_specs=in_specs, out_specs=out_specs, check_vma=False
    )
```

time: 680 us -> 215 us (0.32)
  waiting for transfers between devices: 362 us -> 114 us
  blocking collectives: 194 us -> 10.5 us
  matrix products: 64.5 us -> 0.62 us
  starting transfers between devices: 0.19 us -> 34.9 us
  Pallas kernels: 0 us -> 23.1 us
  other arithmetic: 14.6 us -> 1.9 us
  local copies, waits for them, and re-layouts: 23.8 us -> 13.6 us
    psum x1 -> x0, blocking collectives: 136 us -> none  [per_device(): lax.psum(part_down.astype(jnp.bfloat16), 'dp').astype(jnp.float32)]
    unnamed x6 -> x1, waiting for transfers between devices: 132 us -> 0.02 us
    all_gather x3 -> x1, waiting for transfers between devices: 159 us -> 77 us  [per_device(): own = lax.all_gather(jnp.concatenate(pieces, axis=0), 'fsdp', axis=0)]
    reduce_scatter x1 -> x0, waiting for transfers between devices: 70.8 us -> none  [per_device(): lax.psum_scatter(down_total.astype(jnp.bfloat16), 'fsdp', scatter_dimensi...]
    dot_general x39 -> x2, matrix products: 64.5 us -> 0.62 us  [the longest x1 0.47 us: per_device(): jnp.dot(states[0].reshape(2 * tokens, chan), input_weight, preferred_elem...]
    all_gather x2 -> x0, blocking collectives: 57.6 us -> none  [the longest x1 31.4 us: per_device(): lax.all_gather(down_factor, 'fsdp', axis=0, tiled=True)]
    all_to_all x0 -> x3, waiting for transfers between devices: none -> 37 us  [the longest x1 18.6 us: per_device(): lax.all_to_all(jnp.broadcast_to(part[None], (dp,) + part.shape), 'dp', 0,...]
    all_to_all x0 -> x3, starting transfers between devices: none -> 23.7 us  [the longest x1 13.7 us: per_device(): lax.all_to_all(jnp.broadcast_to(part[None], (dp,) + part.shape), 'dp', 0,...]
  transfers between devices with their start and end apart: 5 -> 5, of which waited for: 5 -> 4; matrix products, arithmetic and copies ran while one was open for 3% -> 4% of each run, Pallas kernels for 0% -> 0%
where the time goes in v1:
time: 215 us; the launch traced here: 214 us
  waiting for transfers between devices  114 us (53%)
  starting transfers between devices  34.9 us (16%)
  Pallas kernels  23.1 us (11%)
  between operations  15 us (7%)
  local copies, waits for them, and re-layouts  13.6 us (6%)
  blocking collectives  10.5 us (5%)
    all_gather x1, waiting for transfers between devices, per_device(): own = lax.all_gather(jnp.concatenate(pieces, axis=0), 'fsdp', axis=0)  77 us
    pallas_call x1, Pallas kernels, step_pair(): pl.pallas_call(step_pair_kernel, out_shape=(jax.ShapeDtypeStruct((tokens,...  23.1 us
    all_to_all x1, waiting for transfers between devices, per_device(): lax.all_to_all(jnp.broadcast_to(part[None], (dp,) + part.shape), 'dp', 0,...  18.6 us
    all_to_all x1, starting transfers between devices, per_device(): lax.all_to_all(jnp.broadcast_to(part[None], (dp,) + part.shape), 'dp', 0,...  13.7 us
    all_to_all x1, waiting for transfers between devices, per_device(): got = lax.all_to_all(out, 'fsdp', 0, 0, tiled=True)  11.8 us
    ppermute x1, starting transfers between devices, per_device(): other = lax.ppermute(own, 'dp', [(i, i ^ 1) for i in range(dp)])  11.1 us
    all_to_all x1, blocking collectives, per_device(): got = lax.all_to_all(out, 'fsdp', 0, 0, tiled=True)  10.5 us
    all_to_all x1, waiting for transfers between devices, per_device(): mods = lax.all_to_all(mods, 'fsdp', 0, 0, tiled=True)  6.63 us
  transfers between devices with their start and end apart: 5, of which 4 were waited for; matrix products, arithmetic and copies ran while one was open for 4% of the time, Pallas kernels for 0%

profile of v1, /device:TPU:1, one launch (start us, length us, event | category | flops | bytes accessed | tf_op | source)
XLA Modules:
  0.0 213.6 jit_solution(732097518022935161)
XLA Ops:
  7.2 0.0 all-gather.3.cloned.1.call-start
  7.2 0.9 dynamic-slice_dynamic-update-slice_fusion.2
  8.1 0.9 dynamic-slice_dynamic-update-slice_fusion.1
  9.0 0.9 dynamic-slice_dynamic-update-slice_fusion
  9.9 0.8 dynamic-slice_dynamic-update-slice_fusion.4
  10.7 0.8 dynamic-slice_dynamic-update-slice_fusion.3
  11.5 0.0 copy-start.1
  11.5 0.7 copy-done.1
  12.2 0.0 all-gather.3.cloned.1.call-update
  12.3 77.0 %all-gather.3.cloned.1.call-done = bf16[6144,384]{1,0:T(8,128)(2,1)} async-done(((bf16[384,384]{1,0:T(8,128)(2,1)}), bf16[6144,384]{1,0:T(8,128)(2,1)}) %all-gather.3.cloned.1.call-update) | async-done | bytes 4718608 | tf_op jit(solution)/shard_map/all_gather | solution.py:312
  89.2 11.1 %collective-permute-start = (bf16[16,384,384]{2,1,0:T(8,128)(2,1)}, bf16[16,384,384]{2,1,0:T(8,128)(2,1)}, u32[]{:S(2)}, u32[]{:S(2)}) collective-permute-start(bf16[16,384,384]{2,1,0:T(8,128)(2,1)} %bitcast.33), channel_id=1, source_target_pairs={{0,16},{16,0},{32,48},{48,32},{64,80},{80,64},{96,112},{112,96},{1... | collective-permute-start | bytes 14155784 | tf_op jit(solution)/shard_map/ppermute | solution.py:313
  101.0 0.8 broadcast_in_dim.17
  101.8 0.7 broadcast_in_dim.19
  102.5 0.0 copy-start.6
  102.5 0.0 copy-start.7
  102.5 0.0 copy-start.5
  102.6 0.0 copy-start.4
  102.6 1.2 reshape.145
  103.8 0.0 copy-start.3
  103.8 0.0 copy-start.2
  103.9 0.0 copy-start
  103.9 0.4 reshape.146
  104.2 0.1 pad.7.clone
  104.4 1.0 maximum_maximum_fusion
  105.3 3.8 %all-to-all-start = ((bf16[16,112,128]{2,1,0:T(8,128)(2,1)}), bf16[16,112,128]{2,1,0:T(8,128)(2,1)S(1)}, u32[]{:S(2)}, u32[]{:S(2)}) async-start(bf16[16,112,128]{2,1,0:T(8,128)(2,1)} %maximum_maximum_fusion), calls=%async_computation | async-start | bytes 917504 | tf_op jit(solution)/shard_map/all_to_all | solution.py:335
  109.1 0.0 copy-done.6
  109.1 0.1 broadcast_in_dim_tile.6.qgain_ref
  109.2 0.0 copy-done.7
  109.2 0.1 broadcast_in_dim_tile.7.kgain_ref
  109.3 0.0 copy-done.5
  109.3 0.0 copy-done.4
  109.4 0.0 copy-done.3
  109.4 0.1 copy.47
  109.5 0.0 copy-done.2
  109.5 0.2 copy.48.wout_ref
  109.8 0.0 copy-done
  109.8 0.5 multiply_reduce_fusion
  110.3 11.8 %all-to-all-done = bf16[16,112,128]{2,1,0:T(8,128)(2,1)S(1)} async-done(((bf16[16,112,128]{2,1,0:T(8,128)(2,1)}), bf16[16,112,128]{2,1,0:T(8,128)(2,1)S(1)}, u32[]{:S(2)}, u32[]{:S(2)}) %all-to-all-start) | async-done | bytes 458784 | tf_op jit(solution)/shard_map/all_to_all | solution.py:335
  122.1 0.3 reshape.147
  122.3 0.2 fusion.12
  122.6 0.1 fusion.6
  122.7 0.1 fusion.1
  122.9 0.6 copy.45
  123.5 6.3 %all-to-all-start.1 = ((f32[16,2,288]{2,1,0:T(2,128)}), f32[16,2,288]{2,1,0:T(2,128)S(1)}, u32[]{:S(2)}, u32[]{:S(2)}) async-start(f32[16,2,288]{2,1,0:T(2,128)} %copy.45), calls=%async_computation.1 | async-start | bytes 98304 | tf_op jit(solution)/shard_map/all_to_all | solution.py:346
  129.8 0.1 pad_maximum_fusion.1.coef_ref
  129.9 0.1 reshape.149.down_ref
  130.0 0.1 slice.42
  130.1 0.2 reshape.150.up_ref
  130.3 6.6 %all-to-all-done.1 = f32[16,2,288]{2,1,0:T(2,128)S(1)} async-done(((f32[16,2,288]{2,1,0:T(2,128)}), f32[16,2,288]{2,1,0:T(2,128)S(1)}, u32[]{:S(2)}, u32[]{:S(2)}) %all-to-all-start.1) | async-done | bytes 36896 | tf_op jit(solution)/shard_map/all_to_all | solution.py:346
  137.0 0.1 reshape.148
  137.1 0.3 fusion.normed_ref
  137.3 0.0 collective-permute-done.other_ref
  137.4 23.1 %shard_map.148 = (f32[128,64]{1,0:T(8,128)S(1)}, bf16[768,64]{1,0:T(8,128)(2,1)S(1)}, bf16[64,1536]{1,0:T(8,128)(2,1)S(1)}) custom-call(s32[1]{0:T(128)} %bitcast.core_ref, f32[2,4]{1,0:T(2,128)S(1)} %pad_maximum_fusion.1.coef_ref, bf16[16,384,384]{2,1,0:T(8,128)(2,1)} %bitcast.34, bf16[16,384,384]{2,1,0:T(8,128)(2,1)} %collective-permute-done.other_ref, ...), custom_call_target="tpu_custom_call" | custom-call | tf_op jit(solution)/shard_map/pallas_call | solution.py:240
  160.4 0.1 reshape.151
  160.6 0.3 reshape.152
  160.9 10.5 %all_to_all.20 = bf16[16,72,128]{2,1,0:T(8,128)(2,1)S(1)} all-to-all(bf16[16,72,128]{2,1,0:T(8,128)(2,1)S(1)} %pad_maximum_fusion), channel_id=1, replica_groups=mesh['dp'=32,'fsdp'=16] {'fsdp'}, dimensions={0} | all-to-all | bytes 589824 | tf_op jit(solution)/shard_map/all_to_all | solution.py:381
  171.4 0.9 broadcast_in_dim.44
  172.3 13.7 %all-to-all-start.3 = ((bf16[32,72,128]{2,1,0:T(8,128)(2,1)}), bf16[32,72,128]{2,1,0:T(8,128)(2,1)S(1)}, u32[]{:S(2)}, u32[]{:S(2)}) async-start(bf16[32,72,128]{2,1,0:T(8,128)(2,1)} %broadcast_in_dim.44), calls=%async_computation.3 | async-start | bytes 1179648 | tf_op jit(solution)/shard_map/all_to_all | solution.py:383
  186.0 0.7 copy.49
  186.7 18.6 %all-to-all-done.3 = bf16[32,72,128]{2,1,0:T(8,128)(2,1)S(1)} async-done(((bf16[32,72,128]{2,1,0:T(8,128)(2,1)}), bf16[32,72,128]{2,1,0:T(8,128)(2,1)S(1)}, u32[]{:S(2)}, u32[]{:S(2)}) %all-to-all-start.3) | async-done | bytes 589856 | tf_op jit(solution)/shard_map/all_to_all | solution.py:383
  205.3 0.1 convert_reduce_fusion
  205.4 0.6 reshape.154
  206.0 0.7 reshape.153
  (21 shorter events, 0.3 us)
Async XLA Ops:
  7.2 82.1 %all-gather.3.cloned.1.call-start = ((), (), s32[]{:S(2)}) async-start(), calls=%async_computation.4 | async-start | bytes 5013504 | tf_op jit(solution)/shard_map/all_gather | solution.py:312
  11.5 0.7 copy-start.1
  89.2 48.1 %collective-permute-start = (bf16[16,384,384]{2,1,0:T(8,128)(2,1)}, bf16[16,384,384]{2,1,0:T(8,128)(2,1)}, u32[]{:S(2)}, u32[]{:S(2)}) collective-permute-start(bf16[16,384,384]{2,1,0:T(8,128)(2,1)} %bitcast.33), channel_id=1, source_target_pairs={{0,16},{16,0},{32,48},{48,32},{64,80},{80,64},{96,112},{112,96},{1... | collective-permute-start | bytes 14155784 | tf_op jit(solution)/shard_map/ppermute | solution.py:313
  102.5 6.6 %copy-start.6 = (f32[64]{0:T(128)S(1)}, f32[64]{0:T(128)}, u32[]{:S(2)}) copy-start(f32[64]{0:T(128)} %param.22) | copy-start | bytes 772
  102.5 6.7 %copy-start.7 = (f32[64]{0:T(128)S(1)}, f32[64]{0:T(128)}, u32[]{:S(2)}) copy-start(f32[64]{0:T(128)} %param.23) | copy-start | bytes 772
  102.5 6.8 %copy-start.5 = (f32[1536]{0:T(1024)S(1)}, f32[1536]{0:T(1024)}, u32[]{:S(2)}) copy-start(f32[1536]{0:T(1024)} %param.24) | copy-start | bytes 18436
  102.6 6.8 %copy-start.4 = (bf16[1,2,128,64]{2,3,1,0:T(8,128)(2,1)S(1)}, bf16[1,2,128,64]{2,3,1,0:T(8,128)(2,1)}, u32[]{:S(2)}) copy-start(bf16[1,2,128,64]{2,3,1,0:T(8,128)(2,1)} %param.13) | copy-start | bytes 98308
  103.8 5.6 %copy-start.3 = (f32[1,128,64]{1,2,0:T(8,128)S(1)}, f32[1,128,64]{1,2,0:T(8,128)}, u32[]{:S(2)}) copy-start(f32[1,128,64]{1,2,0:T(8,128)} %param.14) | copy-start | bytes 98308
  103.8 5.7 %copy-start.2 = (bf16[1536,64]{0,1:T(8,128)(2,1)S(1)}, bf16[1536,64]{0,1:T(8,128)(2,1)}, u32[]{:S(2)}) copy-start(bf16[1536,64]{0,1:T(8,128)(2,1)} %param.25) | copy-start | bytes 589828
  103.9 5.9 %copy-start = (bf16[64,1536]{1,0:T(8,128)(2,1)S(1)}, bf16[64,1536]{1,0:T(8,128)(2,1)}, u32[]{:S(2)}) copy-start(bf16[64,1536]{1,0:T(8,128)(2,1)} %win_ref.1) | copy-start | bytes 589828
  105.3 16.7 %all-to-all-start = ((bf16[16,112,128]{2,1,0:T(8,128)(2,1)}), bf16[16,112,128]{2,1,0:T(8,128)(2,1)S(1)}, u32[]{:S(2)}, u32[]{:S(2)}) async-start(bf16[16,112,128]{2,1,0:T(8,128)(2,1)} %maximum_maximum_fusion), calls=%async_computation | async-start | bytes 917504 | tf_op jit(solution)/shard_map/all_to_all | solution.py:335
  123.5 13.4 %all-to-all-start.1 = ((f32[16,2,288]{2,1,0:T(2,128)}), f32[16,2,288]{2,1,0:T(2,128)S(1)}, u32[]{:S(2)}, u32[]{:S(2)}) async-start(f32[16,2,288]{2,1,0:T(2,128)} %copy.45), calls=%async_computation.1 | async-start | bytes 98304 | tf_op jit(solution)/shard_map/all_to_all | solution.py:346
  172.3 33.0 %all-to-all-start.3 = ((bf16[32,72,128]{2,1,0:T(8,128)(2,1)}), bf16[32,72,128]{2,1,0:T(8,128)(2,1)S(1)}, u32[]{:S(2)}, u32[]{:S(2)}) async-start(bf16[32,72,128]{2,1,0:T(8,128)(2,1)} %broadcast_in_dim.44), calls=%async_computation.3 | async-start | bytes 1179648 | tf_op jit(solution)/shard_map/all_to_all | solution.py:383
Sparse Core Ops, SparseCore 0:
  12.4 76.7 all-gather.2

commit v2 on v1

--- a/solution.py
+++ b/solution.py
@@ -12,6 +12,7 @@
 STEPS = 28
 LANES = 128
 EPS = 1e-06
+Y_CHIPS = 8
 BF = jnp.bfloat16
 F32 = jnp.float32
 
@@ -29,59 +30,70 @@
 
 
 def step_pair_kernel(
-    core_ref,
+    place_ref,
     coef_ref,
-    own_ref,
-    other_ref,
-    normed_ref,
-    hidden_ref,
-    adjoint_ref,
-    scale1_ref,
-    gate_ref,
-    down_ref,
-    up_ref,
-    qgain_ref,
-    kgain_ref,
-    fgain_ref,
-    wout_ref,
-    win_ref,
-    adjoint_out_ref,
-    down_out_ref,
-    up_out_ref,
-    weights,
-    sems,
-    qn,
-    qz,
-    qr,
-    kn,
-    kz,
-    kr,
-    vn,
-    att,
-    blended,
-    base_u,
-    adj_u,
-    base_vel,
-    adj_vel,
-    lowrank,
-    adj_grad,
-    low_grad,
+    *refs,
 ):
+    (
+        own_home,
+        own_parts,
+        other_home,
+        other_parts,
+        normed_ref,
+        hidden_ref,
+        adjoint_ref,
+        scale1_ref,
+        gate_ref,
+        down_ref,
+        up_ref,
+        qgain_ref,
+        kgain_ref,
+        fgain_ref,
+        wout_ref,
+        win_ref,
+        adjoint_out_ref,
+        down_out_ref,
+        up_out_ref,
+        weights,
+        sems,
+        qn,
+        qz,
+        qr,
+        kn,
+        kz,
+        kr,
+        vn,
+        att,
+        blended,
+        base_u,
+        adj_u,
+        base_vel,
+        adj_vel,
+        lowrank,
+        adj_grad,
+        low_grad,
+    ) = (refs[0], refs[1:4], refs[4], refs[5:8]) + refs[8:]
     tokens = adjoint_ref.shape[0]
     rows = 2 * tokens
     width = hidden_ref.shape[1]
-    half = weights.shape[3]
-    shards = weights.shape[1]
-    per_qkv = width // shards
+    _, _, shards, per_qkv, half = weights.shape
     inner = 2 * half
     per_proj = inner // shards
     pairs = half // LANES
-    core = core_ref[0]
-
-    copy_own = pltpu.make_async_copy(own_ref, weights.at[core], sems.at[0])
-    copy_other = pltpu.make_async_copy(other_ref, weights.at[1 - core], sems.at[1])
-    copy_own.start()
-    copy_other.start()
+    core, color = place_ref[0], place_ref[1]
+
+    copies = []
+    for side, home, parts in ((core, own_home, own_parts), (1 - core, other_home, other_parts)):
+        copies.append((home.at[:, pl.ds(0, per_qkv), :], weights.at[side, color]))
+        for n, part in enumerate(parts):
+            piece = (color + jnp.where(side == 0, n + 1, 3 - n)) & 3
+            copies.append((part, weights.at[side, piece]))
+    copies = [
+        pltpu.make_async_copy(source, target, sems.at[n])
+        for n, (source, target) in enumerate(copies)
+    ]
+    for copy in copies:
+        copy.start()
 
     lane = lax.broadcasted_iota(jnp.int32, (1, LANES), 1)
     even_f = (lane < HEAD_DIM).astype(F32)
@@ -101,14 +113,13 @@
         return jnp.concatenate([tile * even, tile * odd], axis=0)
 
     def qkv_block(h, part):
-        return weights[h, :, part * per_qkv : (part + 1) * per_qkv, :].reshape(width, half)
+        return weights[h, part].reshape(width, half)
 
     def proj_block(h, b):
-        start = 3 * per_qkv + b * per_proj
-        return weights[h, :, start : start + per_proj, :].reshape(inner, half)
-
-    copy_own.wait()
-    copy_other.wait()
+        return weights[h, 3, :, b * per_proj : (b + 1) * per_proj, :].reshape(inner, half)
+
+    for copy in copies:
+        copy.wait()
 
     normed = normed_ref[...]
     for h in range(2):
@@ -226,10 +237,10 @@
     up_out_ref[...] = dot_tn(lowrank[...], adj_grad[...]).astype(BF)
 
 
-def step_pair(core, coef, own, other, normed, hidden, adjoint, *rest):
+def step_pair(place, coef, gathered, normed, hidden, adjoint, *rest):
     tokens, chan = adjoint.shape
     rows, width = hidden.shape
-    shards, packed, half = own.shape
+    shards, packed, half = gathered[1].shape
     inner, rank = rest[2].shape
     tiles = inner // LANES
     vmem = pl.BlockSpec(memory_space=pltpu.VMEM)
@@ -244,11 +255,11 @@
             jax.ShapeDtypeStruct((inner, rank), BF),
             jax.ShapeDtypeStruct((rank, width), BF),
         ),
-        in_specs=[smem, smem, hbm, hbm] + [vmem] * (3 + len(rest)),
+        in_specs=[smem, smem] + [hbm] * len(gathered) + [vmem] * (3 + len(rest)),
         out_specs=(vmem, vmem, vmem),
         scratch_shapes=[
-            pltpu.VMEM((2, shards, packed, half), BF),
-            pltpu.SemaphoreType.DMA((2,)),
+            pltpu.VMEM((2, 4, shards, packed, half), BF),
+            pltpu.SemaphoreType.DMA((len(gathered),)),
             bf_tiles,
             f32_tiles,
             f32_tiles,
@@ -267,7 +278,84 @@
             pltpu.VMEM((rows, rank), BF),
         ],
         compiler_params=pltpu.CompilerParams(vmem_limit_bytes=50 * 1024 * 1024),
-    )(core, coef, own, other, normed, hidden, adjoint, *rest)
+    )(place, coef, *gathered, normed, hidden, adjoint, *rest)
+
+
+def pieces_kernel(place_ref, qkv_ref, proj_ref, time_ref, extra_ref, out_ref):
+    shards, _, half = out_ref.shape
+    rows, per_proj = qkv_ref.shape[0], proj_ref.shape[0]
+    time_rows, extra_rows = time_ref.shape[0], extra_ref.shape[0]
+    owners = time_ref.shape[1] // half
+    core, color = place_ref[0], place_ref[1]
+
+    def columns(start):
+        return pl.ds(pl.multiple_of(start, LANES), half)
+
+    for r in range(shards):
+        piece = (color + r // Y_CHIPS + 2 * (r % Y_CHIPS)) & 3
+
+        @pl.when(piece < 3)
+        def _():
+            out_ref[r, 0:rows, :] = qkv_ref[:, columns((2 * piece + core) * half)]
+
+        @pl.when(piece == 3)
+        def _():
+            for b in range(2):
+                out_ref[r, b * per_proj : (b + 1) * per_proj, :] = proj_ref[
+                    :, columns((2 * core + b) * half)
+                ]
+
+        owned = min(r, owners - 1)
+        out_ref[r, rows : rows + time_rows, :] = time_ref[:, owned * half : (owned + 1) * half]
+        out_ref[r, rows + time_rows : rows + time_rows + extra_rows, :] = extra_ref[...]
+
+
+def pieces_for(place, qkv, proj, time, extra, shards):
+    vmem = pl.BlockSpec(memory_space=pltpu.VMEM)
+    rows = qkv.shape[0] + time.shape[0] + extra.shape[0]
+    return pl.pallas_call(
+        pieces_kernel,
+        out_shape=jax.ShapeDtypeStruct((shards, rows, proj.shape[1] // 4), BF),
+        in_specs=[pl.BlockSpec(memory_space=pltpu.SMEM)] + [vmem] * 4,
+        out_specs=vmem,
+    )(place, qkv, proj, time, extra)
+
+
+def gather_weights(qkv, proj, time, extra, dp, shards):
+    z_chips = dp // 4
+    d, f = lax.axis_index("dp"), lax.axis_index("fsdp")
+    core, z, x_hi = d % 2, (d // 2) % z_chips, d // (2 * z_chips)
+    plane = 2 * x_hi + z
+    color = (plane + f // Y_CHIPS + 2 * (f % Y_CHIPS)) % 4
+    place = jnp.stack([core, plane]).astype(jnp.int32)
+    home = lax.all_to_all(
+        pieces_for(place, qkv, proj, time, extra, shards), "fsdp", 0, 0, tiled=True
+    )
+
+    def index(x, y, z, c):
+        return ((x // 2 * z_chips + z) * 2 + c) * shards + (x % 2) * Y_CHIPS + y
+
+    def neighbours(dx, dy, dz):
+        return [
+            (
+                index((x + s * dx) % 4, (y + s * dy) % Y_CHIPS, (z + s * dz) % z_chips, c),
+                index(x, y, z, c),
+            )
+            for x in range(4)
+            for y in range(Y_CHIPS)
+            for z in range(z_chips)
+            for c, s in ((0, 1), (1, -1))
+        ]
+
+    piece = home[:, : qkv.shape[0]]
+    parts = [
+        lax.ppermute(piece, ("dp", "fsdp"), neighbours(*step))
+        for step in ((1, 0, 0), (0, 1, 0), (0, 0, -1))
+    ]
+    own = [home] + parts
+    swap = [(i, i ^ 1) for i in range(dp)]
+    other = [lax.ppermute(block, "dp", swap) for block in own]
+    return jnp.stack([core, color]).astype(jnp.int32), own + other
 
 
 def time_features(upper_time):
@@ -297,53 +385,48 @@
     core = lax.axis_index("dp") % 2
     tokens, chan = states.shape[2:]
     width = input_weight.shape[1]
-    inner = projection_weight.shape[1] // 2
-    half = inner // 2
     rank = down_factor.shape[1]
 
-    pieces = [
-        lax.dynamic_slice_in_dim(query_key_value_weight, part * inner + core * half, half, 1)
-        for part in range(3)
-    ]
-    pieces += [
-        lax.dynamic_slice_in_dim(projection_weight, core * inner + b * half, half, 1)
-        for b in range(2)
-    ]
-    own = lax.all_gather(jnp.concatenate(pieces, axis=0), "fsdp", axis=0)
-    other = lax.ppermute(own, "dp", [(i, i ^ 1) for i in range(dp)])
-
-    mod_cols = 3 * width // shards
-    time_rows = timestep_weight.shape[0]
-    n_time = time_rows * mod_cols // LANES
-    n_down = down_factor.size // LANES
-    n_up = up_factor.size // LANES
-
-    def to_all(rows):
-        return jnp.broadcast_to(rows[None], (shards,) + rows.shape)
-
-    out = jnp.concatenate(
+    half = projection_weight.shape[1] // 4
+    rows, time_rows = query_key_value_weight.shape[0], timestep_weight.shape[0]
+    n_up = up_factor.size // 2 // half
+    n_down = down_factor.size // 2 // half
+    n_step = -(n_up + n_down) % 8
+    extra = jnp.concatenate(
         [
-            timestep_weight.reshape(time_rows, shards, mod_cols)
-            .transpose(1, 0, 2)
-            .reshape(shards, n_time, LANES),
-            to_all(down_factor.reshape(n_down, LANES)),
-            to_all(up_factor.reshape(n_up, LANES)),
-            to_all(jnp.broadcast_to(grid_step_index.astype(BF)[:, None], (4, LANES))),
+            lax.dynamic_slice_in_dim(up_factor.reshape(2 * n_up, half), core * n_up, n_up, 0),
+            lax.dynamic_slice_in_dim(
+                down_factor.reshape(2 * n_down, half), core * n_down, n_down, 0
+            ),
+            jnp.broadcast_to(grid_step_index.astype(BF)[:, None], (n_step, half)),
         ],
-        axis=1,
-    )
-    got = lax.all_to_all(out, "fsdp", 0, 0, tiled=True)
-    time_cols = got[:, :n_time].reshape(shards * time_rows, mod_cols)
-    down_full = got[:, n_time : n_time + n_down].reshape(shards * down_factor.shape[0], rank)
-    up_full = got[:, n_time + n_down : n_time + n_down + n_up].reshape(rank, width)
-    steps = got[:, n_time + n_down + n_up, 0].astype(F32)
-
+        axis=0,
+    )
+    place, gathered = gather_weights(
+        query_key_value_weight, projection_weight, timestep_weight, extra, dp, shards
+    )
+    home, other_home = gathered[0], gathered[4]
+    first = rows + time_rows
+
+    def both(start, stop):
+        mine, theirs = home[:, start:stop], other_home[:, start:stop]
+        return jnp.stack(
+            [jnp.where(core == 0, mine, theirs), jnp.where(core == 0, theirs, mine)], axis=1
+        )
+
+    up_full = both(first, first + n_up).reshape(rank, width)
+    down_full = both(first + n_up, first + n_up + n_down).reshape(-1, rank)
+
+    owners = 3 * width // half
+    steps = home[:, first + n_up + n_down, 0].astype(F32)
     turns = jnp.arange(2, dtype=F32)
     feats = time_features((steps[:, None] + 1.0 - turns) / STEPS)
     mods = jnp.dot(
-        feats.reshape(2 * shards, TIME_FEAT), time_cols, preferred_element_type=F32
-    ).reshape(shards, 2, mod_cols)
-    mods = lax.all_to_all(mods, "fsdp", 0, 0, tiled=True)
+        feats.reshape(2 * shards, TIME_FEAT),
+        home[:, rows:first].reshape(TIME_FEAT, half),
+        preferred_element_type=F32,
+    ).reshape(shards, 2, half)
+    mods = lax.all_to_all(mods, "fsdp", 0, 0, tiled=True)[:owners]
     mods = mods.transpose(1, 0, 2).reshape(2, 3 * width)
     shift, scale1, gate = mods[:, :width], 1.0 + mods[:, width : 2 * width], mods[:, 2 * width :]
 
@@ -357,10 +440,9 @@
     coef = jnp.stack([2.0 / sigma, sigma, 4.0 / (sigma * sample_batch), 1.0 / times], axis=1)
 
     adjoint_out, down_grad, up_grad = step_pair(
-        core.astype(jnp.int32)[None],
+        place,
         coef,
-        own,
-        other,
+        gathered,
         normed,
         hidden,
         adjoint[0],
@@ -376,18 +458,33 @@
     )
 
     out = jnp.concatenate(
-        [down_grad.reshape(shards, n_down, LANES), up_grad.reshape(shards, n_up, LANES)], axis=1
-    )
+        [down_grad.reshape(shards, -1, LANES), up_grad.reshape(shards, -1, LANES)], axis=1
+    )
+    n_half = out.shape[1] // 2
+    swap = [(i, i ^ 1) for i in range(dp)]
+    keep = lax.dynamic_slice_in_dim(out, core * n_half, n_half, 1)
+    give = lax.dynamic_slice_in_dim(out, (1 - core) * n_half, n_half, 1)
+    out = (keep.astype(F32) + lax.ppermute(give, "dp", swap).astype(F32)).astype(BF)
     got = lax.all_to_all(out, "fsdp", 0, 0, tiled=True)
     part = jnp.sum(got.astype(F32), axis=0).astype(BF)
+    chips = dp // 2
     got = lax.all_to_all(
-        jnp.broadcast_to(part[None], (dp,) + part.shape), "dp", 0, 0, tiled=True
-    )
-    part = jnp.sum(got.astype(F32), axis=0)
+        jnp.broadcast_to(part[None], (chips,) + part.shape),
+        "dp",
+        0,
+        0,
+        axis_index_groups=[[2 * i + c for i in range(chips)] for c in range(2)],
+        tiled=True,
+    )
+    mine = jnp.sum(got.astype(F32), axis=0)
+    theirs = lax.ppermute(mine, "dp", swap)
+    part = jnp.concatenate(
+        [jnp.where(core == 0, mine, theirs), jnp.where(core == 0, theirs, mine)], axis=0
+    )
     return (
         adjoint_out[None],
-        part[:n_down].reshape(down_factor.shape),
-        part[n_down:].reshape(up_factor.shape),
+        part[: down_factor.size // LANES].reshape(down_factor.shape),
+        part[down_factor.size // LANES :].reshape(up_factor.shape),
     )
 
 

time: 215 us -> 160 us (0.74)
  waiting for transfers between devices: 114 us -> 36 us
  blocking collectives: 10.5 us -> 27.9 us
  starting transfers between devices: 34.9 us -> 50.5 us
  between operations: 15 us -> 1.86 us
  local copies, waits for them, and re-layouts: 13.6 us -> 8.01 us
  other arithmetic: 1.9 us -> 6.45 us
  Pallas kernels: 23.1 us -> 26.4 us
    all_gather x1 -> x0, waiting for transfers between devices: 77 us -> none  [per_device(): own = lax.all_gather(jnp.concatenate(pieces, axis=0), 'fsdp', axis=0)]
    ppermute x1 -> x9, starting transfers between devices: 11.1 us -> 35 us  [the longest x3 16.3 us: gather_weights(): lax.ppermute(piece, ('dp', 'fsdp'), neighbours(*step))]
    all_to_all x0 -> x1, blocking collectives: none -> 15.2 us  [per_device(): lax.all_to_all(jnp.broadcast_to(part[None], (chips,) + part.shape), 'dp',...]
    all_to_all x3 -> x2, starting transfers between devices: 23.7 us -> 15.6 us  [the longest x1 8.86 us: gather_weights(): lax.all_to_all(pieces_for(place, qkv, proj, time, extra, shards), 'fsdp',...]
    unnamed x24 -> x19, local copies, waits for them, and re-layouts: 5.31 us -> 1.09 us
    another operation x1 -> x7, other arithmetic: 0.14 us -> 2.82 us  [the longest x4 2.05 us: both(): jnp.stack([jnp.where(core == 0, mine, theirs), jnp.where(core == 0, their...]
    pallas_call x0 -> x1, Pallas kernels: none -> 2.59 us  [pieces_for(): pl.pallas_call(pieces_kernel, out_shape=jax.ShapeDtypeStruct((shards, row...]
    all_to_all x3 -> x2, waiting for transfers between devices: 37 us -> 34.5 us  [the longest x1 34.5 us: gather_weights(): lax.all_to_all(pieces_for(place, qkv, proj, time, extra, shards), 'fsdp',...]
  transfers between devices with their start and end apart: 5 -> 11, of which waited for: 4 -> 3; matrix products, arithmetic and copies ran while one was open for 4% -> 6% of each run, Pallas kernels for 0% -> 0%
where the time goes in v2:
time: 160 us; the launch traced here: 159 us
  starting transfers between devices  50.5 us (32%)
  waiting for transfers between devices  36 us (22%)
  blocking collectives  27.9 us (17%)
  Pallas kernels  26.4 us (16%)
  local copies, waits for them, and re-layouts  8.01 us (5%)
  other arithmetic  6.45 us (4%)
  between operations  1.86 us (1%)
  matrix products  1.68 us (1%)
    all_to_all x1, waiting for transfers between devices, gather_weights(): lax.all_to_all(pieces_for(place, qkv, proj, time, extra, shards), 'fsdp',...  34.5 us
    pallas_call x1, Pallas kernels, step_pair(): pl.pallas_call(step_pair_kernel, out_shape=(jax.ShapeDtypeStruct((tokens,...  23.8 us
    ppermute x3, starting transfers between devices, gather_weights(): lax.ppermute(piece, ('dp', 'fsdp'), neighbours(*step))  16.3 us
    all_to_all x1, blocking collectives, per_device(): lax.all_to_all(jnp.broadcast_to(part[None], (chips,) + part.shape), 'dp',...  15.2 us
    all_to_all x1, blocking collectives, per_device(): got = lax.all_to_all(out, 'fsdp', 0, 0, tiled=True)  12.6 us
    ppermute x4, starting transfers between devices, gather_weights(): other = [lax.ppermute(block, 'dp', swap) for block in own]  11.4 us
    all_to_all x1, starting transfers between devices, gather_weights(): lax.all_to_all(pieces_for(place, qkv, proj, time, extra, shards), 'fsdp',...  8.86 us
    all_to_all x1, starting transfers between devices, per_device(): mods = lax.all_to_all(mods, 'fsdp', 0, 0, tiled=True)[:owners]  6.74 us
  transfers between devices with their start and end apart: 11, of which 3 were waited for; matrix products, arithmetic and copies ran while one was open for 6% of the time, Pallas kernels for 0%

profile of v2, /device:TPU:1, one launch (start us, length us, event | category | flops | bytes accessed | tf_op | source)
XLA Modules:
  0.0 158.9 jit_solution(9353925139757179237)
XLA Ops:
  0.7 0.7 reshape.143
  1.4 0.8 reshape.144
  2.9 0.1 pad.10.clone
  3.0 0.6 pad_add_fusion.1.place_ref
  3.6 0.7 maximum_maximum_fusion.extra_ref
  4.2 2.6 %shard_map.148 = bf16[16,128,384]{2,1,0:T(8,128)(2,1)} custom-call(s32[2]{0:T(128)} %pad_add_fusion.1.place_ref, bf16[96,2304]{1,0:T(8,128)(2,1)} %qkv_ref.1, bf16[48,1536]{1,0:T(8,128)(2,1)} %proj_ref.1, bf16[16,4608]{1,0:T(8,128)(2,1)} %time_ref.1, bf16[16,384]{1,0:T(8,128)(2,1)} %maximum_maximum_fusion.extra_ref), custom_call_target="tpu_custom_call" | custom-call | tf_op jit(solution)/shard_map/pallas_call | solution.py:316
  6.8 8.9 %all-to-all-start = ((bf16[16,128,384]{2,1,0:T(8,128)(2,1)}), bf16[16,128,384]{2,1,0:T(8,128)(2,1)}, u32[]{:S(2)}, u32[]{:S(2)}) async-start(bf16[16,128,384]{2,1,0:T(8,128)(2,1)} %shard_map.148), calls=%async_computation | async-start | bytes 3145728 | tf_op jit(solution)/shard_map/all_to_all | solution.py:331
  15.7 0.0 copy-done.3
  15.8 0.0 copy-done
  15.8 1.5 multiply_reduce_fusion
  17.4 0.0 copy-start.6
  17.4 34.5 %all-to-all-done.refs_0_ = bf16[16,128,384]{2,1,0:T(8,128)(2,1)} async-done(((bf16[16,128,384]{2,1,0:T(8,128)(2,1)}), bf16[16,128,384]{2,1,0:T(8,128)(2,1)}, u32[]{:S(2)}, u32[]{:S(2)}) %all-to-all-start) | async-done | bytes 1572896 | tf_op jit(solution)/shard_map/all_to_all | solution.py:331
  51.9 1.4 slice.52
  53.3 2.4 %collective-permute-start = (bf16[16,96,384]{2,1,0:T(8,128)(2,1)S(1)}, bf16[16,96,384]{2,1,0:T(8,128)(2,1)S(1)}, u32[]{:S(2)}, u32[]{:S(2)}) collective-permute-start(bf16[16,96,384]{2,1,0:T(8,128)(2,1)S(1)} %slice.52), channel_id=1, source_target_pairs={{8,0},{280,16},{40,32},{312,48},{72,64},{344,80},{104,96},{376,112... | collective-permute-start | bytes 3538952 | tf_op jit(solution)/shard_map/ppermute | solution.py:352
  55.7 2.1 %collective-permute-start.1 = (bf16[16,96,384]{2,1,0:T(8,128)(2,1)S(1)}, bf16[16,96,384]{2,1,0:T(8,128)(2,1)}, u32[]{:S(2)}, u32[]{:S(2)}) collective-permute-start(bf16[16,96,384]{2,1,0:T(8,128)(2,1)S(1)} %slice.52), channel_id=1, source_target_pairs={{1,0},{23,16},{33,32},{55,48},{65,64},{87,80},{97,96},{119,112},{1... | collective-permute-start | bytes 3538952 | tf_op jit(solution)/shard_map/ppermute | solution.py:352
  57.8 11.8 %collective-permute-start.2 = (bf16[16,96,384]{2,1,0:T(8,128)(2,1)S(1)}, bf16[16,96,384]{2,1,0:T(8,128)(2,1)}, u32[]{:S(2)}, u32[]{:S(2)}) collective-permute-start(bf16[16,96,384]{2,1,0:T(8,128)(2,1)S(1)} %slice.52), channel_id=1, source_target_pairs={{224,0},{48,16},{0,32},{80,48},{32,64},{112,80},{64,96},{144,112},... | collective-permute-start | bytes 3538952 | tf_op jit(solution)/shard_map/ppermute | solution.py:352
  69.7 0.1 pad_maximum_fusion.3.coef_ref
  69.8 1.9 %collective-permute-start.3 = (bf16[16,128,384]{2,1,0:T(8,128)(2,1)}, bf16[16,128,384]{2,1,0:T(8,128)(2,1)}, u32[]{:S(2)}, u32[]{:S(2)}) collective-permute-start(bf16[16,128,384]{2,1,0:T(8,128)(2,1)} %all-to-all-done.refs_0_), channel_id=1, source_target_pairs={{0,16},{16,0},{32,48},{48,32},{64,80},{80,64},{96,112},{112,96},{1... | collective-permute-start | bytes 4718600 | tf_op jit(solution)/shard_map/ppermute | solution.py:357
  71.7 1.0 slice.54
  72.7 1.0 fusion.11
  73.7 0.1 fusion.4
  73.8 0.1 fusion.6
  74.0 0.7 copy.50
  74.6 6.7 %all-to-all-start.1 = ((f32[16,2,384]{2,1,0:T(2,128)}), f32[16,2,384]{2,1,0:T(2,128)S(1)}, u32[]{:S(2)}, u32[]{:S(2)}) async-start(f32[16,2,384]{2,1,0:T(2,128)} %copy.50), calls=%async_computation.1 | async-start | bytes 98304 | tf_op jit(solution)/shard_map/all_to_all | solution.py:429
  81.4 0.0 collective-permute-done.refs_1_
  81.4 2.7 %collective-permute-start.4 = (bf16[16,96,384]{2,1,0:T(8,128)(2,1)S(1)}, bf16[16,96,384]{2,1,0:T(8,128)(2,1)}, u32[]{:S(2)}, u32[]{:S(2)}) collective-permute-start(bf16[16,96,384]{2,1,0:T(8,128)(2,1)S(1)} %collective-permute-done.refs_1_), channel_id=1, source_target_pairs={{0,16},{16,0},{32,48},{48,32},{64,80},{80,64},{96,112},{112,96},{1... | collective-permute-start | bytes 3538952 | tf_op jit(solution)/shard_map/ppermute | solution.py:357
  84.1 0.0 collective-permute-done.1.refs_2_
  84.1 1.9 %collective-permute-start.5 = (bf16[16,96,384]{2,1,0:T(8,128)(2,1)}, bf16[16,96,384]{2,1,0:T(8,128)(2,1)}, u32[]{:S(2)}, u32[]{:S(2)}) collective-permute-start(bf16[16,96,384]{2,1,0:T(8,128)(2,1)} %collective-permute-done.1.refs_2_), channel_id=1, source_target_pairs={{0,16},{16,0},{32,48},{48,32},{64,80},{80,64},{96,112},{112,96},{1... | collective-permute-start | bytes 3538952 | tf_op jit(solution)/shard_map/ppermute | solution.py:357
  86.0 0.0 collective-permute-done.2.refs_3_
  86.0 4.8 %collective-permute-start.6 = (bf16[16,96,384]{2,1,0:T(8,128)(2,1)}, bf16[16,96,384]{2,1,0:T(8,128)(2,1)}, u32[]{:S(2)}, u32[]{:S(2)}) collective-permute-start(bf16[16,96,384]{2,1,0:T(8,128)(2,1)} %collective-permute-done.2.refs_3_), channel_id=1, source_target_pairs={{0,16},{16,0},{32,48},{48,32},{64,80},{80,64},{96,112},{112,96},{1... | collective-permute-start | bytes 3538952 | tf_op jit(solution)/shard_map/ppermute | solution.py:357
  90.9 0.1 pad_add_fusion.place_ref
  90.9 0.0 copy-done.1
  90.9 0.2 copy.54.refs_18_
  91.2 0.0 copy-done.2
  91.2 0.1 copy.51
  91.3 0.0 copy-done.4
  91.3 0.0 copy-done.5
  91.3 0.1 broadcast_in_dim_tile.6.refs_15_
  91.4 0.1 broadcast_in_dim_tile.7.refs_16_
  91.5 0.0 all-to-all-done.1
  91.5 1.7 %fusion.refs_8_ = bf16[256,1536]{1,0:T(8,128)(2,1)S(1)} fusion(f32[256,1536]{1,0:T(8,128)} %get-tuple-element.39.refs_9_, f32[2,1536]{1,0:T(2,128)S(1)} %get-tuple-element.34, f32[2,1536]{1,0:T(2,128)S(1)} %get-tuple-element.35.refs_11_, f32[256]{0:T(256)S(1)} %add_rsqrt_fusion), kind=kLoop, calls=%fused_computation.1 | loop fusion | flops 1572864 | bytes 2384896 | tf_op jit(solution)/shard_map/convert_element_type | solution.py:436
  93.2 0.0 collective-permute-done.3.refs_4_
  93.2 1.0 select_bitcast_fusion.1
  94.2 0.1 reshape.148.refs_14_
  94.4 1.0 select_bitcast_fusion.3
  95.4 0.1 pad_maximum_fusion.1
  95.5 0.1 reshape.147.refs_13_
  95.6 0.0 collective-permute-done.4.refs_5_
  95.7 0.0 collective-permute-done.5.refs_6_
  95.7 0.0 collective-permute-done.6.refs_7_
  95.7 23.8 %shard_map.149 = (f32[128,64]{1,0:T(8,128)S(1)}, bf16[768,64]{1,0:T(8,128)(2,1)S(1)}, bf16[64,1536]{1,0:T(8,128)(2,1)S(1)}) custom-call(s32[2]{0:T(128)S(1)} %pad_add_fusion.place_ref, f32[2,4]{1,0:T(2,128)S(1)} %pad_maximum_fusion.3.coef_ref, bf16[16,128,384]{2,1,0:T(8,128)(2,1)} %all-to-all-done.refs_0_, ...), custom_call_target="tpu_custom_call" | custom-call | tf_op jit(solution)/shard_map/pallas_call | solution.py:251
  119.5 0.1 reshape.149
  119.7 0.3 reshape.150
  120.0 0.1 constant_dynamic-slice_fusion
  120.0 1.9 %collective-permute-start.7 = (bf16[16,36,128]{2,1,0:T(8,128)(2,1)S(1)}, bf16[16,36,128]{2,1,0:T(8,128)(2,1)S(1)}, u32[]{:S(2)}, u32[]{:S(2)}) collective-permute-start(bf16[16,36,128]{2,1,0:T(8,128)(2,1)S(1)} %constant_dynamic-slice_fusion), channel_id=1, source_target_pairs={{0,16},{16,0},{32,48},{48,32},{64,80},{80,64},{96,112},{112,96},{1... | collective-permute-start | bytes 442376 | tf_op jit(solution)/shard_map/ppermute | solution.py:467
  122.0 1.4 collective-permute-done.7
  123.3 0.1 add_convert_fusion
  123.4 12.6 %all_to_all.20 = bf16[16,36,128]{2,1,0:T(8,128)(2,1)S(1)} all-to-all(bf16[16,36,128]{2,1,0:T(8,128)(2,1)S(1)} %add_convert_fusion), channel_id=1, replica_groups=mesh['dp'=32,'fsdp'=16] {'fsdp'}, dimensions={0} | all-to-all | bytes 294912 | tf_op jit(solution)/shard_map/all_to_all | solution.py:468
  136.1 15.2 %all_to_all.21 = bf16[16,36,128]{2,1,0:T(8,128)(2,1)S(1)} all-to-all(bf16[16,36,128]{2,1,0:T(8,128)(2,1)S(1)} %broadcast_in_dim.14), channel_id=1, replica_groups={{0,32,64,96,128,160,192,224,256,288,320,352,384,416,448,480},{16,48,80,..., dimensions={0} | all-to-all | bytes 294912 | tf_op jit(solution)/shard_map/all_to_all | solution.py:471
  151.4 5.3 %collective-permute-start.8 = (f32[36,128]{1,0:T(8,128)S(1)}, f32[36,128]{1,0:T(8,128)S(1)}, u32[]{:S(2)}, u32[]{:S(2)}) collective-permute-start(f32[36,128]{1,0:T(8,128)S(1)} %convert_reduce_fusion), channel_id=1, source_target_pairs={{0,16},{16,0},{32,48},{48,32},{64,80},{80,64},{96,112},{112,96},{1... | collective-permute-start | bytes 55304 | tf_op jit(solution)/shard_map/ppermute | solution.py:480
  156.7 0.7 copy.56
  157.4 0.1 collective-permute-done.8
  157.6 0.6 reshape.152
  158.2 0.7 reshape.151
  (32 shorter events, 0.4 us)
Async XLA Ops:
  6.8 8.9 %copy-start.3 = (bf16[1,2,128,64]{2,3,1,0:T(8,128)(2,1)S(1)}, bf16[1,2,128,64]{2,3,1,0:T(8,128)(2,1)}, u32[]{:S(2)}) copy-start(bf16[1,2,128,64]{2,3,1,0:T(8,128)(2,1)} %param.13) | copy-start | bytes 98308
  6.8 9.0 %copy-start = (bf16[64,1536]{1,0:T(8,128)(2,1)S(1)}, bf16[64,1536]{1,0:T(8,128)(2,1)}, u32[]{:S(2)}) copy-start(bf16[64,1536]{1,0:T(8,128)(2,1)} %refs_19_.1) | copy-start | bytes 589828
  6.8 45.1 %all-to-all-start = ((bf16[16,128,384]{2,1,0:T(8,128)(2,1)}), bf16[16,128,384]{2,1,0:T(8,128)(2,1)}, u32[]{:S(2)}, u32[]{:S(2)}) async-start(bf16[16,128,384]{2,1,0:T(8,128)(2,1)} %shard_map.148), calls=%async_computation | async-start | bytes 3145728 | tf_op jit(solution)/shard_map/all_to_all | solution.py:331
  17.3 73.6 %copy-start.1 = (bf16[1536,64]{0,1:T(8,128)(2,1)S(1)}, bf16[1536,64]{0,1:T(8,128)(2,1)}, u32[]{:S(2)}) copy-start(bf16[1536,64]{0,1:T(8,128)(2,1)} %param.25) | copy-start | bytes 589828
  17.3 73.8 %copy-start.2 = (f32[1,128,64]{1,2,0:T(8,128)S(1)}, f32[1,128,64]{1,2,0:T(8,128)}, u32[]{:S(2)}) copy-start(f32[1,128,64]{1,2,0:T(8,128)} %param.14) | copy-start | bytes 98308
  17.3 73.9 %copy-start.4 = (f32[1536]{0:T(1024)S(1)}, f32[1536]{0:T(1024)}, u32[]{:S(2)}) copy-start(f32[1536]{0:T(1024)} %param.24) | copy-start | bytes 18436
  17.3 74.0 %copy-start.5 = (f32[64]{0:T(128)S(1)}, f32[64]{0:T(128)}, u32[]{:S(2)}) copy-start(f32[64]{0:T(128)} %param.22) | copy-start | bytes 772
  17.4 74.1 %copy-start.6 = (f32[64]{0:T(128)S(1)}, f32[64]{0:T(128)}, u32[]{:S(2)}) copy-start(f32[64]{0:T(128)} %param.23) | copy-start | bytes 772
  53.3 28.1 %collective-permute-start = (bf16[16,96,384]{2,1,0:T(8,128)(2,1)S(1)}, bf16[16,96,384]{2,1,0:T(8,128)(2,1)S(1)}, u32[]{:S(2)}, u32[]{:S(2)}) collective-permute-start(bf16[16,96,384]{2,1,0:T(8,128)(2,1)S(1)} %slice.52), channel_id=1, source_target_pairs={{8,0},{280,16},{40,32},{312,48},{72,64},{344,80},{104,96},{376,112... | collective-permute-start | bytes 3538952 | tf_op jit(solution)/shard_map/ppermute | solution.py:352
  55.7 28.4 %collective-permute-start.1 = (bf16[16,96,384]{2,1,0:T(8,128)(2,1)S(1)}, bf16[16,96,384]{2,1,0:T(8,128)(2,1)}, u32[]{:S(2)}, u32[]{:S(2)}) collective-permute-start(bf16[16,96,384]{2,1,0:T(8,128)(2,1)S(1)} %slice.52), channel_id=1, source_target_pairs={{1,0},{23,16},{33,32},{55,48},{65,64},{87,80},{97,96},{119,112},{1... | collective-permute-start | bytes 3538952 | tf_op jit(solution)/shard_map/ppermute | solution.py:352
  57.8 28.2 %collective-permute-start.2 = (bf16[16,96,384]{2,1,0:T(8,128)(2,1)S(1)}, bf16[16,96,384]{2,1,0:T(8,128)(2,1)}, u32[]{:S(2)}, u32[]{:S(2)}) collective-permute-start(bf16[16,96,384]{2,1,0:T(8,128)(2,1)S(1)} %slice.52), channel_id=1, source_target_pairs={{224,0},{48,16},{0,32},{80,48},{32,64},{112,80},{64,96},{144,112},... | collective-permute-start | bytes 3538952 | tf_op jit(solution)/shard_map/ppermute | solution.py:352
  69.8 23.4 %collective-permute-start.3 = (bf16[16,128,384]{2,1,0:T(8,128)(2,1)}, bf16[16,128,384]{2,1,0:T(8,128)(2,1)}, u32[]{:S(2)}, u32[]{:S(2)}) collective-permute-start(bf16[16,128,384]{2,1,0:T(8,128)(2,1)} %all-to-all-done.refs_0_), channel_id=1, source_target_pairs={{0,16},{16,0},{32,48},{48,32},{64,80},{80,64},{96,112},{112,96},{1... | collective-permute-start | bytes 4718600 | tf_op jit(solution)/shard_map/ppermute | solution.py:357
  74.6 16.9 %all-to-all-start.1 = ((f32[16,2,384]{2,1,0:T(2,128)}), f32[16,2,384]{2,1,0:T(2,128)S(1)}, u32[]{:S(2)}, u32[]{:S(2)}) async-start(f32[16,2,384]{2,1,0:T(2,128)} %copy.50), calls=%async_computation.1 | async-start | bytes 98304 | tf_op jit(solution)/shard_map/all_to_all | solution.py:429
  81.4 14.3 %collective-permute-start.4 = (bf16[16,96,384]{2,1,0:T(8,128)(2,1)S(1)}, bf16[16,96,384]{2,1,0:T(8,128)(2,1)}, u32[]{:S(2)}, u32[]{:S(2)}) collective-permute-start(bf16[16,96,384]{2,1,0:T(8,128)(2,1)S(1)} %collective-permute-done.refs_1_), channel_id=1, source_target_pairs={{0,16},{16,0},{32,48},{48,32},{64,80},{80,64},{96,112},{112,96},{1... | collective-permute-start | bytes 3538952 | tf_op jit(solution)/shard_map/ppermute | solution.py:357
  84.1 11.6 %collective-permute-start.5 = (bf16[16,96,384]{2,1,0:T(8,128)(2,1)}, bf16[16,96,384]{2,1,0:T(8,128)(2,1)}, u32[]{:S(2)}, u32[]{:S(2)}) collective-permute-start(bf16[16,96,384]{2,1,0:T(8,128)(2,1)} %collective-permute-done.1.refs_2_), channel_id=1, source_target_pairs={{0,16},{16,0},{32,48},{48,32},{64,80},{80,64},{96,112},{112,96},{1... | collective-permute-start | bytes 3538952 | tf_op jit(solution)/shard_map/ppermute | solution.py:357
  86.0 9.7 %collective-permute-start.6 = (bf16[16,96,384]{2,1,0:T(8,128)(2,1)}, bf16[16,96,384]{2,1,0:T(8,128)(2,1)}, u32[]{:S(2)}, u32[]{:S(2)}) collective-permute-start(bf16[16,96,384]{2,1,0:T(8,128)(2,1)} %collective-permute-done.2.refs_3_), channel_id=1, source_target_pairs={{0,16},{16,0},{32,48},{48,32},{64,80},{80,64},{96,112},{112,96},{1... | collective-permute-start | bytes 3538952 | tf_op jit(solution)/shard_map/ppermute | solution.py:357
  120.0 3.3 %collective-permute-start.7 = (bf16[16,36,128]{2,1,0:T(8,128)(2,1)S(1)}, bf16[16,36,128]{2,1,0:T(8,128)(2,1)S(1)}, u32[]{:S(2)}, u32[]{:S(2)}) collective-permute-start(bf16[16,36,128]{2,1,0:T(8,128)(2,1)S(1)} %constant_dynamic-slice_fusion), channel_id=1, source_target_pairs={{0,16},{16,0},{32,48},{48,32},{64,80},{80,64},{96,112},{112,96},{1... | collective-permute-start | bytes 442376 | tf_op jit(solution)/shard_map/ppermute | solution.py:467
  151.4 6.2 %collective-permute-start.8 = (f32[36,128]{1,0:T(8,128)S(1)}, f32[36,128]{1,0:T(8,128)S(1)}, u32[]{:S(2)}, u32[]{:S(2)}) collective-permute-start(f32[36,128]{1,0:T(8,128)S(1)} %convert_reduce_fusion), channel_id=1, source_target_pairs={{0,16},{16,0},{32,48},{48,32},{64,80},{80,64},{96,112},{112,96},{1... | collective-permute-start | bytes 55304 | tf_op jit(solution)/shard_map/ppermute | solution.py:480

commit v3 on v0

v3 whole, which is shorter than its diff:
```python
from functools import partial
import math

import jax
import jax.numpy as jnp
from jax import lax
from jax.experimental import pallas as pl
from jax.experimental.pallas import tpu as pltpu
from jax.sharding import PartitionSpec as P

HEAD_DIM = 64
TIME_FEAT = 256
STEPS = 28
LANES = 128
EPS = 1e-06
Y_CHIPS = 8
BF = jnp.bfloat16
F32 = jnp.float32


def dot_nn(a, b):
    return lax.dot_general(a, b, (((1,), (0,)), ((), ())), preferred_element_type=F32)


def dot_nt(a, b):
    return lax.dot_general(a, b, (((1,), (1,)), ((), ())), preferred_element_type=F32)


def dot_tn(a, b):
    return lax.dot_general(a, b, (((0,), (0,)), ((), ())), preferred_element_type=F32)


def row_norm(u):
    return lax.rsqrt(jnp.mean(u * u, axis=-1, keepdims=True) + EPS)


def lane_index():
    return lax.broadcasted_iota(jnp.int32, (1, LANES), 1)


def split_heads(tile):
    even = (lane_index() < HEAD_DIM).astype(F32)
    return jnp.concatenate([tile * even.astype(BF), tile * (1.0 - even).astype(BF)], axis=0)


def head_averager():
    row = lax.broadcasted_iota(jnp.int32, (2 * LANES, LANES), 0) & (LANES - 1)
    col = lax.broadcasted_iota(jnp.int32, (2 * LANES, LANES), 1)
    same = ((row >= HEAD_DIM) == (col >= HEAD_DIM)).astype(F32)
    return (same * (1.0 / HEAD_DIM)).astype(BF)


def head_mean(values, averager):
    high = values.astype(BF)
    low = (values - high.astype(F32)).astype(BF)
    return dot_nn(jnp.concatenate([high, low], axis=1), averager)


def placement():
    z_chips = lax.axis_size("dp") // 4
    d, f = lax.axis_index("dp"), lax.axis_index("fsdp")
    core = lax.rem(d, 2)
    plane = 2 * lax.div(d, 2 * z_chips) + lax.rem(lax.div(d, 2), z_chips)
    return core, plane, (plane + lax.div(f, Y_CHIPS) + 2 * lax.rem(f, Y_CHIPS)) & 3


def load(sources, targets, sems):
    copies = [
        pltpu.make_async_copy(source, target, sems.at[n])
        for n, (source, target) in enumerate(zip(sources, targets, strict=True))
    ]
    for copy in copies:
        copy.start()
    return copies


def modulation(mods, j, which):
    width = mods.shape[1] // 3
    return mods[j : j + 1, which * width : (which + 1) * width]


def turn_time(step_ref, j):
    return (jnp.full((1, 1), step_ref[0], jnp.int32) + (1 - j)).astype(F32) / STEPS


def start_weights(gathered, weights, sems, pieces):
    core, _, color = placement()
    rows = pl.ds(0, weights.shape[3])
    for piece in pieces:
        for side, blocks in ((core, gathered[:4]), (1 - core, gathered[4:])):
            for n, block in enumerate(blocks):
                held = color if n == 0 else (color + jnp.where(side == 0, n, 4 - n)) & 3

                @pl.when(held == piece)
                def _():
                    pltpu.make_async_copy(
                        block.at[:, rows, :], weights.at[side, piece], sems.at[side, piece]
                    ).start()


def wait_weights(gathered, weights, sems, piece):
    for h in range(2):
        pltpu.make_async_copy(
            gathered[0].at[:, pl.ds(0, weights.shape[3]), :],
            weights.at[h, piece],
            sems.at[h, piece],
        ).wait()


def qkv_block(weights, part):
    half = weights.shape[4]
    return jnp.concatenate([weights[h, part].reshape(-1, half) for h in range(2)], axis=1)


def proj_block(weights, h):
    half, rows = weights.shape[4], weights.shape[3] // 2
    return jnp.concatenate(
        [weights[h, 3, :, b * rows : (b + 1) * rows, :].reshape(-1, half) for b in range(2)],
        axis=1,
    )


def tail_back(u, cotangent, wout_ref, fgain):
    dz = dot_nn(cotangent.astype(BF), wout_ref[...]) * fgain
    r = row_norm(u)
    z = u * r
    return r * (dz - z * jnp.mean(dz * z, axis=-1, keepdims=True))


def latent_step(
    current, decay, gate, scale1, hidden, wait, weights, base_u, att, norms, bits, gains, wout_ref,
    fgain, win_ref,
):
    tokens = current.shape[0]
    inner = weights.shape[4] * 2
    tiles = inner // LANES
    averager = head_averager()
    wait("base")
    hidden_grad = tail_back(base_u[...], current, wout_ref, fgain)
    proj_grad = (hidden_grad * gate).astype(BF)
    wait(3)
    blend_grad = jnp.zeros((tokens, inner), F32)
    for h in range(2):
        blend_grad = blend_grad + dot_nt(
            proj_grad[:, h * inner : (h + 1) * inner], proj_block(weights, h)
        )
    blend_grad = blend_grad.astype(BF)

    wait("state")
    grads = [[], [], []]
    for i in range(tiles):
        db = split_heads(blend_grad[:, i * LANES : (i + 1) * LANES])
        a = att[i]
        da = dot_nt(db, bits[2, i])
        ds = a * (da - jnp.sum(da * a, axis=-1, keepdims=True))
        ds = (ds * (1.0 / math.sqrt(HEAD_DIM))).astype(BF)
        grads[2].append(dot_tn(a.astype(BF), db).astype(BF))
        dq = dot_nn(ds, bits[1, i])
        dq = jnp.where(lane_index() < HEAD_DIM, dq[:tokens], dq[tokens:])
        dk = dot_tn(ds, split_heads(bits[0, i]))
        for n, grad in enumerate((dq, dk)):
            dz = grad * gains[n][...]
            z = norms[n, i]
            mean = head_mean(dz * z, averager)
            grads[n].append((norms[2 + n, i] * (dz - z * mean)).astype(BF))
    normed_grad = None
    for part in range(3):
        wait(part)
        term = dot_nt(jnp.concatenate(grads[part], axis=1), qkv_block(weights, part))
        normed_grad = term if normed_grad is None else normed_grad + term

    wait("hidden")
    hid = hidden[...]
    rh = row_norm(hid)
    hn = hid * rh
    dhn = normed_grad * scale1
    total = hidden_grad + rh * (dhn - hn * jnp.mean(dhn * hn, axis=-1, keepdims=True))
    latent_grad = dot_nt(total.astype(BF), win_ref[...])
    return current + (2.0 * latent_grad - current * decay) * (1.0 / STEPS)


def prepare_kernel(*refs):
    sources, outs = refs[:4], refs[4:8]
    blocks, hidden_ref, extra, in_sems = refs[8:12]
    up_wide, down_wide = refs[12:14]
    results, out_sems = refs[14:18], refs[18]
    normed, mods, up, down = results
    core, _, _ = placement()
    tokens, half = hidden_ref.shape[0] // 2, blocks.shape[2]
    extra_rows, shards = extra.shape[2], extra.shape[1]
    rows = pl.ds(sources[2].shape[1] - extra_rows, extra_rows)
    loads = load(
        [sources[0], sources[1], sources[2].at[:, rows, :], sources[3].at[:, rows, :]],
        [blocks, hidden_ref, extra.at[core], extra.at[1 - core]],
        in_sems,
    )

    for copy in loads[2:]:
        copy.wait()
    for h in range(2):
        for f in range(0, shards, 2):
            pair = [extra[h, f + n].astype(F32) for n in range(2)]
            for b in range(2):
                cols = slice((2 * h + b) * half, (2 * h + b + 1) * half)
                up_wide[4 * f : 4 * f + 8, cols] = jnp.concatenate(
                    [block[4 * b : 4 * b + 4] for block in pair], axis=0
                )
            for n in range(2):
                for k in range(3):
                    row = 48 * (f + n) + 24 * h + 8 * k
                    down_wide[row : row + 8, :] = pair[n][8:16, k * LANES : (k + 1) * LANES]
    up[...] = up_wide[...].astype(BF)
    down[...] = down_wide[:, 0 : down.shape[1]].astype(BF)

    for copy in loads[:2]:
        copy.wait()
    per = mods.shape[1] // 3 // half
    for o in range(3 * per):
        offset = 1.0 if o // per == 1 else 0.0
        mods[0:2, o * half : (o + 1) * half] = blocks[o] + offset
    for j in range(2):
        hid = hidden_ref[j * tokens : (j + 1) * tokens, :]
        scaled = hid * row_norm(hid) * modulation(mods, j, 1) + modulation(mods, j, 0)
        normed[j * tokens : (j + 1) * tokens, :] = scaled.astype(BF)
    for copy in load(results, outs, out_sems):
        copy.wait()


def prepare(blocks, hidden, home, other_home):
    rows, width = hidden.shape
    shards, _, half = home.shape
    inner, rank = 2 * half, HEAD_DIM
    results = [
        jax.ShapeDtypeStruct((rows, width), BF),
        jax.ShapeDtypeStruct((8, 3 * width), F32),
        jax.ShapeDtypeStruct((rank, width), BF),
        jax.ShapeDtypeStruct((inner, rank), BF),
    ]
    return pl.pallas_call(
        prepare_kernel,
        out_shape=results,
        in_specs=[HBM] * 4,
        out_specs=[HBM] * 4,
        scratch_shapes=like([blocks, hidden])
        + [
            pltpu.VMEM((2, shards, 16, half), BF),
            DMA((4,)),
            pltpu.VMEM((rank, width), F32),
            pltpu.VMEM((inner, LANES), F32),
        ]
        + like(results)
        + [DMA((4,))],
        compiler_params=pltpu.CompilerParams(vmem_limit_bytes=VMEM_LIMIT),
        cost_estimate=pl.CostEstimate(
            flops=5_000_000, bytes_accessed=8_000_000, transcendentals=0
        ),
    )(blocks, hidden, home, other_home)


def first_kernel(sample_batch, *refs):
    step_ref, gathered, refs = refs[0], refs[1:9], refs[9:]
    sources, refs = refs[:11], refs[11:]
    adjoint_out, packed_out, base_out, att_out, norms_out, bits_out = refs[:6]
    weights, sems, in_sems, out_sems = refs[6:10]
    targets, refs = refs[10:21], refs[21:]
    normed_ref, qgain_ref, kgain_ref, mods, hidden_ref, up_ref, down_ref, adjoint_ref, fgain_ref, wout_ref, win_ref = targets
    (
        base_u,
        att,
        norms,
        bits,
        blended,
        adj_u,
        adj_grad,
        low_grad,
        packed,
    ) = refs
    tokens = adjoint_ref.shape[1]
    inner = 2 * weights.shape[4]
    half = inner // 2
    tiles = inner // LANES
    shards = weights.shape[2]
    turns = [slice(j * tokens, (j + 1) * tokens) for j in range(2)]
    gains = (qgain_ref, kgain_ref)
    early = load(sources[:3], targets[:3], in_sems)
    start_weights(gathered, weights, sems, range(4))
    late = load(sources[3:], targets[3:], in_sems.at[pl.ds(3, 8)])

    def arrived(piece):
        wait_weights(gathered, weights, sems, piece)

    for copy in early:
        copy.wait()
    normed = normed_ref[...]
    averager = head_averager()
    for part in range(2):
        arrived(part)
        raw = dot_nn(normed, qkv_block(weights, part))
        for i in range(tiles):
            x = raw[:, i * LANES : (i + 1) * LANES]
            r = lax.rsqrt(head_mean(x * x, averager) + EPS)
            z = x * r
            n = (z * gains[part][...]).astype(BF)
            for j, rs in enumerate(turns):
                norms[j, part, i] = z[rs]
                norms[j, 2 + part, i] = r[rs]
                bits[j, part, i] = n[rs]
    arrived(2)
    raw = dot_nn(normed, qkv_block(weights, 2)).astype(BF)
    for i in range(tiles):
        for j, rs in enumerate(turns):
            bits[j, 2, i] = raw[rs, i * LANES : (i + 1) * LANES]

    for i in range(tiles):
        for j, rs in enumerate(turns):
            score = dot_nt(split_heads(bits[j, 0, i]), bits[j, 1, i]) * (1.0 / math.sqrt(HEAD_DIM))
            e = jnp.exp(score)
            a = e * (1.0 / jnp.sum(e, axis=-1, keepdims=True))
            att[j, i] = a
            ab = a.astype(BF)
            mixed = dot_nn(
                jnp.concatenate([ab[:tokens], ab[tokens:]], axis=1), split_heads(bits[j, 2, i])
            )
            blended[rs, i * LANES : (i + 1) * LANES] = mixed.astype(BF)

    for copy in late:
        copy.wait()
    fgain = fgain_ref[...]
    gates = [modulation(mods, j, 2) for j in range(2)]
    lowrank = dot_nn(blended[...], down_ref[...]).astype(BF)
    arrived(3)
    for h in range(2):
        cols = slice(h * inner, (h + 1) * inner)
        base = dot_nn(blended[...], proj_block(weights, h))
        extra = dot_nn(lowrank, up_ref[:, cols])
        for j, rs in enumerate(turns):
            gate = gates[j][:, cols]
            u = hidden_ref[rs, cols] + gate * base[rs]
            base_u[j, :, cols] = u
            adj_u[j, :, cols] = u + gate * extra[rs]

    outs = [
        pltpu.make_async_copy(source.at[1], target, out_sems.at[n])
        for n, (source, target) in enumerate(
            ((base_u, base_out), (att, att_out), (norms, norms_out), (bits, bits_out))
        )
    ]
    for copy in outs:
        copy.start()

    def velocity(u):
        return dot_nt((u * row_norm(u) * fgain).astype(BF), wout_ref[...])

    def regression(j, current):
        time = turn_time(step_ref, j)
        sigma = jnp.sqrt(2.0 * (1.0 - time) / time)
        gap = velocity(adj_u[j]) - velocity(base_u[j])
        residual = 2.0 / sigma * gap + sigma * current
        cotangent = 4.0 * residual / (sigma * sample_batch)
        grad = (tail_back(adj_u[j], cotangent, wout_ref, fgain) * gates[j]).astype(BF)
        adj_grad[turns[j], :] = grad
        low_grad[turns[j], :] = dot_nt(grad, up_ref[...]).astype(BF)

    current = adjoint_ref[...].T
    regression(0, current)
    current = latent_step(
        current,
        1.0 / turn_time(step_ref, 0),
        gates[0],
        modulation(mods, 0, 1),
        hidden_ref.at[turns[0], :],
        lambda what: None,
        weights,
        base_u.at[0],
        att.at[0],
        norms.at[0],
        bits.at[0],
        gains,
        wout_ref,
        fgain,
        win_ref,
    )
    regression(1, current)
    adjoint_out[...] = current

    down_grad = dot_tn(blended[...], low_grad[...])
    up_grad = dot_tn(lowrank, adj_grad[...])
    blank = jnp.zeros((8, LANES - down_grad.shape[1]), F32)
    for h in range(2):
        for f in range(shards):
            up_rows = jnp.concatenate(
                [
                    up_grad[4 * f : 4 * f + 4, (2 * h + b) * half : (2 * h + b + 1) * half]
                    for b in range(2)
                ],
                axis=0,
            )
            row = 48 * f + 24 * h
            down_rows = jnp.concatenate(
                [
                    jnp.concatenate([down_grad[row + 8 * k : row + 8 * k + 8], blank], axis=1)
                    for k in range(3)
                ],
                axis=1,
            )
            packed[h, f] = jnp.concatenate([up_rows, down_rows], axis=0).astype(BF)
    for copy in load([packed], [packed_out], in_sems):
        copy.wait()
    for copy in outs:
        copy.wait()


def second_kernel(*refs):
    step_ref, gathered, refs = refs[0], refs[1:9], refs[9:]
    sources, refs = refs[:12], refs[12:]
    adjoint_out, weights, sems, in_sems = refs[:4]
    targets = refs[4:]
    (
        base_u,
        adjoint_ref,
        mods,
        fgain_ref,
        wout_ref,
        att,
        norms,
        bits,
        qgain_ref,
        kgain_ref,
        hidden,
        win_ref,
    ) = targets
    tokens = adjoint_ref.shape[0]
    sources = list(sources)
    sources[10] = sources[10].at[pl.ds(tokens, tokens), :]
    loads = load(sources[:5], targets[:5], in_sems)
    start_weights(gathered, weights, sems, (3,))
    loads += load(sources[5:10], targets[5:10], in_sems.at[pl.ds(5, 5)])
    start_weights(gathered, weights, sems, range(3))
    loads += load(sources[10:], targets[10:], in_sems.at[pl.ds(10, 2)])
    for copy in loads[:5]:
        copy.wait()

    def wait(what):
        if what == "state":
            for copy in loads[5:10]:
                copy.wait()
        elif what == "hidden":
            for copy in loads[10:]:
                copy.wait()
        elif what != "base":
            wait_weights(gathered, weights, sems, what)

    result = latent_step(
        adjoint_ref[...],
        1.0 / turn_time(step_ref, 1),
        modulation(mods, 1, 2),
        modulation(mods, 1, 1),
        hidden,
        wait,
        weights,
        base_u,
        att,
        norms,
        bits,
        (qgain_ref, kgain_ref),
        wout_ref,
        fgain_ref[...],
        win_ref,
    )
    adjoint_out[...] = result.T


VMEM_LIMIT = 60 * 1024 * 1024


def state_shapes(tokens, width, inner):
    tiles = inner // LANES
    return (
        ((tokens, width), F32),
        ((tiles, 2 * tokens, tokens), F32),
        ((4, tiles, tokens, LANES), F32),
        ((3, tiles, tokens, LANES), BF),
    )


VMEM = pl.BlockSpec(memory_space=pltpu.VMEM)
SMEM = pl.BlockSpec(memory_space=pltpu.SMEM)
HBM = pl.BlockSpec(memory_space=pl.ANY)
DMA = pltpu.SemaphoreType.DMA


def like(arrays):
    return [pltpu.VMEM(a.shape, a.dtype) for a in arrays]


def step_pair_first(sample_batch, step, gathered, *rest):
    hidden, adjoint = rest[4], rest[7]
    chan, tokens = adjoint.shape
    rows, width = hidden.shape
    shards, _, half = gathered[0].shape
    per_qkv = width // shards
    inner, rank = 2 * half, HEAD_DIM
    state = state_shapes(tokens, width, inner)
    grads = (2, shards, 16, half)
    return pl.pallas_call(
        partial(first_kernel, sample_batch),
        out_shape=(jax.ShapeDtypeStruct((tokens, chan), F32), jax.ShapeDtypeStruct(grads, BF))
        + tuple(jax.ShapeDtypeStruct(*leaf) for leaf in state),
        in_specs=[SMEM] + [HBM] * (len(gathered) + len(rest)),
        out_specs=(VMEM, HBM) + (HBM,) * len(state),
        scratch_shapes=[
            pltpu.VMEM((2, 4, shards, per_qkv, half), BF),
            DMA((2, 4)),
            DMA((len(rest),)),
            DMA((len(state),)),
        ]
        + like(rest)
        + [pltpu.VMEM((2,) + shape, dtype) for shape, dtype in state]
        + [
            pltpu.VMEM((rows, inner), BF),
            pltpu.VMEM((2, tokens, width), F32),
            pltpu.VMEM((rows, width), BF),
            pltpu.VMEM((rows, rank), BF),
            pltpu.VMEM(grads, BF),
        ],
        compiler_params=pltpu.CompilerParams(vmem_limit_bytes=VMEM_LIMIT),
        cost_estimate=pl.CostEstimate(
            flops=5_000_000_000, bytes_accessed=20_000_000, transcendentals=400_000
        ),
    )(step, *gathered, *rest)


def step_pair_second(step, gathered, *rest):
    adjoint, hidden = rest[1], rest[10]
    tokens, chan = adjoint.shape
    width = hidden.shape[1]
    shards, _, half = gathered[0].shape
    scratch = like(rest)
    scratch[10] = pltpu.VMEM((tokens, width), F32)
    return pl.pallas_call(
        second_kernel,
        out_shape=jax.ShapeDtypeStruct((chan, tokens), F32),
        in_specs=[SMEM] + [HBM] * (len(gathered) + len(rest)),
        out_specs=VMEM,
        scratch_shapes=[
            pltpu.VMEM((2, 4, shards, width // shards, half), BF),
            DMA((2, 4)),
            DMA((len(rest),)),
        ]
        + scratch,
        compiler_params=pltpu.CompilerParams(vmem_limit_bytes=VMEM_LIMIT),
        cost_estimate=pl.CostEstimate(
            flops=3_000_000_000, bytes_accessed=20_000_000, transcendentals=0
        ),
    )(step, *gathered, *rest)


def pieces_kernel(step_ref, *refs):
    sources, out_ref = refs[:5], refs[5]
    targets, extra, out, in_sems, out_sems = refs[6:11], refs[11], refs[12], refs[13], refs[14]
    qkv_ref, proj_ref, time_ref, up_ref, down_ref = targets
    loads = load(sources, targets, in_sems)
    core, plane, _ = placement()
    shards, _, half = out.shape
    rows, per_proj, time_rows = qkv_ref.shape[0], proj_ref.shape[0], time_ref.shape[0]
    owners = time_ref.shape[1] // half
    first = rows + time_rows

    def columns(start):
        return pl.ds(pl.multiple_of(start, LANES), half)

    for copy in loads:
        copy.wait()
    for b in range(2):
        extra[4 * b : 4 * b + 4, :] = up_ref[:, columns((2 * core + b) * half)].astype(F32)
    extra[8:16, :] = jnp.full((8, half), step_ref[0], jnp.int32).astype(F32)
    down = down_ref[...].astype(F32)
    down = jnp.where(core == 0, down[:24], down[24:])
    for k in range(3):
        extra[8:16, k * LANES : k * LANES + down.shape[1]] = down[8 * k : 8 * k + 8]
    extra_bits = extra[...].astype(BF)

    copies = []
    for r in range(shards):
        piece = (plane + r // Y_CHIPS + 2 * (r % Y_CHIPS)) & 3

        @pl.when(piece < 3)
        def _():
            out[r, 0:rows, :] = qkv_ref[:, columns((2 * piece + core) * half)]

        @pl.when(piece == 3)
        def _():
            for b in range(2):
                out[r, b * per_proj : (b + 1) * per_proj, :] = proj_ref[
                    :, columns((2 * core + b) * half)
                ]

        owned = min(r, owners - 1)
        out[r, rows:first, :] = time_ref[:, owned * half : (owned + 1) * half]
        out[r, first : first + 16, :] = extra_bits
        copies.append(pltpu.make_async_copy(out.at[r], out_ref.at[r], out_sems.at[r]))
        copies[-1].start()
    for copy in copies:
        copy.wait()


def pieces_for(step, qkv, proj, time, up, down, shards):
    half = proj.shape[1] // 4
    shape = (shards, qkv.shape[0] + time.shape[0] + 16, half)
    inputs = (qkv, proj, time, up, down)
    return pl.pallas_call(
        pieces_kernel,
        out_shape=jax.ShapeDtypeStruct(shape, BF),
        in_specs=[SMEM] + [HBM] * len(inputs),
        out_specs=HBM,
        scratch_shapes=like(inputs)
        + [pltpu.VMEM((16, half), F32), pltpu.VMEM(shape, BF), DMA((len(inputs),)), DMA((shards,))],
        compiler_params=pltpu.CompilerParams(vmem_limit_bytes=VMEM_LIMIT),
    )(step, *inputs)


def gather_neighbours(home, mods, rows, dp, shards):
    z_chips = dp // 4

    def index(x, y, z, c):
        return ((x // 2 * z_chips + z) * 2 + c) * shards + (x % 2) * Y_CHIPS + y

    def neighbours(dx, dy, dz):
        return [
            (
                index((x + s * dx) % 4, (y + s * dy) % Y_CHIPS, (z + s * dz) % z_chips, c),
                index(x, y, z, c),
            )
            for x in range(4)
            for y in range(Y_CHIPS)
            for z in range(z_chips)
            for c, s in ((0, 1), (1, -1))
        ]

    swap = [(i, i ^ 1) for i in range(dp)]
    piece = home[:, :rows]
    parts = [
        lax.ppermute(piece, ("dp", "fsdp"), neighbours(*step))
        for step in ((0, 0, 1), (0, 1, 0), (-1, 0, 0))
    ]
    home, *parts[:2], mods = lax.optimization_barrier((home, *parts[:2], mods))
    own = [home] + parts
    return own + [lax.ppermute(block, "dp", swap) for block in own], mods


def time_features(upper_time):
    halves = TIME_FEAT // 2
    frequency = jnp.exp(-math.log(10000.0) * jnp.arange(halves, dtype=F32) / halves)
    angles = 1000.0 * upper_time[..., None] * frequency
    return jnp.concatenate([jnp.cos(angles), jnp.sin(angles)], axis=-1).astype(BF)


def per_device(
    states,
    adjoint,
    grid_step_index,
    input_weight,
    timestep_weight,
    query_key_value_weight,
    projection_weight,
    down_factor,
    up_factor,
    query_norm_gain,
    key_norm_gain,
    final_norm_gain,
    output_weight,
):
    dp, shards = lax.axis_size("dp"), lax.axis_size("fsdp")
    sample_batch = dp * shards * states.shape[0]
    core = lax.axis_index("dp") % 2
    tokens, chan = states.shape[2:]
    half = projection_weight.shape[1] // 4
    rows, time_rows = query_key_value_weight.shape[0], timestep_weight.shape[0]

    out = pieces_for(
        grid_step_index,
        query_key_value_weight,
        projection_weight,
        timestep_weight,
        up_factor,
        down_factor,
        shards,
    )
    home = lax.all_to_all(out, "fsdp", 0, 0, tiled=True)
    hidden = jnp.dot(states[0].reshape(2 * tokens, chan), input_weight, preferred_element_type=F32)
    gains = [jnp.tile(gain, 2)[None] for gain in (query_norm_gain, key_norm_gain)]
    fgain, wout = final_norm_gain[None], output_weight.T
    home, hidden, gains, fgain = lax.optimization_barrier((home, hidden, gains, fgain))

    steps = home[:, rows + time_rows + 8, HEAD_DIM].astype(F32)
    turns = jnp.arange(2, dtype=F32)
    feats = time_features((steps[:, None] + 1.0 - turns) / STEPS)
    mods = jnp.dot(
        feats.reshape(2 * shards, TIME_FEAT),
        home[:, rows : rows + time_rows].reshape(TIME_FEAT, half),
        preferred_element_type=F32,
    ).reshape(shards, 2, half)
    mods = lax.all_to_all(mods, "fsdp", 0, 0, tiled=True)
    gathered, mods = gather_neighbours(home, mods, rows, dp, shards)
    normed, mods, up_full, down_full = prepare(mods, hidden, home, gathered[4])

    adjoint_mid, out, base, att, norms, bits = step_pair_first(
        sample_batch,
        grid_step_index,
        gathered,
        normed,
        *gains,
        mods,
        hidden,
        up_full,
        down_full,
        adjoint[0].T,
        fgain,
        wout,
        input_weight,
    )

    swap = [(i, i ^ 1) for i in range(dp)]
    chips = dp // 2
    out = out.reshape((2 * shards,) + out.shape[2:])
    groups = [
        [(2 * i + c) * shards + f for c in range(2) for f in range(shards)] for i in range(chips)
    ]
    got = lax.all_to_all(out, ("dp", "fsdp"), 0, 0, axis_index_groups=groups, tiled=True)
    adjoint_out = step_pair_second(
        grid_step_index,
        gathered,
        base,
        adjoint_mid,
        mods,
        fgain,
        wout,
        att,
        norms,
        bits,
        *gains,
        hidden,
        input_weight,
    )
    got, adjoint_out = lax.optimization_barrier((got, adjoint_out))
    part = jnp.sum(got.astype(F32), axis=0).astype(BF)
    got = lax.all_to_all(
        jnp.broadcast_to(part[None], (chips,) + part.shape),
        "dp",
        0,
        0,
        axis_index_groups=[[2 * i + c for i in range(chips)] for c in range(2)],
        tiled=True,
    )
    mine = jnp.sum(got.astype(F32), axis=0)
    theirs = lax.ppermute(mine, "dp", swap)
    halves = [jnp.where(core == 0, mine, theirs), jnp.where(core == 0, theirs, mine)]
    down_grad = [
        block[8:, k * LANES : k * LANES + HEAD_DIM] for block in halves for k in range(3)
    ]
    up_grad = [block[4 * b : 4 * b + 4] for block in halves for b in range(2)]
    return (
        adjoint_out.T[None],
        jnp.concatenate(down_grad, axis=0),
        jnp.concatenate(up_grad, axis=1),
    )


def solution(mesh):
    in_specs = (
        P(("dp", "fsdp"), None, None, None),
        P(("dp", "fsdp"), None, None),
        P(("dp", "fsdp")),
        P(),
        P("fsdp", None),
        P("fsdp", None),
        P("fsdp", None),
        P("fsdp", None),
        P("fsdp", None),
        P(),
        P(),
        P(),
        P(),
    )
    out_specs = (P(("dp", "fsdp"), None, None), P("fsdp", None), P("fsdp", None))
    return jax.shard_map(
        per_device, mesh=mesh, in_specs=in_specs, out_specs=out_specs, check_vma=False
    )
```

time: 680 us -> 155 us (0.23)
  waiting for transfers between devices: 362 us -> 35.8 us
  blocking collectives: 194 us -> 27.3 us
  matrix products: 64.5 us -> 1.71 us
  starting transfers between devices: 0.19 us -> 48.6 us
  Pallas kernels: 0 us -> 34.6 us
  local copies, waits for them, and re-layouts: 23.8 us -> 3.31 us
  between operations: 16.5 us -> 1.63 us
  other arithmetic: 14.6 us -> 1.18 us
    all_gather x3 -> x0, waiting for transfers between devices: 159 us -> none  [the longest x1 94.4 us: per_device(): lax.all_gather(query_key_value_weight, 'fsdp', axis=0, tiled=True)]
    psum x1 -> x0, blocking collectives: 136 us -> none  [per_device(): lax.psum(part_down.astype(jnp.bfloat16), 'dp').astype(jnp.float32)]
    unnamed x6 -> x0, waiting for transfers between devices: 132 us -> none
    reduce_scatter x1 -> x0, waiting for transfers between devices: 70.8 us -> none  [per_device(): lax.psum_scatter(down_total.astype(jnp.bfloat16), 'fsdp', scatter_dimensi...]
    dot_general x39 -> x2, matrix products: 64.5 us -> 1.71 us  [the longest x1 1.56 us: per_device(): jnp.dot(states[0].reshape(2 * tokens, chan), input_weight, preferred_elem...]
    all_gather x2 -> x0, blocking collectives: 57.6 us -> none  [the longest x1 31.4 us: per_device(): lax.all_gather(down_factor, 'fsdp', axis=0, tiled=True)]
    all_to_all x0 -> x2, waiting for transfers between devices: none -> 35 us  [the longest x1 32.4 us: per_device(): home = lax.all_to_all(out, 'fsdp', 0, 0, tiled=True)]
    pallas_call x0 -> x4, Pallas kernels: none -> 34.6 us  [the longest x1 18.3 us: step_pair_first(): pl.pallas_call(partial(first_kernel, sample_batch), out_shape=(jax.ShapeD...]
  transfers between devices with their start and end apart: 5 -> 10, of which waited for: 5 -> 3; matrix products, arithmetic and copies ran while one was open for 3% -> 3% of each run, Pallas kernels for 0% -> 9%
where the time goes in v3:
time: 155 us; the launch traced here: 154 us
  starting transfers between devices  48.6 us (31%)
  waiting for transfers between devices  35.8 us (23%)
  Pallas kernels  34.6 us (22%)
  blocking collectives  27.3 us (18%)
  local copies, waits for them, and re-layouts  3.31 us (2%)
  matrix products  1.71 us (1%)
  between operations  1.63 us (1%)
    all_to_all x1, waiting for transfers between devices, per_device(): home = lax.all_to_all(out, 'fsdp', 0, 0, tiled=True)  32.4 us
    pallas_call x1, Pallas kernels, step_pair_first(): pl.pallas_call(partial(first_kernel, sample_batch), out_shape=(jax.ShapeD...  18.3 us
    ppermute x4, starting transfers between devices, gather_neighbours(): return (own + [lax.ppermute(block, 'dp', swap) for block in own], mods)  17.8 us
    all_to_all x1, blocking collectives, per_device(): mods = lax.all_to_all(mods, 'fsdp', 0, 0, tiled=True)  14.2 us
    all_to_all x1, blocking collectives, per_device(): lax.all_to_all(jnp.broadcast_to(part[None], (chips,) + part.shape), 'dp',...  13.1 us
    ppermute x3, starting transfers between devices, gather_neighbours(): lax.ppermute(piece, ('dp', 'fsdp'), neighbours(*step))  11.2 us
    pallas_call x1, Pallas kernels, step_pair_second(): pl.pallas_call(second_kernel, out_shape=jax.ShapeDtypeStruct((chan, token...  10.8 us
    all_to_all x1, starting transfers between devices, per_device(): home = lax.all_to_all(out, 'fsdp', 0, 0, tiled=True)  8.83 us
  transfers between devices with their start and end apart: 10, of which 3 were waited for; matrix products, arithmetic and copies ran while one was open for 3% of the time, Pallas kernels for 9%

profile of v3, /device:TPU:1, one launch (start us, length us, event | category | flops | bytes accessed | tf_op | source)
XLA Modules:
  0.0 154.1 jit_solution(6305258197610849138)
XLA Ops:
  1.3 2.5 %shard_map.148 = bf16[16,128,384]{2,1,0:T(8,128)(2,1)} custom-call(s32[1]{0:T(128)S(6)} %copy.31.step_ref.refs_0_, bf16[96,2304]{1,0:T(8,128)(2,1)} %refs_0_.3, bf16[48,1536]{1,0:T(8,128)(2,1)} %refs_1_.1, bf16[16,4608]{1,0:T(8,128)(2,1)} %refs_2_.1, bf16[4,1536]{1,0:T(4,128)(2,1)} %refs_3_.1, bf16[48,64]{1,0:T(8,128)(2,1)} %refs_4_.1), custom_call_target="tpu_custom_call" | custom-call | tf_op jit(solution)/shard_map/pallas_call | solution.py:611
  3.8 0.0 copy-start.3
  3.8 0.0 copy-start.4
  3.8 0.0 copy-start.6
  3.8 0.0 copy-start.7
  3.8 0.0 copy-start.2
  3.8 8.8 %all-to-all-start = ((bf16[16,128,384]{2,1,0:T(8,128)(2,1)}), bf16[16,128,384]{2,1,0:T(8,128)(2,1)S(1)}, u32[]{:S(2)}, u32[]{:S(2)}) async-start(bf16[16,128,384]{2,1,0:T(8,128)(2,1)} %shard_map.148), calls=%async_computation | async-start | bytes 3145728 | tf_op jit(solution)/shard_map/all_to_all | solution.py:689
  12.6 0.0 copy-done.3
  12.7 0.0 copy-done.4
  12.7 0.6 broadcast_in_dim.6.refs_17_.refs_12_
  13.3 0.0 copy-done.6
  13.3 0.6 broadcast_in_dim_tile.6.refs_10_.refs_17_
  13.9 0.0 copy-done.7
  13.9 0.7 broadcast_in_dim_tile.7.refs_11_.refs_18_
  14.6 0.0 copy-done.2
  14.6 1.6 %fusion.refs_1_.refs_13_.refs_19_ = f32[256,1536]{1,0:T(8,128)} fusion(bf16[64,1536]{1,0:T(8,128)(2,1)S(1)} %copy-done.2, bf16[8,8,2,128]{3,2,1,0:T(2,128)(2,1)S(1)} %bitcast.24), kind=kOutput, calls=%fused_computation.1 | convolution fusion | flops 50331648 | bytes 1802240 | tf_op jit(solution)/shard_map/dot_general | solution.py:690
  16.1 32.4 %all-to-all-done.refs_2_.refs_1_ = bf16[16,128,384]{2,1,0:T(8,128)(2,1)S(1)} async-done(((bf16[16,128,384]{2,1,0:T(8,128)(2,1)}), bf16[16,128,384]{2,1,0:T(8,128)(2,1)S(1)}, u32[]{:S(2)}, u32[]{:S(2)}) %all-to-all-start) | async-done | bytes 1572896 | tf_op jit(solution)/shard_map/all_to_all | solution.py:689
  48.5 0.0 copy-start
  48.5 0.1 slice.39
  48.7 4.4 %collective-permute-start = (bf16[16,96,384]{2,1,0:T(8,128)(2,1)S(1)}, bf16[16,96,384]{2,1,0:T(8,128)(2,1)}, u32[]{:S(2)}, u32[]{:S(2)}) collective-permute-start(bf16[16,96,384]{2,1,0:T(8,128)(2,1)S(1)} %slice.39), channel_id=1, source_target_pairs={{32,0},{240,16},{64,32},{16,48},{96,64},{48,80},{128,96},{80,112},... | collective-permute-start | bytes 3538952 | tf_op jit(solution)/shard_map/ppermute | solution.py:643
  53.0 3.4 %collective-permute-start.1 = (bf16[16,96,384]{2,1,0:T(8,128)(2,1)S(1)}, bf16[16,96,384]{2,1,0:T(8,128)(2,1)}, u32[]{:S(2)}, u32[]{:S(2)}) collective-permute-start(bf16[16,96,384]{2,1,0:T(8,128)(2,1)S(1)} %slice.39), channel_id=1, source_target_pairs={{1,0},{23,16},{33,32},{55,48},{65,64},{87,80},{97,96},{119,112},{1... | collective-permute-start | bytes 3538952 | tf_op jit(solution)/shard_map/ppermute | solution.py:643
  56.5 3.4 %collective-permute-start.2 = (bf16[16,96,384]{2,1,0:T(8,128)(2,1)S(1)}, bf16[16,96,384]{2,1,0:T(8,128)(2,1)}, u32[]{:S(2)}, u32[]{:S(2)}) collective-permute-start(bf16[16,96,384]{2,1,0:T(8,128)(2,1)S(1)} %slice.39), channel_id=1, source_target_pairs={{264,0},{24,16},{296,32},{56,48},{328,64},{88,80},{360,96},{120,11... | collective-permute-start | bytes 3538952 | tf_op jit(solution)/shard_map/ppermute | solution.py:643
  59.9 0.3 add_reduce_fusion
  60.3 0.1 fusion.3
  60.4 0.1 fusion.5
  60.6 14.2 %all_to_all.20.refs_0_ = f32[16,2,384]{2,1,0:T(2,128)} all-to-all(f32[16,2,384]{2,1,0:T(2,128)S(1)} %copy.20), channel_id=1, replica_groups=mesh['dp'=32,'fsdp'=16] {'fsdp'}, dimensions={0} | all-to-all | bytes 98304 | tf_op jit(solution)/shard_map/all_to_all | solution.py:703
  74.8 0.0 collective-permute-done.refs_2_
  74.8 0.0 collective-permute-done.1.refs_3_
  74.8 0.0 copy-done
  74.8 11.3 %collective-permute-start.3 = (bf16[16,128,384]{2,1,0:T(8,128)(2,1)S(1)}, bf16[16,128,384]{2,1,0:T(8,128)(2,1)S(1)}, u32[]{:S(2)}, u32[]{:S(2)}) collective-permute-start(bf16[16,128,384]{2,1,0:T(8,128)(2,1)S(1)} %all-to-all-done.refs_2_.refs_1_), channel_id=1, source_target_pairs={{0,16},{16,0},{32,48},{48,32},{64,80},{80,64},{96,112},{112,96},{1... | collective-permute-start | bytes 4718600 | tf_op jit(solution)/shard_map/ppermute | solution.py:648
  86.2 1.9 %collective-permute-start.4 = (bf16[16,96,384]{2,1,0:T(8,128)(2,1)}, bf16[16,96,384]{2,1,0:T(8,128)(2,1)}, u32[]{:S(2)}, u32[]{:S(2)}) collective-permute-start(bf16[16,96,384]{2,1,0:T(8,128)(2,1)} %collective-permute-done.refs_2_), channel_id=1, source_target_pairs={{0,16},{16,0},{32,48},{48,32},{64,80},{80,64},{96,112},{112,96},{1... | collective-permute-start | bytes 3538952 | tf_op jit(solution)/shard_map/ppermute | solution.py:648
  88.1 2.4 %collective-permute-start.5 = (bf16[16,96,384]{2,1,0:T(8,128)(2,1)}, bf16[16,96,384]{2,1,0:T(8,128)(2,1)}, u32[]{:S(2)}, u32[]{:S(2)}) collective-permute-start(bf16[16,96,384]{2,1,0:T(8,128)(2,1)} %collective-permute-done.1.refs_3_), channel_id=1, source_target_pairs={{0,16},{16,0},{32,48},{48,32},{64,80},{80,64},{96,112},{112,96},{1... | collective-permute-start | bytes 3538952 | tf_op jit(solution)/shard_map/ppermute | solution.py:648
  90.5 0.0 collective-permute-done.2.refs_4_
  90.5 2.1 %collective-permute-start.6 = (bf16[16,96,384]{2,1,0:T(8,128)(2,1)}, bf16[16,96,384]{2,1,0:T(8,128)(2,1)}, u32[]{:S(2)}, u32[]{:S(2)}) collective-permute-start(bf16[16,96,384]{2,1,0:T(8,128)(2,1)} %collective-permute-done.2.refs_4_), channel_id=1, source_target_pairs={{0,16},{16,0},{32,48},{48,32},{64,80},{80,64},{96,112},{112,96},{1... | collective-permute-start | bytes 3538952 | tf_op jit(solution)/shard_map/ppermute | solution.py:648
  92.6 0.0 collective-permute-done.3.refs_3_.refs_5_
  92.6 0.0 copy-start.1
  92.7 1.1 copy-done.1
  93.8 3.0 %shard_map.149 = (bf16[256,1536]{1,0:T(8,128)(2,1)}, f32[8,4608]{1,0:T(8,128)}, bf16[64,1536]{1,0:T(8,128)(2,1)}, bf16[768,64]{1,0:T(8,128)(2,1)}) custom-call(f32[16,2,384]{2,1,0:T(2,128)} %all_to_all.20.refs_0_, f32[256,1536]{1,0:T(8,128)} %fusion.refs_1_.refs_13_.refs_19_, bf16[16,128,384]{2,1,0:T(8,128)(2,1)} %copy-done, bf16[16,128,384]{2,1,0:T(8,128)(2,1)} %copy-done.1), custom_call_target="tpu_custom_call" | custom-call | flops 5000000 | bytes 8000000 | tf_op jit(solution)/shard_map/pallas_call | solution.py:239
  96.8 0.0 collective-permute-done.4.refs_6_
  96.9 0.0 collective-permute-done.5.refs_7_
  96.9 0.0 collective-permute-done.6.refs_8_
  96.9 18.3 %shard_map.150 = (f32[128,64]{1,0:T(8,128)}, bf16[2,16,16,384]{3,2,1,0:T(8,128)(2,1)}, f32[128,1536]{1,0:T(8,128)}, f32[6,256,128]{2,1,0:T(8,128)}, f32[4,6,128,...) custom-call(s32[1]{0:T(128)S(6)} %copy.31.step_ref.refs_0_, bf16[16,128,384]{2,1,0:T(8,128)(2,1)} %copy-done, ...), custom_call_target="tpu_custom_call" | custom-call | flops 5000000000 | bytes 20000000 | tf_op jit(solution)/shard_map/pallas_call | solution.py:505
  115.2 6.6 %all-to-all-start.2 = ((bf16[32,16,384]{2,1,0:T(8,128)(2,1)}), bf16[32,16,384]{2,1,0:T(8,128)(2,1)S(1)}, u32[]{:S(2)}, u32[]{:S(2)}) async-start(bf16[32,16,384]{2,1,0:T(8,128)(2,1)} %bitcast.21), calls=%async_computation.2 | async-start | bytes 786432 | tf_op jit(solution)/shard_map/all_to_all | solution.py:729
  121.8 10.8 %shard_map.151 = f32[64,128]{1,0:T(8,128)} custom-call(s32[1]{0:T(128)S(6)} %copy.31.step_ref.refs_0_, bf16[16,128,384]{2,1,0:T(8,128)(2,1)} %copy-done, bf16[16,96,384]{2,1,0:T(8,128)(2,1)} %collective-permute-done.refs_2_, bf16[16,96,384]{2,1,0:T(8,128)(2,1)} %collective-permute-done.1.refs_3_, bf16[16,96,384]{2,1,0:T(8,128)(2,1)} %collective-permute-done.2.refs_4_, ...), custom_call_target="tpu_custom_call" | custom-call | flops 3000000000 | bytes 20000000 | tf_op jit(solution)/shard_map/pallas_call | solution.py:540
  132.6 2.6 %all-to-all-done.2 = bf16[32,16,384]{2,1,0:T(8,128)(2,1)S(1)} async-done(((bf16[32,16,384]{2,1,0:T(8,128)(2,1)}), bf16[32,16,384]{2,1,0:T(8,128)(2,1)S(1)}, u32[]{:S(2)}, u32[]{:S(2)}) %all-to-all-start.2) | async-done | bytes 393248 | tf_op jit(solution)/shard_map/all_to_all | solution.py:729
  135.2 0.1 reduce_sum.21
  135.3 13.1 %all_to_all.21 = bf16[16,16,384]{2,1,0:T(8,128)(2,1)S(1)} all-to-all(bf16[16,16,384]{2,1,0:T(8,128)(2,1)S(1)} %broadcast_in_dim.8), channel_id=1, replica_groups={{0,32,64,96,128,160,192,224,256,288,320,352,384,416,448,480},{16,48,80,..., dimensions={0} | all-to-all | bytes 393216 | tf_op jit(solution)/shard_map/all_to_all | solution.py:747
  148.4 4.2 %collective-permute-start.7 = (f32[16,384]{1,0:T(8,128)S(1)}, f32[16,384]{1,0:T(8,128)S(1)}, u32[]{:S(2)}, u32[]{:S(2)}) collective-permute-start(f32[16,384]{1,0:T(8,128)S(1)} %convert_reduce_fusion), channel_id=1, source_target_pairs={{0,16},{16,0},{32,48},{48,32},{64,80},{80,64},{96,112},{112,96},{1... | collective-permute-start | bytes 73736 | tf_op jit(solution)/shard_map/ppermute | solution.py:756
  152.6 0.8 collective-permute-done.7
  153.5 0.0 copy-start.5
  153.5 0.6 pad_maximum_fusion
  154.1 0.0 copy-done.5
  (17 shorter events, 0.2 us)
Async XLA Ops:
  3.8 8.9 %copy-start.3 = (bf16[1,2,128,64]{2,3,1,0:T(8,128)(2,1)S(1)}, bf16[1,2,128,64]{2,3,1,0:T(8,128)(2,1)}, u32[]{:S(2)}) copy-start(bf16[1,2,128,64]{2,3,1,0:T(8,128)(2,1)} %param.13) | copy-start | bytes 98308
  3.8 8.9 %copy-start.4 = (f32[1536]{0:T(1024)S(1)}, f32[1536]{0:T(1024)}, u32[]{:S(2)}) copy-start(f32[1536]{0:T(1024)} %param.24) | copy-start | bytes 18436
  3.8 9.5 %copy-start.6 = (f32[64]{0:T(128)S(1)}, f32[64]{0:T(128)}, u32[]{:S(2)}) copy-start(f32[64]{0:T(128)} %param.22) | copy-start | bytes 772
  3.8 10.1 %copy-start.7 = (f32[64]{0:T(128)S(1)}, f32[64]{0:T(128)}, u32[]{:S(2)}) copy-start(f32[64]{0:T(128)} %param.23) | copy-start | bytes 772
  3.8 10.8 %copy-start.2 = (bf16[64,1536]{1,0:T(8,128)(2,1)S(1)}, bf16[64,1536]{1,0:T(8,128)(2,1)}, u32[]{:S(2)}) copy-start(bf16[64,1536]{1,0:T(8,128)(2,1)} %refs_20_.1) | copy-start | bytes 589828
  3.8 44.7 %all-to-all-start = ((bf16[16,128,384]{2,1,0:T(8,128)(2,1)}), bf16[16,128,384]{2,1,0:T(8,128)(2,1)S(1)}, u32[]{:S(2)}, u32[]{:S(2)}) async-start(bf16[16,128,384]{2,1,0:T(8,128)(2,1)} %shard_map.148), calls=%async_computation | async-start | bytes 3145728 | tf_op jit(solution)/shard_map/all_to_all | solution.py:689
  48.5 26.3 %copy-start = (bf16[16,128,384]{2,1,0:T(8,128)(2,1)}, bf16[16,128,384]{2,1,0:T(8,128)(2,1)S(1)}, u32[]{:S(2)}) copy-start(bf16[16,128,384]{2,1,0:T(8,128)(2,1)S(1)} %all-to-all-done.refs_2_.refs_1_) | copy-start | bytes 4718596
  48.7 26.2 %collective-permute-start = (bf16[16,96,384]{2,1,0:T(8,128)(2,1)S(1)}, bf16[16,96,384]{2,1,0:T(8,128)(2,1)}, u32[]{:S(2)}, u32[]{:S(2)}) collective-permute-start(bf16[16,96,384]{2,1,0:T(8,128)(2,1)S(1)} %slice.39), channel_id=1, source_target_pairs={{32,0},{240,16},{64,32},{16,48},{96,64},{48,80},{128,96},{80,112},... | collective-permute-start | bytes 3538952 | tf_op jit(solution)/shard_map/ppermute | solution.py:643
  53.0 21.8 %collective-permute-start.1 = (bf16[16,96,384]{2,1,0:T(8,128)(2,1)S(1)}, bf16[16,96,384]{2,1,0:T(8,128)(2,1)}, u32[]{:S(2)}, u32[]{:S(2)}) collective-permute-start(bf16[16,96,384]{2,1,0:T(8,128)(2,1)S(1)} %slice.39), channel_id=1, source_target_pairs={{1,0},{23,16},{33,32},{55,48},{65,64},{87,80},{97,96},{119,112},{1... | collective-permute-start | bytes 3538952 | tf_op jit(solution)/shard_map/ppermute | solution.py:643
  56.5 34.0 %collective-permute-start.2 = (bf16[16,96,384]{2,1,0:T(8,128)(2,1)S(1)}, bf16[16,96,384]{2,1,0:T(8,128)(2,1)}, u32[]{:S(2)}, u32[]{:S(2)}) collective-permute-start(bf16[16,96,384]{2,1,0:T(8,128)(2,1)S(1)} %slice.39), channel_id=1, source_target_pairs={{264,0},{24,16},{296,32},{56,48},{328,64},{88,80},{360,96},{120,11... | collective-permute-start | bytes 3538952 | tf_op jit(solution)/shard_map/ppermute | solution.py:643
  74.8 17.8 %collective-permute-start.3 = (bf16[16,128,384]{2,1,0:T(8,128)(2,1)S(1)}, bf16[16,128,384]{2,1,0:T(8,128)(2,1)S(1)}, u32[]{:S(2)}, u32[]{:S(2)}) collective-permute-start(bf16[16,128,384]{2,1,0:T(8,128)(2,1)S(1)} %all-to-all-done.refs_2_.refs_1_), channel_id=1, source_target_pairs={{0,16},{16,0},{32,48},{48,32},{64,80},{80,64},{96,112},{112,96},{1... | collective-permute-start | bytes 4718600 | tf_op jit(solution)/shard_map/ppermute | solution.py:648
  86.2 10.7 %collective-permute-start.4 = (bf16[16,96,384]{2,1,0:T(8,128)(2,1)}, bf16[16,96,384]{2,1,0:T(8,128)(2,1)}, u32[]{:S(2)}, u32[]{:S(2)}) collective-permute-start(bf16[16,96,384]{2,1,0:T(8,128)(2,1)} %collective-permute-done.refs_2_), channel_id=1, source_target_pairs={{0,16},{16,0},{32,48},{48,32},{64,80},{80,64},{96,112},{112,96},{1... | collective-permute-start | bytes 3538952 | tf_op jit(solution)/shard_map/ppermute | solution.py:648
  88.1 8.8 %collective-permute-start.5 = (bf16[16,96,384]{2,1,0:T(8,128)(2,1)}, bf16[16,96,384]{2,1,0:T(8,128)(2,1)}, u32[]{:S(2)}, u32[]{:S(2)}) collective-permute-start(bf16[16,96,384]{2,1,0:T(8,128)(2,1)} %collective-permute-done.1.refs_3_), channel_id=1, source_target_pairs={{0,16},{16,0},{32,48},{48,32},{64,80},{80,64},{96,112},{112,96},{1... | collective-permute-start | bytes 3538952 | tf_op jit(solution)/shard_map/ppermute | solution.py:648
  90.5 6.3 %collective-permute-start.6 = (bf16[16,96,384]{2,1,0:T(8,128)(2,1)}, bf16[16,96,384]{2,1,0:T(8,128)(2,1)}, u32[]{:S(2)}, u32[]{:S(2)}) collective-permute-start(bf16[16,96,384]{2,1,0:T(8,128)(2,1)} %collective-permute-done.2.refs_4_), channel_id=1, source_target_pairs={{0,16},{16,0},{32,48},{48,32},{64,80},{80,64},{96,112},{112,96},{1... | collective-permute-start | bytes 3538952 | tf_op jit(solution)/shard_map/ppermute | solution.py:648
  92.6 1.2 copy-start.1
  115.2 20.0 %all-to-all-start.2 = ((bf16[32,16,384]{2,1,0:T(8,128)(2,1)}), bf16[32,16,384]{2,1,0:T(8,128)(2,1)S(1)}, u32[]{:S(2)}, u32[]{:S(2)}) async-start(bf16[32,16,384]{2,1,0:T(8,128)(2,1)} %bitcast.21), calls=%async_computation.2 | async-start | bytes 786432 | tf_op jit(solution)/shard_map/all_to_all | solution.py:729
  148.4 5.0 %collective-permute-start.7 = (f32[16,384]{1,0:T(8,128)S(1)}, f32[16,384]{1,0:T(8,128)S(1)}, u32[]{:S(2)}, u32[]{:S(2)}) collective-permute-start(f32[16,384]{1,0:T(8,128)S(1)} %convert_reduce_fusion), channel_id=1, source_target_pairs={{0,16},{16,0},{32,48},{48,32},{64,80},{80,64},{96,112},{112,96},{1... | collective-permute-start | bytes 73736 | tf_op jit(solution)/shard_map/ppermute | solution.py:756
  153.5 0.6 copy-start.5

commit v4 on v3

--- a/solution.py
+++ b/solution.py
@@ -179,92 +179,20 @@
     return current + (2.0 * latent_grad - current * decay) * (1.0 / STEPS)
 
 
-def prepare_kernel(*refs):
-    sources, outs = refs[:4], refs[4:8]
-    blocks, hidden_ref, extra, in_sems = refs[8:12]
-    up_wide, down_wide = refs[12:14]
-    results, out_sems = refs[14:18], refs[18]
-    normed, mods, up, down = results
-    core, _, _ = placement()
-    tokens, half = hidden_ref.shape[0] // 2, blocks.shape[2]
-    extra_rows, shards = extra.shape[2], extra.shape[1]
-    rows = pl.ds(sources[2].shape[1] - extra_rows, extra_rows)
-    loads = load(
-        [sources[0], sources[1], sources[2].at[:, rows, :], sources[3].at[:, rows, :]],
-        [blocks, hidden_ref, extra.at[core], extra.at[1 - core]],
-        in_sems,
-    )
-
-    for copy in loads[2:]:
-        copy.wait()
-    for h in range(2):
-        for f in range(0, shards, 2):
-            pair = [extra[h, f + n].astype(F32) for n in range(2)]
-            for b in range(2):
-                cols = slice((2 * h + b) * half, (2 * h + b + 1) * half)
-                up_wide[4 * f : 4 * f + 8, cols] = jnp.concatenate(
-                    [block[4 * b : 4 * b + 4] for block in pair], axis=0
-                )
-            for n in range(2):
-                for k in range(3):
-                    row = 48 * (f + n) + 24 * h + 8 * k
-                    down_wide[row : row + 8, :] = pair[n][8:16, k * LANES : (k + 1) * LANES]
-    up[...] = up_wide[...].astype(BF)
-    down[...] = down_wide[:, 0 : down.shape[1]].astype(BF)
-
-    for copy in loads[:2]:
-        copy.wait()
-    per = mods.shape[1] // 3 // half
-    for o in range(3 * per):
-        offset = 1.0 if o // per == 1 else 0.0
-        mods[0:2, o * half : (o + 1) * half] = blocks[o] + offset
-    for j in range(2):
-        hid = hidden_ref[j * tokens : (j + 1) * tokens, :]
-        scaled = hid * row_norm(hid) * modulation(mods, j, 1) + modulation(mods, j, 0)
-        normed[j * tokens : (j + 1) * tokens, :] = scaled.astype(BF)
-    for copy in load(results, outs, out_sems):
-        copy.wait()
-
-
-def prepare(blocks, hidden, home, other_home):
-    rows, width = hidden.shape
-    shards, _, half = home.shape
-    inner, rank = 2 * half, HEAD_DIM
-    results = [
-        jax.ShapeDtypeStruct((rows, width), BF),
-        jax.ShapeDtypeStruct((8, 3 * width), F32),
-        jax.ShapeDtypeStruct((rank, width), BF),
-        jax.ShapeDtypeStruct((inner, rank), BF),
-    ]
-    return pl.pallas_call(
-        prepare_kernel,
-        out_shape=results,
-        in_specs=[HBM] * 4,
-        out_specs=[HBM] * 4,
-        scratch_shapes=like([blocks, hidden])
-        + [
-            pltpu.VMEM((2, shards, 16, half), BF),
-            DMA((4,)),
-            pltpu.VMEM((rank, width), F32),
-            pltpu.VMEM((inner, LANES), F32),
-        ]
-        + like(results)
-        + [DMA((4,))],
-        compiler_params=pltpu.CompilerParams(vmem_limit_bytes=VMEM_LIMIT),
-        cost_estimate=pl.CostEstimate(
-            flops=5_000_000, bytes_accessed=8_000_000, transcendentals=0
-        ),
-    )(blocks, hidden, home, other_home)
-
-
 def first_kernel(sample_batch, *refs):
     step_ref, gathered, refs = refs[0], refs[1:9], refs[9:]
-    sources, refs = refs[:11], refs[11:]
-    adjoint_out, packed_out, base_out, att_out, norms_out, bits_out = refs[:6]
-    weights, sems, in_sems, out_sems = refs[6:10]
-    targets, refs = refs[10:21], refs[21:]
-    normed_ref, qgain_ref, kgain_ref, mods, hidden_ref, up_ref, down_ref, adjoint_ref, fgain_ref, wout_ref, win_ref = targets
+    sources, refs = refs[:8], refs[8:]
+    adjoint_out, packed_out, base_out, att_out, norms_out, bits_out, mods_out = refs[:7]
+    weights, sems, in_sems, extra_sems, out_sems = refs[7:12]
+    targets, refs = refs[12:20], refs[20:]
+    hidden_ref, blocks, qgain_ref, kgain_ref, adjoint_ref, fgain_ref, wout_ref, win_ref = targets
     (
+        mods,
+        extra,
+        up_wide,
+        up_ref,
+        down_wide,
+        down_ref,
         base_u,
         att,
         norms,
@@ -282,16 +210,32 @@
     shards = weights.shape[2]
     turns = [slice(j * tokens, (j + 1) * tokens) for j in range(2)]
     gains = (qgain_ref, kgain_ref)
-    early = load(sources[:3], targets[:3], in_sems)
+    core, _, _ = placement()
+    early = load(sources[:4], targets[:4], in_sems)
     start_weights(gathered, weights, sems, range(4))
-    late = load(sources[3:], targets[3:], in_sems.at[pl.ds(3, 8)])
+    extra_rows = pl.ds(gathered[0].shape[1] - extra.shape[2], extra.shape[2])
+    late = load(
+        [gathered[n].at[:, extra_rows, :] for n in (0, 4)],
+        [extra.at[core], extra.at[1 - core]],
+        extra_sems,
+    )
+    late += load(sources[4:], targets[4:], in_sems.at[pl.ds(4, 4)])
 
     def arrived(piece):
         wait_weights(gathered, weights, sems, piece)
 
     for copy in early:
         copy.wait()
-    normed = normed_ref[...]
+    per = mods.shape[1] // 3 // half
+    for o in range(3 * per):
+        offset = 1.0 if o // per == 1 else 0.0
+        mods[0:2, o * half : (o + 1) * half] = blocks[o] + offset
+    normed = []
+    for j, rs in enumerate(turns):
+        hid = hidden_ref[rs, :]
+        scaled = hid * row_norm(hid) * modulation(mods, j, 1) + modulation(mods, j, 0)
+        normed.append(scaled.astype(BF))
+    normed = jnp.concatenate(normed, axis=0)
     averager = head_averager()
     for part in range(2):
         arrived(part)
@@ -325,6 +269,21 @@
 
     for copy in late:
         copy.wait()
+    for h in range(2):
+        for f in range(0, shards, 2):
+            pair = [extra[h, f + n].astype(F32) for n in range(2)]
+            for b in range(2):
+                cols = slice((2 * h + b) * half, (2 * h + b + 1) * half)
+                up_wide[4 * f : 4 * f + 8, cols] = jnp.concatenate(
+                    [block[4 * b : 4 * b + 4] for block in pair], axis=0
+                )
+            for n in range(2):
+                for k in range(3):
+                    row = 48 * (f + n) + 24 * h + 8 * k
+                    down_wide[row : row + 8, :] = pair[n][8:16, k * LANES : (k + 1) * LANES]
+    up_ref[...] = up_wide[...].astype(BF)
+    down_ref[...] = down_wide[:, 0 : down_ref.shape[1]].astype(BF)
+
     fgain = fgain_ref[...]
     gates = [modulation(mods, j, 2) for j in range(2)]
     lowrank = dot_nn(blended[...], down_ref[...]).astype(BF)
@@ -345,6 +304,7 @@
             ((base_u, base_out), (att, att_out), (norms, norms_out), (bits, bits_out))
         )
     ]
+    outs.append(pltpu.make_async_copy(mods, mods_out, out_sems.at[4]))
     for copy in outs:
         copy.start()
 
@@ -494,7 +454,7 @@
 
 
 def step_pair_first(sample_batch, step, gathered, *rest):
-    hidden, adjoint = rest[4], rest[7]
+    hidden, adjoint = rest[0], rest[4]
     chan, tokens = adjoint.shape
     rows, width = hidden.shape
     shards, _, half = gathered[0].shape
@@ -502,19 +462,30 @@
     inner, rank = 2 * half, HEAD_DIM
     state = state_shapes(tokens, width, inner)
     grads = (2, shards, 16, half)
+    mods = (8, 3 * width)
     return pl.pallas_call(
         partial(first_kernel, sample_batch),
         out_shape=(jax.ShapeDtypeStruct((tokens, chan), F32), jax.ShapeDtypeStruct(grads, BF))
-        + tuple(jax.ShapeDtypeStruct(*leaf) for leaf in state),
+        + tuple(jax.ShapeDtypeStruct(*leaf) for leaf in state)
+        + (jax.ShapeDtypeStruct(mods, F32),),
         in_specs=[SMEM] + [HBM] * (len(gathered) + len(rest)),
-        out_specs=(VMEM, HBM) + (HBM,) * len(state),
+        out_specs=(VMEM, HBM) + (HBM,) * (len(state) + 1),
         scratch_shapes=[
             pltpu.VMEM((2, 4, shards, per_qkv, half), BF),
             DMA((2, 4)),
             DMA((len(rest),)),
-            DMA((len(state),)),
+            DMA((2,)),
+            DMA((len(state) + 1,)),
         ]
         + like(rest)
+        + [
+            pltpu.VMEM(mods, F32),
+            pltpu.VMEM(grads, BF),
+            pltpu.VMEM((rank, width), F32),
+            pltpu.VMEM((rank, width), BF),
+            pltpu.VMEM((inner, LANES), F32),
+            pltpu.VMEM((inner, rank), BF),
+        ]
         + [pltpu.VMEM((2,) + shape, dtype) for shape, dtype in state]
         + [
             pltpu.VMEM((rows, inner), BF),
@@ -702,18 +673,14 @@
     ).reshape(shards, 2, half)
     mods = lax.all_to_all(mods, "fsdp", 0, 0, tiled=True)
     gathered, mods = gather_neighbours(home, mods, rows, dp, shards)
-    normed, mods, up_full, down_full = prepare(mods, hidden, home, gathered[4])
-
-    adjoint_mid, out, base, att, norms, bits = step_pair_first(
+
+    adjoint_mid, out, base, att, norms, bits, mods = step_pair_first(
         sample_batch,
         grid_step_index,
         gathered,
-        normed,
+        hidden,
+        mods,
         *gains,
-        mods,
-        hidden,
-        up_full,
-        down_full,
         adjoint[0].T,
         fgain,
         wout,

time: 155 us -> 155 us (level)
  waiting for transfers between devices: 35.8 us -> 38.4 us
  Pallas kernels: 34.6 us -> 32.4 us
    pallas_call x1 -> x0, Pallas kernels: 3.04 us -> none  [prepare(): pl.pallas_call(prepare_kernel, out_shape=results, in_specs=[HBM] * 4, out...]
    ppermute x4, waiting for transfers between devices: 0.01 us -> 2.61 us  [gather_neighbours(): return (own + [lax.ppermute(block, 'dp', swap) for block in own], mods)]
  transfers between devices with their start and end apart: 10 -> 10, of which waited for: 3 -> 5; matrix products, arithmetic and copies ran while one was open for 3% -> 3% of each run, Pallas kernels for 9% -> 7%
where the time goes in v4:
time: 155 us
  starting transfers between devices  48.5 us (31%)
  waiting for transfers between devices  38.4 us (25%)
  Pallas kernels  32.4 us (21%)
  blocking collectives  27.1 us (17%)
  local copies, waits for them, and re-layouts  3.62 us (2%)
  matrix products  1.7 us (1%)
  between operations  1.67 us (1%)
    all_to_all x1, waiting for transfers between devices, per_device(): home = lax.all_to_all(out, 'fsdp', 0, 0, tiled=True)  32.4 us
    pallas_call x1, Pallas kernels, step_pair_first(): pl.pallas_call(partial(first_kernel, sample_batch), out_shape=(jax.ShapeD...  19.2 us
    ppermute x4, starting transfers between devices, gather_neighbours(): return (own + [lax.ppermute(block, 'dp', swap) for block in own], mods)  17.8 us
    all_to_all x1, blocking collectives, per_device(): mods = lax.all_to_all(mods, 'fsdp', 0, 0, tiled=True)  14.2 us
    all_to_all x1, blocking collectives, per_device(): lax.all_to_all(jnp.broadcast_to(part[None], (chips,) + part.shape), 'dp',...  12.9 us
    ppermute x3, starting transfers between devices, gather_neighbours(): lax.ppermute(piece, ('dp', 'fsdp'), neighbours(*step))  11.2 us
    pallas_call x1, Pallas kernels, step_pair_second(): pl.pallas_call(second_kernel, out_shape=jax.ShapeDtypeStruct((chan, token...  10.8 us
    all_to_all x1, starting transfers between devices, per_device(): home = lax.all_to_all(out, 'fsdp', 0, 0, tiled=True)  8.83 us
  transfers between devices with their start and end apart: 10, of which 5 were waited for; matrix products, arithmetic and copies ran while one was open for 3% of the time, Pallas kernels for 7%

profile of v4, /device:TPU:1, one launch (start us, length us, event | category | flops | bytes accessed | tf_op | source)
XLA Modules:
  0.0 154.6 jit_solution(9876366603335332252)
XLA Ops:
  1.3 2.5 %shard_map.148 = bf16[16,128,384]{2,1,0:T(8,128)(2,1)} custom-call(s32[1]{0:T(128)S(6)} %copy.31.step_ref.refs_0_, bf16[96,2304]{1,0:T(8,128)(2,1)} %refs_0_.3, bf16[48,1536]{1,0:T(8,128)(2,1)} %refs_1_.1, bf16[16,4608]{1,0:T(8,128)(2,1)} %refs_2_.1, bf16[4,1536]{1,0:T(4,128)(2,1)} %refs_3_.1, bf16[48,64]{1,0:T(8,128)(2,1)} %refs_4_.1), custom_call_target="tpu_custom_call" | custom-call | tf_op jit(solution)/shard_map/pallas_call | solution.py:582
  3.7 0.0 copy-start.9
  3.8 0.0 copy-start.10
  3.8 0.0 copy-start.12
  3.8 0.0 copy-start.13
  3.8 0.0 copy-start.8
  3.8 8.8 %all-to-all-start = ((bf16[16,128,384]{2,1,0:T(8,128)(2,1)}), bf16[16,128,384]{2,1,0:T(8,128)(2,1)S(1)}, u32[]{:S(2)}, u32[]{:S(2)}) async-start(bf16[16,128,384]{2,1,0:T(8,128)(2,1)} %shard_map.148), calls=%async_computation | async-start | bytes 3145728 | tf_op jit(solution)/shard_map/all_to_all | solution.py:660
  12.6 0.0 copy-done.9
  12.7 0.0 copy-done.10
  12.7 0.6 broadcast_in_dim.6.refs_14_.refs_12_
  13.3 0.0 copy-done.12
  13.3 0.6 broadcast_in_dim_tile.6.refs_11_.refs_17_
  13.9 0.0 copy-done.13
  13.9 0.6 broadcast_in_dim_tile.7.refs_12_.refs_18_
  14.5 0.0 copy-done.8
  14.5 1.6 %fusion.refs_9_.refs_19_ = f32[256,1536]{1,0:T(8,128)} fusion(bf16[64,1536]{1,0:T(8,128)(2,1)S(1)} %copy-done.8, bf16[8,8,2,128]{3,2,1,0:T(2,128)(2,1)S(1)} %bitcast.24), kind=kOutput, calls=%fused_computation.1 | convolution fusion | flops 50331648 | bytes 1802240 | tf_op jit(solution)/shard_map/dot_general | solution.py:661
  16.1 32.4 %all-to-all-done.refs_1_ = bf16[16,128,384]{2,1,0:T(8,128)(2,1)S(1)} async-done(((bf16[16,128,384]{2,1,0:T(8,128)(2,1)}), bf16[16,128,384]{2,1,0:T(8,128)(2,1)S(1)}, u32[]{:S(2)}, u32[]{:S(2)}) %all-to-all-start) | async-done | bytes 1572896 | tf_op jit(solution)/shard_map/all_to_all | solution.py:660
  48.5 0.0 copy-start
  48.5 0.1 slice.39
  48.6 4.4 %collective-permute-start = (bf16[16,96,384]{2,1,0:T(8,128)(2,1)S(1)}, bf16[16,96,384]{2,1,0:T(8,128)(2,1)S(1)}, u32[]{:S(2)}, u32[]{:S(2)}) collective-permute-start(bf16[16,96,384]{2,1,0:T(8,128)(2,1)S(1)} %slice.39), channel_id=1, source_target_pairs={{32,0},{240,16},{64,32},{16,48},{96,64},{48,80},{128,96},{80,112},... | collective-permute-start | bytes 3538952 | tf_op jit(solution)/shard_map/ppermute | solution.py:614
  53.0 3.4 %collective-permute-start.1 = (bf16[16,96,384]{2,1,0:T(8,128)(2,1)S(1)}, bf16[16,96,384]{2,1,0:T(8,128)(2,1)S(1)}, u32[]{:S(2)}, u32[]{:S(2)}) collective-permute-start(bf16[16,96,384]{2,1,0:T(8,128)(2,1)S(1)} %slice.39), channel_id=1, source_target_pairs={{1,0},{23,16},{33,32},{55,48},{65,64},{87,80},{97,96},{119,112},{1... | collective-permute-start | bytes 3538952 | tf_op jit(solution)/shard_map/ppermute | solution.py:614
  56.5 3.4 %collective-permute-start.2 = (bf16[16,96,384]{2,1,0:T(8,128)(2,1)S(1)}, bf16[16,96,384]{2,1,0:T(8,128)(2,1)S(1)}, u32[]{:S(2)}, u32[]{:S(2)}) collective-permute-start(bf16[16,96,384]{2,1,0:T(8,128)(2,1)S(1)} %slice.39), channel_id=1, source_target_pairs={{264,0},{24,16},{296,32},{56,48},{328,64},{88,80},{360,96},{120,11... | collective-permute-start | bytes 3538952 | tf_op jit(solution)/shard_map/ppermute | solution.py:614
  59.9 0.3 add_reduce_fusion
  60.2 0.1 fusion.3
  60.4 0.1 fusion.5
  60.6 14.2 %all_to_all.20.refs_10_ = f32[16,2,384]{2,1,0:T(2,128)} all-to-all(f32[16,2,384]{2,1,0:T(2,128)S(1)} %copy.20), channel_id=1, replica_groups=mesh['dp'=32,'fsdp'=16] {'fsdp'}, dimensions={0} | all-to-all | bytes 98304 | tf_op jit(solution)/shard_map/all_to_all | solution.py:674
  74.8 0.0 collective-permute-done.refs_2_
  74.8 0.0 copy-start.2
  74.8 0.0 collective-permute-done.1.refs_3_
  74.8 0.0 copy-done
  74.8 0.0 copy-start.3
  74.8 11.3 %collective-permute-start.3 = (bf16[16,128,384]{2,1,0:T(8,128)(2,1)S(1)}, bf16[16,128,384]{2,1,0:T(8,128)(2,1)S(1)}, u32[]{:S(2)}, u32[]{:S(2)}) collective-permute-start(bf16[16,128,384]{2,1,0:T(8,128)(2,1)S(1)} %all-to-all-done.refs_1_), channel_id=1, source_target_pairs={{0,16},{16,0},{32,48},{48,32},{64,80},{80,64},{96,112},{112,96},{1... | collective-permute-start | bytes 4718600 | tf_op jit(solution)/shard_map/ppermute | solution.py:619
  86.2 1.9 %collective-permute-start.4 = (bf16[16,96,384]{2,1,0:T(8,128)(2,1)S(1)}, bf16[16,96,384]{2,1,0:T(8,128)(2,1)S(1)}, u32[]{:S(2)}, u32[]{:S(2)}) collective-permute-start(bf16[16,96,384]{2,1,0:T(8,128)(2,1)S(1)} %collective-permute-done.refs_2_), channel_id=1, source_target_pairs={{0,16},{16,0},{32,48},{48,32},{64,80},{80,64},{96,112},{112,96},{1... | collective-permute-start | bytes 3538952 | tf_op jit(solution)/shard_map/ppermute | solution.py:619
  88.1 2.4 %collective-permute-start.5 = (bf16[16,96,384]{2,1,0:T(8,128)(2,1)S(1)}, bf16[16,96,384]{2,1,0:T(8,128)(2,1)S(1)}, u32[]{:S(2)}, u32[]{:S(2)}) collective-permute-start(bf16[16,96,384]{2,1,0:T(8,128)(2,1)S(1)} %collective-permute-done.1.refs_3_), channel_id=1, source_target_pairs={{0,16},{16,0},{32,48},{48,32},{64,80},{80,64},{96,112},{112,96},{1... | collective-permute-start | bytes 3538952 | tf_op jit(solution)/shard_map/ppermute | solution.py:619
  90.5 0.0 collective-permute-done.2.refs_4_
  90.5 0.0 copy-start.4
  90.5 2.1 %collective-permute-start.6 = (bf16[16,96,384]{2,1,0:T(8,128)(2,1)S(1)}, bf16[16,96,384]{2,1,0:T(8,128)(2,1)S(1)}, u32[]{:S(2)}, u32[]{:S(2)}) collective-permute-start(bf16[16,96,384]{2,1,0:T(8,128)(2,1)S(1)} %collective-permute-done.2.refs_4_), channel_id=1, source_target_pairs={{0,16},{16,0},{32,48},{48,32},{64,80},{80,64},{96,112},{112,96},{1... | collective-permute-start | bytes 3538952 | tf_op jit(solution)/shard_map/ppermute | solution.py:619
  92.6 0.0 collective-permute-done.4.refs_6_
  92.7 0.0 copy-start.5
  92.7 0.3 collective-permute-done.5.refs_7_
  93.0 0.0 copy-start.6
  93.0 2.3 %collective-permute-done.6.refs_8_ = bf16[16,96,384]{2,1,0:T(8,128)(2,1)S(1)} collective-permute-done((bf16[16,96,384]{2,1,0:T(8,128)(2,1)S(1)}, bf16[16,96,384]{2,1,0:T(8,128)(2,1)S(1)}, u32[]{:S(2)}, u32[]{:S(2)}) %collective-permute-start.6) | collective-permute-done | bytes 1179680 | tf_op jit(solution)/shard_map/ppermute | solution.py:619
  95.3 0.0 copy-start.7
  95.3 0.0 collective-permute-done.3.refs_5_
  95.3 0.0 copy-done.2
  95.3 0.0 copy-start.1
  95.3 0.0 copy-done.3
  95.3 0.0 copy-done.4
  95.3 0.0 copy-done.5
  95.3 0.0 copy-done.6
  95.3 1.0 copy-done.7
  96.4 0.4 copy-done.1
  96.8 19.2 %shard_map.149 = (f32[128,64]{1,0:T(8,128)}, bf16[2,16,16,384]{3,2,1,0:T(8,128)(2,1)}, f32[128,1536]{1,0:T(8,128)}, f32[6,256,128]{2,1,0:T(8,128)}, f32[4,6,128,...) custom-call(s32[1]{0:T(128)S(6)} %copy.31.step_ref.refs_0_, bf16[16,128,384]{2,1,0:T(8,128)(2,1)} %copy-done, ...), custom_call_target="tpu_custom_call" | custom-call | flops 5000000000 | bytes 20000000 | tf_op jit(solution)/shard_map/pallas_call | solution.py:466
  116.0 6.5 %all-to-all-start.2 = ((bf16[32,16,384]{2,1,0:T(8,128)(2,1)}), bf16[32,16,384]{2,1,0:T(8,128)(2,1)S(1)}, u32[]{:S(2)}, u32[]{:S(2)}) async-start(bf16[32,16,384]{2,1,0:T(8,128)(2,1)} %bitcast.21), calls=%async_computation.2 | async-start | bytes 786432 | tf_op jit(solution)/shard_map/all_to_all | solution.py:696
  122.5 10.8 %shard_map.150 = f32[64,128]{1,0:T(8,128)} custom-call(s32[1]{0:T(128)S(6)} %copy.31.step_ref.refs_0_, bf16[16,128,384]{2,1,0:T(8,128)(2,1)} %copy-done, bf16[16,96,384]{2,1,0:T(8,128)(2,1)} %copy-done.2, bf16[16,96,384]{2,1,0:T(8,128)(2,1)} %copy-done.3, bf16[16,96,384]{2,1,0:T(8,128)(2,1)} %copy-done.4, bf16[16,128,384]{2,1,0:T(8,128)(2,1)} %copy-done.1, ...), custom_call_target="tpu_custom_call" | custom-call | flops 3000000000 | bytes 20000000 | tf_op jit(solution)/shard_map/pallas_call | solution.py:511
  133.3 2.6 %all-to-all-done.2 = bf16[32,16,384]{2,1,0:T(8,128)(2,1)S(1)} async-done(((bf16[32,16,384]{2,1,0:T(8,128)(2,1)}), bf16[32,16,384]{2,1,0:T(8,128)(2,1)S(1)}, u32[]{:S(2)}, u32[]{:S(2)}) %all-to-all-start.2) | async-done | bytes 393248 | tf_op jit(solution)/shard_map/all_to_all | solution.py:696
  135.9 0.1 reduce_sum.21
  136.0 12.9 %all_to_all.21 = bf16[16,16,384]{2,1,0:T(8,128)(2,1)S(1)} all-to-all(bf16[16,16,384]{2,1,0:T(8,128)(2,1)S(1)} %broadcast_in_dim.8), channel_id=1, replica_groups={{0,32,64,96,128,160,192,224,256,288,320,352,384,416,448,480},{16,48,80,..., dimensions={0} | all-to-all | bytes 393216 | tf_op jit(solution)/shard_map/all_to_all | solution.py:714
  148.9 4.2 %collective-permute-start.7 = (f32[16,384]{1,0:T(8,128)S(1)}, f32[16,384]{1,0:T(8,128)S(1)}, u32[]{:S(2)}, u32[]{:S(2)}) collective-permute-start(f32[16,384]{1,0:T(8,128)S(1)} %convert_reduce_fusion), channel_id=1, source_target_pairs={{0,16},{16,0},{32,48},{48,32},{64,80},{80,64},{96,112},{112,96},{1... | collective-permute-start | bytes 73736 | tf_op jit(solution)/shard_map/ppermute | solution.py:723
  153.1 0.8 collective-permute-done.7
  154.0 0.0 copy-start.11
  154.0 0.6 pad_maximum_fusion
  154.6 0.0 copy-done.11
  (17 shorter events, 0.2 us)
Async XLA Ops:
  3.7 8.9 %copy-start.9 = (bf16[1,2,128,64]{2,3,1,0:T(8,128)(2,1)S(1)}, bf16[1,2,128,64]{2,3,1,0:T(8,128)(2,1)}, u32[]{:S(2)}) copy-start(bf16[1,2,128,64]{2,3,1,0:T(8,128)(2,1)} %param.13) | copy-start | bytes 98308
  3.8 8.9 %copy-start.10 = (f32[1536]{0:T(1024)S(1)}, f32[1536]{0:T(1024)}, u32[]{:S(2)}) copy-start(f32[1536]{0:T(1024)} %param.24) | copy-start | bytes 18436
  3.8 9.5 %copy-start.12 = (f32[64]{0:T(128)S(1)}, f32[64]{0:T(128)}, u32[]{:S(2)}) copy-start(f32[64]{0:T(128)} %param.22) | copy-start | bytes 772
  3.8 10.1 %copy-start.13 = (f32[64]{0:T(128)S(1)}, f32[64]{0:T(128)}, u32[]{:S(2)}) copy-start(f32[64]{0:T(128)} %param.23) | copy-start | bytes 772
  3.8 10.8 %copy-start.8 = (bf16[64,1536]{1,0:T(8,128)(2,1)S(1)}, bf16[64,1536]{1,0:T(8,128)(2,1)}, u32[]{:S(2)}) copy-start(bf16[64,1536]{1,0:T(8,128)(2,1)} %refs_20_.1) | copy-start | bytes 589828
  3.8 44.7 %all-to-all-start = ((bf16[16,128,384]{2,1,0:T(8,128)(2,1)}), bf16[16,128,384]{2,1,0:T(8,128)(2,1)S(1)}, u32[]{:S(2)}, u32[]{:S(2)}) async-start(bf16[16,128,384]{2,1,0:T(8,128)(2,1)} %shard_map.148), calls=%async_computation | async-start | bytes 3145728 | tf_op jit(solution)/shard_map/all_to_all | solution.py:660
  48.5 26.3 %copy-start = (bf16[16,128,384]{2,1,0:T(8,128)(2,1)}, bf16[16,128,384]{2,1,0:T(8,128)(2,1)S(1)}, u32[]{:S(2)}) copy-start(bf16[16,128,384]{2,1,0:T(8,128)(2,1)S(1)} %all-to-all-done.refs_1_) | copy-start | bytes 4718596
  48.6 26.2 %collective-permute-start = (bf16[16,96,384]{2,1,0:T(8,128)(2,1)S(1)}, bf16[16,96,384]{2,1,0:T(8,128)(2,1)S(1)}, u32[]{:S(2)}, u32[]{:S(2)}) collective-permute-start(bf16[16,96,384]{2,1,0:T(8,128)(2,1)S(1)} %slice.39), channel_id=1, source_target_pairs={{32,0},{240,16},{64,32},{16,48},{96,64},{48,80},{128,96},{80,112},... | collective-permute-start | bytes 3538952 | tf_op jit(solution)/shard_map/ppermute | solution.py:614
  53.0 21.8 %collective-permute-start.1 = (bf16[16,96,384]{2,1,0:T(8,128)(2,1)S(1)}, bf16[16,96,384]{2,1,0:T(8,128)(2,1)S(1)}, u32[]{:S(2)}, u32[]{:S(2)}) collective-permute-start(bf16[16,96,384]{2,1,0:T(8,128)(2,1)S(1)} %slice.39), channel_id=1, source_target_pairs={{1,0},{23,16},{33,32},{55,48},{65,64},{87,80},{97,96},{119,112},{1... | collective-permute-start | bytes 3538952 | tf_op jit(solution)/shard_map/ppermute | solution.py:614
  56.5 34.0 %collective-permute-start.2 = (bf16[16,96,384]{2,1,0:T(8,128)(2,1)S(1)}, bf16[16,96,384]{2,1,0:T(8,128)(2,1)S(1)}, u32[]{:S(2)}, u32[]{:S(2)}) collective-permute-start(bf16[16,96,384]{2,1,0:T(8,128)(2,1)S(1)} %slice.39), channel_id=1, source_target_pairs={{264,0},{24,16},{296,32},{56,48},{328,64},{88,80},{360,96},{120,11... | collective-permute-start | bytes 3538952 | tf_op jit(solution)/shard_map/ppermute | solution.py:614
  74.8 20.5 %copy-start.2 = (bf16[16,96,384]{2,1,0:T(8,128)(2,1)}, bf16[16,96,384]{2,1,0:T(8,128)(2,1)S(1)}, u32[]{:S(2)}) copy-start(bf16[16,96,384]{2,1,0:T(8,128)(2,1)S(1)} %collective-permute-done.refs_2_) | copy-start | bytes 3538948
  74.8 20.5 %copy-start.3 = (bf16[16,96,384]{2,1,0:T(8,128)(2,1)}, bf16[16,96,384]{2,1,0:T(8,128)(2,1)S(1)}, u32[]{:S(2)}) copy-start(bf16[16,96,384]{2,1,0:T(8,128)(2,1)S(1)} %collective-permute-done.1.refs_3_) | copy-start | bytes 3538948
  74.8 20.4 %collective-permute-start.3 = (bf16[16,128,384]{2,1,0:T(8,128)(2,1)S(1)}, bf16[16,128,384]{2,1,0:T(8,128)(2,1)S(1)}, u32[]{:S(2)}, u32[]{:S(2)}) collective-permute-start(bf16[16,128,384]{2,1,0:T(8,128)(2,1)S(1)} %all-to-all-done.refs_1_), channel_id=1, source_target_pairs={{0,16},{16,0},{32,48},{48,32},{64,80},{80,64},{96,112},{112,96},{1... | collective-permute-start | bytes 4718600 | tf_op jit(solution)/shard_map/ppermute | solution.py:619
  86.2 6.5 %collective-permute-start.4 = (bf16[16,96,384]{2,1,0:T(8,128)(2,1)S(1)}, bf16[16,96,384]{2,1,0:T(8,128)(2,1)S(1)}, u32[]{:S(2)}, u32[]{:S(2)}) collective-permute-start(bf16[16,96,384]{2,1,0:T(8,128)(2,1)S(1)} %collective-permute-done.refs_2_), channel_id=1, source_target_pairs={{0,16},{16,0},{32,48},{48,32},{64,80},{80,64},{96,112},{112,96},{1... | collective-permute-start | bytes 3538952 | tf_op jit(solution)/shard_map/ppermute | solution.py:619
  88.1 4.9 %collective-permute-start.5 = (bf16[16,96,384]{2,1,0:T(8,128)(2,1)S(1)}, bf16[16,96,384]{2,1,0:T(8,128)(2,1)S(1)}, u32[]{:S(2)}, u32[]{:S(2)}) collective-permute-start(bf16[16,96,384]{2,1,0:T(8,128)(2,1)S(1)} %collective-permute-done.1.refs_3_), channel_id=1, source_target_pairs={{0,16},{16,0},{32,48},{48,32},{64,80},{80,64},{96,112},{112,96},{1... | collective-permute-start | bytes 3538952 | tf_op jit(solution)/shard_map/ppermute | solution.py:619
  90.5 4.8 %copy-start.4 = (bf16[16,96,384]{2,1,0:T(8,128)(2,1)}, bf16[16,96,384]{2,1,0:T(8,128)(2,1)S(1)}, u32[]{:S(2)}) copy-start(bf16[16,96,384]{2,1,0:T(8,128)(2,1)S(1)} %collective-permute-done.2.refs_4_) | copy-start | bytes 3538948
  90.5 4.7 %collective-permute-start.6 = (bf16[16,96,384]{2,1,0:T(8,128)(2,1)S(1)}, bf16[16,96,384]{2,1,0:T(8,128)(2,1)S(1)}, u32[]{:S(2)}, u32[]{:S(2)}) collective-permute-start(bf16[16,96,384]{2,1,0:T(8,128)(2,1)S(1)} %collective-permute-done.2.refs_4_), channel_id=1, source_target_pairs={{0,16},{16,0},{32,48},{48,32},{64,80},{80,64},{96,112},{112,96},{1... | collective-permute-start | bytes 3538952 | tf_op jit(solution)/shard_map/ppermute | solution.py:619
  92.7 2.7 %copy-start.5 = (bf16[16,96,384]{2,1,0:T(8,128)(2,1)}, bf16[16,96,384]{2,1,0:T(8,128)(2,1)S(1)}, u32[]{:S(2)}) copy-start(bf16[16,96,384]{2,1,0:T(8,128)(2,1)S(1)} %collective-permute-done.4.refs_6_) | copy-start | bytes 3538948
  93.0 2.4 %copy-start.6 = (bf16[16,96,384]{2,1,0:T(8,128)(2,1)}, bf16[16,96,384]{2,1,0:T(8,128)(2,1)S(1)}, u32[]{:S(2)}) copy-start(bf16[16,96,384]{2,1,0:T(8,128)(2,1)S(1)} %collective-permute-done.5.refs_7_) | copy-start | bytes 3538948
  95.3 1.1 copy-start.7
  95.3 1.5 copy-start.1
  116.0 19.9 %all-to-all-start.2 = ((bf16[32,16,384]{2,1,0:T(8,128)(2,1)}), bf16[32,16,384]{2,1,0:T(8,128)(2,1)S(1)}, u32[]{:S(2)}, u32[]{:S(2)}) async-start(bf16[32,16,384]{2,1,0:T(8,128)(2,1)} %bitcast.21), calls=%async_computation.2 | async-start | bytes 786432 | tf_op jit(solution)/shard_map/all_to_all | solution.py:696
  148.9 5.0 %collective-permute-start.7 = (f32[16,384]{1,0:T(8,128)S(1)}, f32[16,384]{1,0:T(8,128)S(1)}, u32[]{:S(2)}, u32[]{:S(2)}) collective-permute-start(f32[16,384]{1,0:T(8,128)S(1)} %convert_reduce_fusion), channel_id=1, source_target_pairs={{0,16},{16,0},{32,48},{48,32},{64,80},{80,64},{96,112},{112,96},{1... | collective-permute-start | bytes 73736 | tf_op jit(solution)/shard_map/ppermute | solution.py:723
  154.0 0.6 copy-start.11

commit v5 on v4

--- a/solution.py
+++ b/solution.py
@@ -201,7 +201,6 @@
         adj_u,
         adj_grad,
         low_grad,
-        packed,
     ) = refs
     tokens = adjoint_ref.shape[1]
     inner = 2 * weights.shape[4]
@@ -345,7 +344,7 @@
 
     down_grad = dot_tn(blended[...], low_grad[...])
     up_grad = dot_tn(lowrank, adj_grad[...])
-    blank = jnp.zeros((8, LANES - down_grad.shape[1]), F32)
+    blank = jnp.zeros((8, HEAD_DIM), F32)
     for h in range(2):
         for f in range(shards):
             up_rows = jnp.concatenate(
@@ -356,16 +355,9 @@
                 axis=0,
             )
             row = 48 * f + 24 * h
-            down_rows = jnp.concatenate(
-                [
-                    jnp.concatenate([down_grad[row + 8 * k : row + 8 * k + 8], blank], axis=1)
-                    for k in range(3)
-                ],
-                axis=1,
-            )
-            packed[h, f] = jnp.concatenate([up_rows, down_rows], axis=0).astype(BF)
-    for copy in load([packed], [packed_out], in_sems):
-        copy.wait()
+            down_rows = [down_grad[row + 8 * k : row + 8 * k + 8] for k in range(3)] + [blank]
+            down_rows = [jnp.concatenate(down_rows[n : n + 2], axis=1) for n in (0, 2)]
+            packed_out[h, f] = jnp.concatenate([up_rows] + down_rows, axis=1).astype(BF)
     for copy in outs:
         copy.wait()
 
@@ -461,7 +453,7 @@
     per_qkv = width // shards
     inner, rank = 2 * half, HEAD_DIM
     state = state_shapes(tokens, width, inner)
-    grads = (2, shards, 16, half)
+    grads = (2, shards, 8, half + 2 * LANES)
     mods = (8, 3 * width)
     return pl.pallas_call(
         partial(first_kernel, sample_batch),
@@ -469,7 +461,7 @@
         + tuple(jax.ShapeDtypeStruct(*leaf) for leaf in state)
         + (jax.ShapeDtypeStruct(mods, F32),),
         in_specs=[SMEM] + [HBM] * (len(gathered) + len(rest)),
-        out_specs=(VMEM, HBM) + (HBM,) * (len(state) + 1),
+        out_specs=(VMEM, VMEM) + (HBM,) * (len(state) + 1),
         scratch_shapes=[
             pltpu.VMEM((2, 4, shards, per_qkv, half), BF),
             DMA((2, 4)),
@@ -480,7 +472,7 @@
         + like(rest)
         + [
             pltpu.VMEM(mods, F32),
-            pltpu.VMEM(grads, BF),
+            pltpu.VMEM((2, shards, 16, half), BF),
             pltpu.VMEM((rank, width), F32),
             pltpu.VMEM((rank, width), BF),
             pltpu.VMEM((inner, LANES), F32),
@@ -492,7 +484,6 @@
             pltpu.VMEM((2, tokens, width), F32),
             pltpu.VMEM((rows, width), BF),
             pltpu.VMEM((rows, rank), BF),
-            pltpu.VMEM(grads, BF),
         ],
         compiler_params=pltpu.CompilerParams(vmem_limit_bytes=VMEM_LIMIT),
         cost_estimate=pl.CostEstimate(
@@ -527,8 +518,8 @@
 
 
 def pieces_kernel(step_ref, *refs):
-    sources, out_ref = refs[:5], refs[5]
-    targets, extra, out, in_sems, out_sems = refs[6:11], refs[11], refs[12], refs[13], refs[14]
+    sources, out = refs[:5], refs[5]
+    targets, extra, in_sems = refs[6:11], refs[11], refs[12]
     qkv_ref, proj_ref, time_ref, up_ref, down_ref = targets
     loads = load(sources, targets, in_sems)
     core, plane, _ = placement()
@@ -551,7 +542,6 @@
         extra[8:16, k * LANES : k * LANES + down.shape[1]] = down[8 * k : 8 * k + 8]
     extra_bits = extra[...].astype(BF)
 
-    copies = []
     for r in range(shards):
         piece = (plane + r // Y_CHIPS + 2 * (r % Y_CHIPS)) & 3
 
@@ -569,10 +559,6 @@
         owned = min(r, owners - 1)
         out[r, rows:first, :] = time_ref[:, owned * half : (owned + 1) * half]
         out[r, first : first + 16, :] = extra_bits
-        copies.append(pltpu.make_async_copy(out.at[r], out_ref.at[r], out_sems.at[r]))
-        copies[-1].start()
-    for copy in copies:
-        copy.wait()
 
 
 def pieces_for(step, qkv, proj, time, up, down, shards):
@@ -583,9 +569,9 @@
         pieces_kernel,
         out_shape=jax.ShapeDtypeStruct(shape, BF),
         in_specs=[SMEM] + [HBM] * len(inputs),
-        out_specs=HBM,
+        out_specs=VMEM,
         scratch_shapes=like(inputs)
-        + [pltpu.VMEM((16, half), F32), pltpu.VMEM(shape, BF), DMA((len(inputs),)), DMA((shards,))],
+        + [pltpu.VMEM((16, half), F32), DMA((len(inputs),))],
         compiler_params=pltpu.CompilerParams(vmem_limit_bytes=VMEM_LIMIT),
     )(step, *inputs)
 
@@ -723,9 +709,11 @@
     theirs = lax.ppermute(mine, "dp", swap)
     halves = [jnp.where(core == 0, mine, theirs), jnp.where(core == 0, theirs, mine)]
     down_grad = [
-        block[8:, k * LANES : k * LANES + HEAD_DIM] for block in halves for k in range(3)
+        block[:, half + k * HEAD_DIM : half + (k + 1) * HEAD_DIM]
+        for block in halves
+        for k in range(3)
     ]
-    up_grad = [block[4 * b : 4 * b + 4] for block in halves for b in range(2)]
+    up_grad = [block[4 * b : 4 * b + 4, :half] for block in halves for b in range(2)]
     return (
         adjoint_out.T[None],
         jnp.concatenate(down_grad, axis=0),

time: 155 us -> 153 us (0.987)
  waiting for transfers between devices: 38.4 us -> 36.8 us
    all_to_all x1, waiting for transfers between devices: 2.6 us -> 0.99 us  [per_device(): lax.all_to_all(out, ('dp', 'fsdp'), 0, 0, axis_index_groups=groups, tiled...]
where the time goes in v5:
time: 153 us
  starting transfers between devices  48.6 us (32%)
  waiting for transfers between devices  36.8 us (24%)
  Pallas kernels  31.9 us (21%)
  blocking collectives  27.1 us (18%)
  local copies, waits for them, and re-layouts  3.76 us (2%)
  matrix products  1.7 us (1%)
  between operations  1.62 us (1%)
    all_to_all x1, waiting for transfers between devices, per_device(): home = lax.all_to_all(out, 'fsdp', 0, 0, tiled=True)  32.4 us
    pallas_call x1, Pallas kernels, step_pair_first(): pl.pallas_call(partial(first_kernel, sample_batch), out_shape=(jax.ShapeD...  18.6 us
    ppermute x4, starting transfers between devices, gather_neighbours(): return (own + [lax.ppermute(block, 'dp', swap) for block in own], mods)  17.8 us
    all_to_all x1, blocking collectives, per_device(): mods = lax.all_to_all(mods, 'fsdp', 0, 0, tiled=True)  14.2 us
    all_to_all x1, blocking collectives, per_device(): lax.all_to_all(jnp.broadcast_to(part[None], (chips,) + part.shape), 'dp',...  12.9 us
    ppermute x3, starting transfers between devices, gather_neighbours(): lax.ppermute(piece, ('dp', 'fsdp'), neighbours(*step))  11.2 us
    pallas_call x1, Pallas kernels, step_pair_second(): pl.pallas_call(second_kernel, out_shape=jax.ShapeDtypeStruct((chan, token...  10.8 us
    all_to_all x1, starting transfers between devices, per_device(): home = lax.all_to_all(out, 'fsdp', 0, 0, tiled=True)  8.83 us
  transfers between devices with their start and end apart: 10, of which 5 were waited for; matrix products, arithmetic and copies ran while one was open for 3% of the time, Pallas kernels for 7%

profile of v5, /device:TPU:1, one launch (start us, length us, event | category | flops | bytes accessed | tf_op | source)
XLA Modules:
  0.0 152.7 jit_solution(9540665634648627177)
XLA Ops:
  1.3 2.6 %shard_map.148 = bf16[16,128,384]{2,1,0:T(8,128)(2,1)} custom-call(s32[1]{0:T(128)S(6)} %copy.31.step_ref.refs_0_, bf16[96,2304]{1,0:T(8,128)(2,1)} %refs_0_.3, bf16[48,1536]{1,0:T(8,128)(2,1)} %refs_1_.1, bf16[16,4608]{1,0:T(8,128)(2,1)} %refs_2_.1, bf16[4,1536]{1,0:T(4,128)(2,1)} %refs_3_.1, bf16[48,64]{1,0:T(8,128)(2,1)} %refs_4_.1), custom_call_target="tpu_custom_call" | custom-call | tf_op jit(solution)/shard_map/pallas_call | solution.py:568
  3.9 0.0 copy-start.9
  3.9 0.0 copy-start.10
  3.9 0.0 copy-start.12
  3.9 0.0 copy-start.13
  3.9 0.0 copy-start.8
  3.9 8.8 %all-to-all-start = ((bf16[16,128,384]{2,1,0:T(8,128)(2,1)}), bf16[16,128,384]{2,1,0:T(8,128)(2,1)S(1)}, u32[]{:S(2)}, u32[]{:S(2)}) async-start(bf16[16,128,384]{2,1,0:T(8,128)(2,1)} %shard_map.148), calls=%async_computation | async-start | bytes 3145728 | tf_op jit(solution)/shard_map/all_to_all | solution.py:646
  12.7 0.0 copy-done.9
  12.8 0.0 copy-done.10
  12.8 0.6 broadcast_in_dim.6.refs_14_.refs_12_
  13.4 0.0 copy-done.12
  13.4 0.6 broadcast_in_dim_tile.6.refs_11_.refs_17_
  14.0 0.0 copy-done.13
  14.0 0.7 broadcast_in_dim_tile.7.refs_12_.refs_18_
  14.7 0.0 copy-done.8
  14.7 1.6 %fusion.refs_9_.refs_19_ = f32[256,1536]{1,0:T(8,128)} fusion(bf16[64,1536]{1,0:T(8,128)(2,1)S(1)} %copy-done.8, bf16[8,8,2,128]{3,2,1,0:T(2,128)(2,1)S(1)} %bitcast.24), kind=kOutput, calls=%fused_computation.1 | convolution fusion | flops 50331648 | bytes 1802240 | tf_op jit(solution)/shard_map/dot_general | solution.py:647
  16.2 32.4 %all-to-all-done.refs_1_ = bf16[16,128,384]{2,1,0:T(8,128)(2,1)S(1)} async-done(((bf16[16,128,384]{2,1,0:T(8,128)(2,1)}), bf16[16,128,384]{2,1,0:T(8,128)(2,1)S(1)}, u32[]{:S(2)}, u32[]{:S(2)}) %all-to-all-start) | async-done | bytes 1572896 | tf_op jit(solution)/shard_map/all_to_all | solution.py:646
  48.6 0.0 copy-start
  48.6 0.1 slice.39
  48.8 4.4 %collective-permute-start = (bf16[16,96,384]{2,1,0:T(8,128)(2,1)S(1)}, bf16[16,96,384]{2,1,0:T(8,128)(2,1)S(1)}, u32[]{:S(2)}, u32[]{:S(2)}) collective-permute-start(bf16[16,96,384]{2,1,0:T(8,128)(2,1)S(1)} %slice.39), channel_id=1, source_target_pairs={{32,0},{240,16},{64,32},{16,48},{96,64},{48,80},{128,96},{80,112},... | collective-permute-start | bytes 3538952 | tf_op jit(solution)/shard_map/ppermute | solution.py:600
  53.1 3.4 %collective-permute-start.1 = (bf16[16,96,384]{2,1,0:T(8,128)(2,1)S(1)}, bf16[16,96,384]{2,1,0:T(8,128)(2,1)S(1)}, u32[]{:S(2)}, u32[]{:S(2)}) collective-permute-start(bf16[16,96,384]{2,1,0:T(8,128)(2,1)S(1)} %slice.39), channel_id=1, source_target_pairs={{1,0},{23,16},{33,32},{55,48},{65,64},{87,80},{97,96},{119,112},{1... | collective-permute-start | bytes 3538952 | tf_op jit(solution)/shard_map/ppermute | solution.py:600
  56.6 3.4 %collective-permute-start.2 = (bf16[16,96,384]{2,1,0:T(8,128)(2,1)S(1)}, bf16[16,96,384]{2,1,0:T(8,128)(2,1)S(1)}, u32[]{:S(2)}, u32[]{:S(2)}) collective-permute-start(bf16[16,96,384]{2,1,0:T(8,128)(2,1)S(1)} %slice.39), channel_id=1, source_target_pairs={{264,0},{24,16},{296,32},{56,48},{328,64},{88,80},{360,96},{120,11... | collective-permute-start | bytes 3538952 | tf_op jit(solution)/shard_map/ppermute | solution.py:600
  60.0 0.3 add_reduce_fusion
  60.4 0.1 fusion.3
  60.5 0.1 fusion.5
  60.7 14.2 %all_to_all.20.refs_10_ = f32[16,2,384]{2,1,0:T(2,128)} all-to-all(f32[16,2,384]{2,1,0:T(2,128)S(1)} %copy.20), channel_id=1, replica_groups=mesh['dp'=32,'fsdp'=16] {'fsdp'}, dimensions={0} | all-to-all | bytes 98304 | tf_op jit(solution)/shard_map/all_to_all | solution.py:660
  74.9 0.0 collective-permute-done.refs_2_
  74.9 0.0 copy-start.2
  74.9 0.0 collective-permute-done.1.refs_3_
  74.9 0.0 copy-done
  74.9 0.0 copy-start.3
  75.0 11.3 %collective-permute-start.3 = (bf16[16,128,384]{2,1,0:T(8,128)(2,1)S(1)}, bf16[16,128,384]{2,1,0:T(8,128)(2,1)S(1)}, u32[]{:S(2)}, u32[]{:S(2)}) collective-permute-start(bf16[16,128,384]{2,1,0:T(8,128)(2,1)S(1)} %all-to-all-done.refs_1_), channel_id=1, source_target_pairs={{0,16},{16,0},{32,48},{48,32},{64,80},{80,64},{96,112},{112,96},{1... | collective-permute-start | bytes 4718600 | tf_op jit(solution)/shard_map/ppermute | solution.py:605
  86.3 1.9 %collective-permute-start.4 = (bf16[16,96,384]{2,1,0:T(8,128)(2,1)S(1)}, bf16[16,96,384]{2,1,0:T(8,128)(2,1)S(1)}, u32[]{:S(2)}, u32[]{:S(2)}) collective-permute-start(bf16[16,96,384]{2,1,0:T(8,128)(2,1)S(1)} %collective-permute-done.refs_2_), channel_id=1, source_target_pairs={{0,16},{16,0},{32,48},{48,32},{64,80},{80,64},{96,112},{112,96},{1... | collective-permute-start | bytes 3538952 | tf_op jit(solution)/shard_map/ppermute | solution.py:605
  88.2 2.4 %collective-permute-start.5 = (bf16[16,96,384]{2,1,0:T(8,128)(2,1)S(1)}, bf16[16,96,384]{2,1,0:T(8,128)(2,1)S(1)}, u32[]{:S(2)}, u32[]{:S(2)}) collective-permute-start(bf16[16,96,384]{2,1,0:T(8,128)(2,1)S(1)} %collective-permute-done.1.refs_3_), channel_id=1, source_target_pairs={{0,16},{16,0},{32,48},{48,32},{64,80},{80,64},{96,112},{112,96},{1... | collective-permute-start | bytes 3538952 | tf_op jit(solution)/shard_map/ppermute | solution.py:605
  90.6 0.0 collective-permute-done.2.refs_4_
  90.6 0.0 copy-start.4
  90.6 2.1 %collective-permute-start.6 = (bf16[16,96,384]{2,1,0:T(8,128)(2,1)S(1)}, bf16[16,96,384]{2,1,0:T(8,128)(2,1)S(1)}, u32[]{:S(2)}, u32[]{:S(2)}) collective-permute-start(bf16[16,96,384]{2,1,0:T(8,128)(2,1)S(1)} %collective-permute-done.2.refs_4_), channel_id=1, source_target_pairs={{0,16},{16,0},{32,48},{48,32},{64,80},{80,64},{96,112},{112,96},{1... | collective-permute-start | bytes 3538952 | tf_op jit(solution)/shard_map/ppermute | solution.py:605
  92.8 0.0 collective-permute-done.4.refs_6_
  92.8 0.0 copy-start.5
  92.8 0.3 collective-permute-done.5.refs_7_
  93.1 0.0 copy-start.6
  93.1 2.3 %collective-permute-done.6.refs_8_ = bf16[16,96,384]{2,1,0:T(8,128)(2,1)S(1)} collective-permute-done((bf16[16,96,384]{2,1,0:T(8,128)(2,1)S(1)}, bf16[16,96,384]{2,1,0:T(8,128)(2,1)S(1)}, u32[]{:S(2)}, u32[]{:S(2)}) %collective-permute-start.6) | collective-permute-done | bytes 1179680 | tf_op jit(solution)/shard_map/ppermute | solution.py:605
  95.4 0.0 copy-start.7
  95.4 0.0 collective-permute-done.3.refs_5_
  95.4 0.0 copy-done.2
  95.4 0.0 copy-start.1
  95.4 0.0 copy-done.3
  95.4 0.0 copy-done.4
  95.4 0.0 copy-done.5
  95.4 0.0 copy-done.6
  95.5 1.0 copy-done.7
  96.5 0.4 copy-done.1
  96.9 18.6 %shard_map.149 = (f32[128,64]{1,0:T(8,128)}, bf16[2,16,8,640]{3,2,1,0:T(8,128)(2,1)}, f32[128,1536]{1,0:T(8,128)}, f32[6,256,128]{2,1,0:T(8,128)}, f32[4,6,128,1...) custom-call(s32[1]{0:T(128)S(6)} %copy.31.step_ref.refs_0_, bf16[16,128,384]{2,1,0:T(8,128)(2,1)} %copy-done, ...), custom_call_target="tpu_custom_call" | custom-call | flops 5000000000 | bytes 20000000 | tf_op jit(solution)/shard_map/pallas_call | solution.py:458
  115.5 6.5 %all-to-all-start.2 = ((bf16[32,8,640]{2,1,0:T(8,128)(2,1)}), bf16[32,8,640]{2,1,0:T(8,128)(2,1)S(1)}, u32[]{:S(2)}, u32[]{:S(2)}) async-start(bf16[32,8,640]{2,1,0:T(8,128)(2,1)} %bitcast.21), calls=%async_computation.2 | async-start | bytes 655360 | tf_op jit(solution)/shard_map/all_to_all | solution.py:682
  122.0 10.8 %shard_map.150 = f32[64,128]{1,0:T(8,128)} custom-call(s32[1]{0:T(128)S(6)} %copy.31.step_ref.refs_0_, bf16[16,128,384]{2,1,0:T(8,128)(2,1)} %copy-done, bf16[16,96,384]{2,1,0:T(8,128)(2,1)} %copy-done.2, bf16[16,96,384]{2,1,0:T(8,128)(2,1)} %copy-done.3, bf16[16,96,384]{2,1,0:T(8,128)(2,1)} %copy-done.4, bf16[16,128,384]{2,1,0:T(8,128)(2,1)} %copy-done.1, ...), custom_call_target="tpu_custom_call" | custom-call | flops 3000000000 | bytes 20000000 | tf_op jit(solution)/shard_map/pallas_call | solution.py:502
  132.8 1.0 all-to-all-done.2
  133.8 0.1 reduce_sum.21
  133.9 12.9 %all_to_all.21 = bf16[16,8,640]{2,1,0:T(8,128)(2,1)S(1)} all-to-all(bf16[16,8,640]{2,1,0:T(8,128)(2,1)S(1)} %broadcast_in_dim.8), channel_id=1, replica_groups={{0,32,64,96,128,160,192,224,256,288,320,352,384,416,448,480},{16,48,80,..., dimensions={0} | all-to-all | bytes 327680 | tf_op jit(solution)/shard_map/all_to_all | solution.py:700
  146.8 4.3 %collective-permute-start.7 = (f32[8,640]{1,0:T(8,128)S(1)}, f32[8,640]{1,0:T(8,128)S(1)}, u32[]{:S(2)}, u32[]{:S(2)}) collective-permute-start(f32[8,640]{1,0:T(8,128)S(1)} %convert_reduce_fusion), channel_id=1, source_target_pairs={{0,16},{16,0},{32,48},{48,32},{64,80},{80,64},{96,112},{112,96},{1... | collective-permute-start | bytes 61448 | tf_op jit(solution)/shard_map/ppermute | solution.py:709
  151.1 0.8 collective-permute-done.7
  151.9 0.1 constant_dynamic-update-slice_fusion.4
  152.0 0.1 constant_dynamic-update-slice_fusion.1
  152.1 0.6 pad_maximum_fusion
  152.7 0.0 copy-done.11
  (16 shorter events, 0.2 us)
Async XLA Ops:
  3.9 8.9 %copy-start.9 = (bf16[1,2,128,64]{2,3,1,0:T(8,128)(2,1)S(1)}, bf16[1,2,128,64]{2,3,1,0:T(8,128)(2,1)}, u32[]{:S(2)}) copy-start(bf16[1,2,128,64]{2,3,1,0:T(8,128)(2,1)} %param.13) | copy-start | bytes 98308
  3.9 8.9 %copy-start.10 = (f32[1536]{0:T(1024)S(1)}, f32[1536]{0:T(1024)}, u32[]{:S(2)}) copy-start(f32[1536]{0:T(1024)} %param.24) | copy-start | bytes 18436
  3.9 9.5 %copy-start.12 = (f32[64]{0:T(128)S(1)}, f32[64]{0:T(128)}, u32[]{:S(2)}) copy-start(f32[64]{0:T(128)} %param.22) | copy-start | bytes 772
  3.9 10.1 %copy-start.13 = (f32[64]{0:T(128)S(1)}, f32[64]{0:T(128)}, u32[]{:S(2)}) copy-start(f32[64]{0:T(128)} %param.23) | copy-start | bytes 772
  3.9 10.8 %copy-start.8 = (bf16[64,1536]{1,0:T(8,128)(2,1)S(1)}, bf16[64,1536]{1,0:T(8,128)(2,1)}, u32[]{:S(2)}) copy-start(bf16[64,1536]{1,0:T(8,128)(2,1)} %refs_20_.1) | copy-start | bytes 589828
  3.9 44.7 %all-to-all-start = ((bf16[16,128,384]{2,1,0:T(8,128)(2,1)}), bf16[16,128,384]{2,1,0:T(8,128)(2,1)S(1)}, u32[]{:S(2)}, u32[]{:S(2)}) async-start(bf16[16,128,384]{2,1,0:T(8,128)(2,1)} %shard_map.148), calls=%async_computation | async-start | bytes 3145728 | tf_op jit(solution)/shard_map/all_to_all | solution.py:646
  48.6 26.3 %copy-start = (bf16[16,128,384]{2,1,0:T(8,128)(2,1)}, bf16[16,128,384]{2,1,0:T(8,128)(2,1)S(1)}, u32[]{:S(2)}) copy-start(bf16[16,128,384]{2,1,0:T(8,128)(2,1)S(1)} %all-to-all-done.refs_1_) | copy-start | bytes 4718596
  48.8 26.2 %collective-permute-start = (bf16[16,96,384]{2,1,0:T(8,128)(2,1)S(1)}, bf16[16,96,384]{2,1,0:T(8,128)(2,1)S(1)}, u32[]{:S(2)}, u32[]{:S(2)}) collective-permute-start(bf16[16,96,384]{2,1,0:T(8,128)(2,1)S(1)} %slice.39), channel_id=1, source_target_pairs={{32,0},{240,16},{64,32},{16,48},{96,64},{48,80},{128,96},{80,112},... | collective-permute-start | bytes 3538952 | tf_op jit(solution)/shard_map/ppermute | solution.py:600
  53.1 21.8 %collective-permute-start.1 = (bf16[16,96,384]{2,1,0:T(8,128)(2,1)S(1)}, bf16[16,96,384]{2,1,0:T(8,128)(2,1)S(1)}, u32[]{:S(2)}, u32[]{:S(2)}) collective-permute-start(bf16[16,96,384]{2,1,0:T(8,128)(2,1)S(1)} %slice.39), channel_id=1, source_target_pairs={{1,0},{23,16},{33,32},{55,48},{65,64},{87,80},{97,96},{119,112},{1... | collective-permute-start | bytes 3538952 | tf_op jit(solution)/shard_map/ppermute | solution.py:600
  56.6 34.0 %collective-permute-start.2 = (bf16[16,96,384]{2,1,0:T(8,128)(2,1)S(1)}, bf16[16,96,384]{2,1,0:T(8,128)(2,1)S(1)}, u32[]{:S(2)}, u32[]{:S(2)}) collective-permute-start(bf16[16,96,384]{2,1,0:T(8,128)(2,1)S(1)} %slice.39), channel_id=1, source_target_pairs={{264,0},{24,16},{296,32},{56,48},{328,64},{88,80},{360,96},{120,11... | collective-permute-start | bytes 3538952 | tf_op jit(solution)/shard_map/ppermute | solution.py:600
  74.9 20.5 %copy-start.2 = (bf16[16,96,384]{2,1,0:T(8,128)(2,1)}, bf16[16,96,384]{2,1,0:T(8,128)(2,1)S(1)}, u32[]{:S(2)}) copy-start(bf16[16,96,384]{2,1,0:T(8,128)(2,1)S(1)} %collective-permute-done.refs_2_) | copy-start | bytes 3538948
  74.9 20.5 %copy-start.3 = (bf16[16,96,384]{2,1,0:T(8,128)(2,1)}, bf16[16,96,384]{2,1,0:T(8,128)(2,1)S(1)}, u32[]{:S(2)}) copy-start(bf16[16,96,384]{2,1,0:T(8,128)(2,1)S(1)} %collective-permute-done.1.refs_3_) | copy-start | bytes 3538948
  75.0 20.4 %collective-permute-start.3 = (bf16[16,128,384]{2,1,0:T(8,128)(2,1)S(1)}, bf16[16,128,384]{2,1,0:T(8,128)(2,1)S(1)}, u32[]{:S(2)}, u32[]{:S(2)}) collective-permute-start(bf16[16,128,384]{2,1,0:T(8,128)(2,1)S(1)} %all-to-all-done.refs_1_), channel_id=1, source_target_pairs={{0,16},{16,0},{32,48},{48,32},{64,80},{80,64},{96,112},{112,96},{1... | collective-permute-start | bytes 4718600 | tf_op jit(solution)/shard_map/ppermute | solution.py:605
  86.3 6.5 %collective-permute-start.4 = (bf16[16,96,384]{2,1,0:T(8,128)(2,1)S(1)}, bf16[16,96,384]{2,1,0:T(8,128)(2,1)S(1)}, u32[]{:S(2)}, u32[]{:S(2)}) collective-permute-start(bf16[16,96,384]{2,1,0:T(8,128)(2,1)S(1)} %collective-permute-done.refs_2_), channel_id=1, source_target_pairs={{0,16},{16,0},{32,48},{48,32},{64,80},{80,64},{96,112},{112,96},{1... | collective-permute-start | bytes 3538952 | tf_op jit(solution)/shard_map/ppermute | solution.py:605
  88.2 4.9 %collective-permute-start.5 = (bf16[16,96,384]{2,1,0:T(8,128)(2,1)S(1)}, bf16[16,96,384]{2,1,0:T(8,128)(2,1)S(1)}, u32[]{:S(2)}, u32[]{:S(2)}) collective-permute-start(bf16[16,96,384]{2,1,0:T(8,128)(2,1)S(1)} %collective-permute-done.1.refs_3_), channel_id=1, source_target_pairs={{0,16},{16,0},{32,48},{48,32},{64,80},{80,64},{96,112},{112,96},{1... | collective-permute-start | bytes 3538952 | tf_op jit(solution)/shard_map/ppermute | solution.py:605
  90.6 4.8 %copy-start.4 = (bf16[16,96,384]{2,1,0:T(8,128)(2,1)}, bf16[16,96,384]{2,1,0:T(8,128)(2,1)S(1)}, u32[]{:S(2)}) copy-start(bf16[16,96,384]{2,1,0:T(8,128)(2,1)S(1)} %collective-permute-done.2.refs_4_) | copy-start | bytes 3538948
  90.6 4.7 %collective-permute-start.6 = (bf16[16,96,384]{2,1,0:T(8,128)(2,1)S(1)}, bf16[16,96,384]{2,1,0:T(8,128)(2,1)S(1)}, u32[]{:S(2)}, u32[]{:S(2)}) collective-permute-start(bf16[16,96,384]{2,1,0:T(8,128)(2,1)S(1)} %collective-permute-done.2.refs_4_), channel_id=1, source_target_pairs={{0,16},{16,0},{32,48},{48,32},{64,80},{80,64},{96,112},{112,96},{1... | collective-permute-start | bytes 3538952 | tf_op jit(solution)/shard_map/ppermute | solution.py:605
  92.8 2.7 %copy-start.5 = (bf16[16,96,384]{2,1,0:T(8,128)(2,1)}, bf16[16,96,384]{2,1,0:T(8,128)(2,1)S(1)}, u32[]{:S(2)}) copy-start(bf16[16,96,384]{2,1,0:T(8,128)(2,1)S(1)} %collective-permute-done.4.refs_6_) | copy-start | bytes 3538948
  93.1 2.4 %copy-start.6 = (bf16[16,96,384]{2,1,0:T(8,128)(2,1)}, bf16[16,96,384]{2,1,0:T(8,128)(2,1)S(1)}, u32[]{:S(2)}) copy-start(bf16[16,96,384]{2,1,0:T(8,128)(2,1)S(1)} %collective-permute-done.5.refs_7_) | copy-start | bytes 3538948
  95.4 1.1 copy-start.7
  95.4 1.5 copy-start.1
  115.5 18.3 %all-to-all-start.2 = ((bf16[32,8,640]{2,1,0:T(8,128)(2,1)}), bf16[32,8,640]{2,1,0:T(8,128)(2,1)S(1)}, u32[]{:S(2)}, u32[]{:S(2)}) async-start(bf16[32,8,640]{2,1,0:T(8,128)(2,1)} %bitcast.21), calls=%async_computation.2 | async-start | bytes 655360 | tf_op jit(solution)/shard_map/all_to_all | solution.py:682
  146.8 5.1 %collective-permute-start.7 = (f32[8,640]{1,0:T(8,128)S(1)}, f32[8,640]{1,0:T(8,128)S(1)}, u32[]{:S(2)}, u32[]{:S(2)}) collective-permute-start(f32[8,640]{1,0:T(8,128)S(1)} %convert_reduce_fusion), channel_id=1, source_target_pairs={{0,16},{16,0},{32,48},{48,32},{64,80},{80,64},{96,112},{112,96},{1... | collective-permute-start | bytes 61448 | tf_op jit(solution)/shard_map/ppermute | solution.py:709
  152.1 0.6 copy-start.11

commit v6 on v5

--- a/solution.py
+++ b/solution.py
@@ -598,7 +598,7 @@
     piece = home[:, :rows]
     parts = [
         lax.ppermute(piece, ("dp", "fsdp"), neighbours(*step))
-        for step in ((0, 0, 1), (0, 1, 0), (-1, 0, 0))
+        for step in ((1, 0, 0), (0, 1, 0), (0, 0, -1))
     ]
     home, *parts[:2], mods = lax.optimization_barrier((home, *parts[:2], mods))
     own = [home] + parts

time: 153 us -> 151 us (0.987)
  starting transfers between devices: 48.6 us -> 42.5 us
  blocking collectives: 27.1 us -> 31.2 us
    ppermute x4, starting transfers between devices: 17.8 us -> 8.83 us  [gather_neighbours(): return (own + [lax.ppermute(block, 'dp', swap) for block in own], mods)]
    ppermute x3, starting transfers between devices: 11.2 us -> 16.6 us  [gather_neighbours(): lax.ppermute(piece, ('dp', 'fsdp'), neighbours(*step))]
    all_to_all x1, blocking collectives: 12.9 us -> 17.2 us  [per_device(): lax.all_to_all(jnp.broadcast_to(part[None], (chips,) + part.shape), 'dp',...]
    all_to_all x1, starting transfers between devices: 6.48 us -> 3.89 us  [per_device(): lax.all_to_all(out, ('dp', 'fsdp'), 0, 0, axis_index_groups=groups, tiled...]
where the time goes in v6:
time: 151 us; the launch traced here: 150 us
  starting transfers between devices  42.5 us (28%)
  waiting for transfers between devices  36.5 us (24%)
  Pallas kernels  31.9 us (21%)
  blocking collectives  31.2 us (21%)
  local copies, waits for them, and re-layouts  3.77 us (2%)
  matrix products  1.7 us (1%)
  between operations  1.61 us (1%)
    all_to_all x1, waiting for transfers between devices, per_device(): home = lax.all_to_all(out, 'fsdp', 0, 0, tiled=True)  32.4 us
    pallas_call x1, Pallas kernels, step_pair_first(): pl.pallas_call(partial(first_kernel, sample_batch), out_shape=(jax.ShapeD...  18.6 us
    all_to_all x1, blocking collectives, per_device(): lax.all_to_all(jnp.broadcast_to(part[None], (chips,) + part.shape), 'dp',...  17.2 us
    ppermute x3, starting transfers between devices, gather_neighbours(): lax.ppermute(piece, ('dp', 'fsdp'), neighbours(*step))  16.6 us
    all_to_all x1, blocking collectives, per_device(): mods = lax.all_to_all(mods, 'fsdp', 0, 0, tiled=True)  14 us
    pallas_call x1, Pallas kernels, step_pair_second(): pl.pallas_call(second_kernel, out_shape=jax.ShapeDtypeStruct((chan, token...  10.8 us
    ppermute x4, starting transfers between devices, gather_neighbours(): return (own + [lax.ppermute(block, 'dp', swap) for block in own], mods)  8.83 us
    all_to_all x1, starting transfers between devices, per_device(): home = lax.all_to_all(out, 'fsdp', 0, 0, tiled=True)  8.83 us
  transfers between devices with their start and end apart: 10, of which 5 were waited for; matrix products, arithmetic and copies ran while one was open for 3% of the time, Pallas kernels for 7%

profile of v6, /device:TPU:1, one launch (start us, length us, event | category | flops | bytes accessed | tf_op | source)
XLA Modules:
  0.0 150.3 jit_solution(17195336329682789216)
XLA Ops:
  1.3 2.6 %shard_map.148 = bf16[16,128,384]{2,1,0:T(8,128)(2,1)} custom-call(s32[1]{0:T(128)S(6)} %copy.31.step_ref.refs_0_, bf16[96,2304]{1,0:T(8,128)(2,1)} %refs_0_.3, bf16[48,1536]{1,0:T(8,128)(2,1)} %refs_1_.1, bf16[16,4608]{1,0:T(8,128)(2,1)} %refs_2_.1, bf16[4,1536]{1,0:T(4,128)(2,1)} %refs_3_.1, bf16[48,64]{1,0:T(8,128)(2,1)} %refs_4_.1), custom_call_target="tpu_custom_call" | custom-call | tf_op jit(solution)/shard_map/pallas_call | solution.py:568
  3.9 0.0 copy-start.9
  3.9 0.0 copy-start.10
  3.9 0.0 copy-start.12
  3.9 0.0 copy-start.13
  3.9 0.0 copy-start.8
  3.9 8.8 %all-to-all-start = ((bf16[16,128,384]{2,1,0:T(8,128)(2,1)}), bf16[16,128,384]{2,1,0:T(8,128)(2,1)S(1)}, u32[]{:S(2)}, u32[]{:S(2)}) async-start(bf16[16,128,384]{2,1,0:T(8,128)(2,1)} %shard_map.148), calls=%async_computation | async-start | bytes 3145728 | tf_op jit(solution)/shard_map/all_to_all | solution.py:646
  12.7 0.0 copy-done.9
  12.8 0.0 copy-done.10
  12.8 0.6 broadcast_in_dim.6.refs_14_.refs_12_
  13.4 0.0 copy-done.12
  13.4 0.6 broadcast_in_dim_tile.6.refs_11_.refs_17_
  14.0 0.0 copy-done.13
  14.0 0.7 broadcast_in_dim_tile.7.refs_12_.refs_18_
  14.7 0.0 copy-done.8
  14.7 1.6 %fusion.refs_9_.refs_19_ = f32[256,1536]{1,0:T(8,128)} fusion(bf16[64,1536]{1,0:T(8,128)(2,1)S(1)} %copy-done.8, bf16[8,8,2,128]{3,2,1,0:T(2,128)(2,1)S(1)} %bitcast.24), kind=kOutput, calls=%fused_computation.1 | convolution fusion | flops 50331648 | bytes 1802240 | tf_op jit(solution)/shard_map/dot_general | solution.py:647
  16.2 32.4 %all-to-all-done.refs_1_ = bf16[16,128,384]{2,1,0:T(8,128)(2,1)S(1)} async-done(((bf16[16,128,384]{2,1,0:T(8,128)(2,1)}), bf16[16,128,384]{2,1,0:T(8,128)(2,1)S(1)}, u32[]{:S(2)}, u32[]{:S(2)}) %all-to-all-start) | async-done | bytes 1572896 | tf_op jit(solution)/shard_map/all_to_all | solution.py:646
  48.6 0.1 slice.39
  48.8 2.6 %collective-permute-start = (bf16[16,96,384]{2,1,0:T(8,128)(2,1)S(1)}, bf16[16,96,384]{2,1,0:T(8,128)(2,1)S(1)}, u32[]{:S(2)}, u32[]{:S(2)}) collective-permute-start(bf16[16,96,384]{2,1,0:T(8,128)(2,1)S(1)} %slice.39), channel_id=1, source_target_pairs={{8,0},{280,16},{40,32},{312,48},{72,64},{344,80},{104,96},{376,112... | collective-permute-start | bytes 3538952 | tf_op jit(solution)/shard_map/ppermute | solution.py:600
  51.4 2.7 %collective-permute-start.1 = (bf16[16,96,384]{2,1,0:T(8,128)(2,1)S(1)}, bf16[16,96,384]{2,1,0:T(8,128)(2,1)S(1)}, u32[]{:S(2)}, u32[]{:S(2)}) collective-permute-start(bf16[16,96,384]{2,1,0:T(8,128)(2,1)S(1)} %slice.39), channel_id=1, source_target_pairs={{1,0},{23,16},{33,32},{55,48},{65,64},{87,80},{97,96},{119,112},{1... | collective-permute-start | bytes 3538952 | tf_op jit(solution)/shard_map/ppermute | solution.py:600
  54.2 11.2 %collective-permute-start.2 = (bf16[16,96,384]{2,1,0:T(8,128)(2,1)S(1)}, bf16[16,96,384]{2,1,0:T(8,128)(2,1)S(1)}, u32[]{:S(2)}, u32[]{:S(2)}) collective-permute-start(bf16[16,96,384]{2,1,0:T(8,128)(2,1)S(1)} %slice.39), channel_id=1, source_target_pairs={{224,0},{48,16},{0,32},{80,48},{32,64},{112,80},{64,96},{144,112},... | collective-permute-start | bytes 3538952 | tf_op jit(solution)/shard_map/ppermute | solution.py:600
  65.4 0.3 add_reduce_fusion
  65.8 0.1 fusion.3
  65.9 0.1 fusion.5
  66.1 14.0 %all_to_all.20.refs_10_ = f32[16,2,384]{2,1,0:T(2,128)} all-to-all(f32[16,2,384]{2,1,0:T(2,128)S(1)} %copy.20), channel_id=1, replica_groups=mesh['dp'=32,'fsdp'=16] {'fsdp'}, dimensions={0} | all-to-all | bytes 98304 | tf_op jit(solution)/shard_map/all_to_all | solution.py:660
  80.1 0.0 collective-permute-done.refs_2_
  80.1 0.0 copy-start.2
  80.1 0.0 collective-permute-done.1.refs_3_
  80.1 0.0 copy-done
  80.1 0.0 copy-start.3
  80.1 1.9 %collective-permute-start.3 = (bf16[16,128,384]{2,1,0:T(8,128)(2,1)S(1)}, bf16[16,128,384]{2,1,0:T(8,128)(2,1)S(1)}, u32[]{:S(2)}, u32[]{:S(2)}) collective-permute-start(bf16[16,128,384]{2,1,0:T(8,128)(2,1)S(1)} %all-to-all-done.refs_1_), channel_id=1, source_target_pairs={{0,16},{16,0},{32,48},{48,32},{64,80},{80,64},{96,112},{112,96},{1... | collective-permute-start | bytes 4718600 | tf_op jit(solution)/shard_map/ppermute | solution.py:605
  82.0 2.4 %collective-permute-start.4 = (bf16[16,96,384]{2,1,0:T(8,128)(2,1)S(1)}, bf16[16,96,384]{2,1,0:T(8,128)(2,1)S(1)}, u32[]{:S(2)}, u32[]{:S(2)}) collective-permute-start(bf16[16,96,384]{2,1,0:T(8,128)(2,1)S(1)} %collective-permute-done.refs_2_), channel_id=1, source_target_pairs={{0,16},{16,0},{32,48},{48,32},{64,80},{80,64},{96,112},{112,96},{1... | collective-permute-start | bytes 3538952 | tf_op jit(solution)/shard_map/ppermute | solution.py:605
  84.5 1.9 %collective-permute-start.5 = (bf16[16,96,384]{2,1,0:T(8,128)(2,1)S(1)}, bf16[16,96,384]{2,1,0:T(8,128)(2,1)S(1)}, u32[]{:S(2)}, u32[]{:S(2)}) collective-permute-start(bf16[16,96,384]{2,1,0:T(8,128)(2,1)S(1)} %collective-permute-done.1.refs_3_), channel_id=1, source_target_pairs={{0,16},{16,0},{32,48},{48,32},{64,80},{80,64},{96,112},{112,96},{1... | collective-permute-start | bytes 3538952 | tf_op jit(solution)/shard_map/ppermute | solution.py:605
  86.4 0.0 collective-permute-done.2.refs_4_
  86.4 0.0 copy-start.4
  86.4 2.6 %collective-permute-start.6 = (bf16[16,96,384]{2,1,0:T(8,128)(2,1)S(1)}, bf16[16,96,384]{2,1,0:T(8,128)(2,1)S(1)}, u32[]{:S(2)}, u32[]{:S(2)}) collective-permute-start(bf16[16,96,384]{2,1,0:T(8,128)(2,1)S(1)} %collective-permute-done.2.refs_4_), channel_id=1, source_target_pairs={{0,16},{16,0},{32,48},{48,32},{64,80},{80,64},{96,112},{112,96},{1... | collective-permute-start | bytes 3538952 | tf_op jit(solution)/shard_map/ppermute | solution.py:605
  89.0 0.0 collective-permute-done.4.refs_6_
  89.0 0.0 copy-start.5
  89.0 0.2 collective-permute-done.5.refs_7_
  89.2 0.0 copy-start.6
  89.2 2.1 %collective-permute-done.6.refs_8_ = bf16[16,96,384]{2,1,0:T(8,128)(2,1)S(1)} collective-permute-done((bf16[16,96,384]{2,1,0:T(8,128)(2,1)S(1)}, bf16[16,96,384]{2,1,0:T(8,128)(2,1)S(1)}, u32[]{:S(2)}, u32[]{:S(2)}) %collective-permute-start.6) | collective-permute-done | bytes 1179680 | tf_op jit(solution)/shard_map/ppermute | solution.py:605
  91.3 0.0 copy-start.7
  91.3 0.0 collective-permute-done.3.refs_5_
  91.3 0.0 copy-done.2
  91.3 0.0 copy-start.1
  91.3 0.0 copy-done.3
  91.3 0.0 copy-done.4
  91.3 0.0 copy-done.5
  91.3 0.0 copy-done.6
  91.3 1.0 copy-done.7
  92.4 0.4 copy-done.1
  92.8 18.6 %shard_map.149 = (f32[128,64]{1,0:T(8,128)}, bf16[2,16,8,640]{3,2,1,0:T(8,128)(2,1)}, f32[128,1536]{1,0:T(8,128)}, f32[6,256,128]{2,1,0:T(8,128)}, f32[4,6,128,1...) custom-call(s32[1]{0:T(128)S(6)} %copy.31.step_ref.refs_0_, bf16[16,128,384]{2,1,0:T(8,128)(2,1)} %copy-done, ...), custom_call_target="tpu_custom_call" | custom-call | flops 5000000000 | bytes 20000000 | tf_op jit(solution)/shard_map/pallas_call | solution.py:458
  111.4 3.9 %all-to-all-start.2 = ((bf16[32,8,640]{2,1,0:T(8,128)(2,1)}), bf16[32,8,640]{2,1,0:T(8,128)(2,1)S(1)}, u32[]{:S(2)}, u32[]{:S(2)}) async-start(bf16[32,8,640]{2,1,0:T(8,128)(2,1)} %bitcast.21), calls=%async_computation.2 | async-start | bytes 655360 | tf_op jit(solution)/shard_map/all_to_all | solution.py:682
  115.3 10.8 %shard_map.150 = f32[64,128]{1,0:T(8,128)} custom-call(s32[1]{0:T(128)S(6)} %copy.31.step_ref.refs_0_, bf16[16,128,384]{2,1,0:T(8,128)(2,1)} %copy-done, bf16[16,96,384]{2,1,0:T(8,128)(2,1)} %copy-done.2, bf16[16,96,384]{2,1,0:T(8,128)(2,1)} %copy-done.3, bf16[16,96,384]{2,1,0:T(8,128)(2,1)} %copy-done.4, bf16[16,128,384]{2,1,0:T(8,128)(2,1)} %copy-done.1, ...), custom_call_target="tpu_custom_call" | custom-call | flops 3000000000 | bytes 20000000 | tf_op jit(solution)/shard_map/pallas_call | solution.py:502
  126.1 1.0 all-to-all-done.2
  127.1 0.1 reduce_sum.21
  127.2 17.2 %all_to_all.21 = bf16[16,8,640]{2,1,0:T(8,128)(2,1)S(1)} all-to-all(bf16[16,8,640]{2,1,0:T(8,128)(2,1)S(1)} %broadcast_in_dim.8), channel_id=1, replica_groups={{0,32,64,96,128,160,192,224,256,288,320,352,384,416,448,480},{16,48,80,..., dimensions={0} | all-to-all | bytes 327680 | tf_op jit(solution)/shard_map/all_to_all | solution.py:700
  144.4 4.3 %collective-permute-start.7 = (f32[8,640]{1,0:T(8,128)S(1)}, f32[8,640]{1,0:T(8,128)S(1)}, u32[]{:S(2)}, u32[]{:S(2)}) collective-permute-start(f32[8,640]{1,0:T(8,128)S(1)} %convert_reduce_fusion), channel_id=1, source_target_pairs={{0,16},{16,0},{32,48},{48,32},{64,80},{80,64},{96,112},{112,96},{1... | collective-permute-start | bytes 61448 | tf_op jit(solution)/shard_map/ppermute | solution.py:709
  148.7 0.8 collective-permute-done.7
  149.6 0.1 constant_dynamic-update-slice_fusion.4
  149.7 0.1 constant_dynamic-update-slice_fusion.1
  149.7 0.0 copy-start.11
  149.7 0.6 pad_maximum_fusion
  150.3 0.0 copy-done.11
  (16 shorter events, 0.2 us)
Async XLA Ops:
  3.9 8.9 %copy-start.9 = (bf16[1,2,128,64]{2,3,1,0:T(8,128)(2,1)S(1)}, bf16[1,2,128,64]{2,3,1,0:T(8,128)(2,1)}, u32[]{:S(2)}) copy-start(bf16[1,2,128,64]{2,3,1,0:T(8,128)(2,1)} %param.13) | copy-start | bytes 98308
  3.9 8.9 %copy-start.10 = (f32[1536]{0:T(1024)S(1)}, f32[1536]{0:T(1024)}, u32[]{:S(2)}) copy-start(f32[1536]{0:T(1024)} %param.24) | copy-start | bytes 18436
  3.9 9.5 %copy-start.12 = (f32[64]{0:T(128)S(1)}, f32[64]{0:T(128)}, u32[]{:S(2)}) copy-start(f32[64]{0:T(128)} %param.22) | copy-start | bytes 772
  3.9 10.1 %copy-start.13 = (f32[64]{0:T(128)S(1)}, f32[64]{0:T(128)}, u32[]{:S(2)}) copy-start(f32[64]{0:T(128)} %param.23) | copy-start | bytes 772
  3.9 10.8 %copy-start.8 = (bf16[64,1536]{1,0:T(8,128)(2,1)S(1)}, bf16[64,1536]{1,0:T(8,128)(2,1)}, u32[]{:S(2)}) copy-start(bf16[64,1536]{1,0:T(8,128)(2,1)} %refs_20_.1) | copy-start | bytes 589828
  3.9 44.7 %all-to-all-start = ((bf16[16,128,384]{2,1,0:T(8,128)(2,1)}), bf16[16,128,384]{2,1,0:T(8,128)(2,1)S(1)}, u32[]{:S(2)}, u32[]{:S(2)}) async-start(bf16[16,128,384]{2,1,0:T(8,128)(2,1)} %shard_map.148), calls=%async_computation | async-start | bytes 3145728 | tf_op jit(solution)/shard_map/all_to_all | solution.py:646
  48.6 31.5 %copy-start = (bf16[16,128,384]{2,1,0:T(8,128)(2,1)}, bf16[16,128,384]{2,1,0:T(8,128)(2,1)S(1)}, u32[]{:S(2)}) copy-start(bf16[16,128,384]{2,1,0:T(8,128)(2,1)S(1)} %all-to-all-done.refs_1_) | copy-start | bytes 4718596
  48.8 31.3 %collective-permute-start = (bf16[16,96,384]{2,1,0:T(8,128)(2,1)S(1)}, bf16[16,96,384]{2,1,0:T(8,128)(2,1)S(1)}, u32[]{:S(2)}, u32[]{:S(2)}) collective-permute-start(bf16[16,96,384]{2,1,0:T(8,128)(2,1)S(1)} %slice.39), channel_id=1, source_target_pairs={{8,0},{280,16},{40,32},{312,48},{72,64},{344,80},{104,96},{376,112... | collective-permute-start | bytes 3538952 | tf_op jit(solution)/shard_map/ppermute | solution.py:600
  51.4 28.7 %collective-permute-start.1 = (bf16[16,96,384]{2,1,0:T(8,128)(2,1)S(1)}, bf16[16,96,384]{2,1,0:T(8,128)(2,1)S(1)}, u32[]{:S(2)}, u32[]{:S(2)}) collective-permute-start(bf16[16,96,384]{2,1,0:T(8,128)(2,1)S(1)} %slice.39), channel_id=1, source_target_pairs={{1,0},{23,16},{33,32},{55,48},{65,64},{87,80},{97,96},{119,112},{1... | collective-permute-start | bytes 3538952 | tf_op jit(solution)/shard_map/ppermute | solution.py:600
  54.2 32.2 %collective-permute-start.2 = (bf16[16,96,384]{2,1,0:T(8,128)(2,1)S(1)}, bf16[16,96,384]{2,1,0:T(8,128)(2,1)S(1)}, u32[]{:S(2)}, u32[]{:S(2)}) collective-permute-start(bf16[16,96,384]{2,1,0:T(8,128)(2,1)S(1)} %slice.39), channel_id=1, source_target_pairs={{224,0},{48,16},{0,32},{80,48},{32,64},{112,80},{64,96},{144,112},... | collective-permute-start | bytes 3538952 | tf_op jit(solution)/shard_map/ppermute | solution.py:600
  80.1 11.2 %copy-start.2 = (bf16[16,96,384]{2,1,0:T(8,128)(2,1)}, bf16[16,96,384]{2,1,0:T(8,128)(2,1)S(1)}, u32[]{:S(2)}) copy-start(bf16[16,96,384]{2,1,0:T(8,128)(2,1)S(1)} %collective-permute-done.refs_2_) | copy-start | bytes 3538948
  80.1 11.2 %copy-start.3 = (bf16[16,96,384]{2,1,0:T(8,128)(2,1)}, bf16[16,96,384]{2,1,0:T(8,128)(2,1)S(1)}, u32[]{:S(2)}) copy-start(bf16[16,96,384]{2,1,0:T(8,128)(2,1)S(1)} %collective-permute-done.1.refs_3_) | copy-start | bytes 3538948
  80.1 11.2 %collective-permute-start.3 = (bf16[16,128,384]{2,1,0:T(8,128)(2,1)S(1)}, bf16[16,128,384]{2,1,0:T(8,128)(2,1)S(1)}, u32[]{:S(2)}, u32[]{:S(2)}) collective-permute-start(bf16[16,128,384]{2,1,0:T(8,128)(2,1)S(1)} %all-to-all-done.refs_1_), channel_id=1, source_target_pairs={{0,16},{16,0},{32,48},{48,32},{64,80},{80,64},{96,112},{112,96},{1... | collective-permute-start | bytes 4718600 | tf_op jit(solution)/shard_map/ppermute | solution.py:605
  82.0 7.0 %collective-permute-start.4 = (bf16[16,96,384]{2,1,0:T(8,128)(2,1)S(1)}, bf16[16,96,384]{2,1,0:T(8,128)(2,1)S(1)}, u32[]{:S(2)}, u32[]{:S(2)}) collective-permute-start(bf16[16,96,384]{2,1,0:T(8,128)(2,1)S(1)} %collective-permute-done.refs_2_), channel_id=1, source_target_pairs={{0,16},{16,0},{32,48},{48,32},{64,80},{80,64},{96,112},{112,96},{1... | collective-permute-start | bytes 3538952 | tf_op jit(solution)/shard_map/ppermute | solution.py:605
  84.5 4.7 %collective-permute-start.5 = (bf16[16,96,384]{2,1,0:T(8,128)(2,1)S(1)}, bf16[16,96,384]{2,1,0:T(8,128)(2,1)S(1)}, u32[]{:S(2)}, u32[]{:S(2)}) collective-permute-start(bf16[16,96,384]{2,1,0:T(8,128)(2,1)S(1)} %collective-permute-done.1.refs_3_), channel_id=1, source_target_pairs={{0,16},{16,0},{32,48},{48,32},{64,80},{80,64},{96,112},{112,96},{1... | collective-permute-start | bytes 3538952 | tf_op jit(solution)/shard_map/ppermute | solution.py:605
  86.4 4.9 %copy-start.4 = (bf16[16,96,384]{2,1,0:T(8,128)(2,1)}, bf16[16,96,384]{2,1,0:T(8,128)(2,1)S(1)}, u32[]{:S(2)}) copy-start(bf16[16,96,384]{2,1,0:T(8,128)(2,1)S(1)} %collective-permute-done.2.refs_4_) | copy-start | bytes 3538948
  86.4 4.9 %collective-permute-start.6 = (bf16[16,96,384]{2,1,0:T(8,128)(2,1)S(1)}, bf16[16,96,384]{2,1,0:T(8,128)(2,1)S(1)}, u32[]{:S(2)}, u32[]{:S(2)}) collective-permute-start(bf16[16,96,384]{2,1,0:T(8,128)(2,1)S(1)} %collective-permute-done.2.refs_4_), channel_id=1, source_target_pairs={{0,16},{16,0},{32,48},{48,32},{64,80},{80,64},{96,112},{112,96},{1... | collective-permute-start | bytes 3538952 | tf_op jit(solution)/shard_map/ppermute | solution.py:605
  89.0 2.3 %copy-start.5 = (bf16[16,96,384]{2,1,0:T(8,128)(2,1)}, bf16[16,96,384]{2,1,0:T(8,128)(2,1)S(1)}, u32[]{:S(2)}) copy-start(bf16[16,96,384]{2,1,0:T(8,128)(2,1)S(1)} %collective-permute-done.4.refs_6_) | copy-start | bytes 3538948
  89.2 2.1 %copy-start.6 = (bf16[16,96,384]{2,1,0:T(8,128)(2,1)}, bf16[16,96,384]{2,1,0:T(8,128)(2,1)S(1)}, u32[]{:S(2)}) copy-start(bf16[16,96,384]{2,1,0:T(8,128)(2,1)S(1)} %collective-permute-done.5.refs_7_) | copy-start | bytes 3538948
  91.3 1.1 copy-start.7
  91.3 1.5 %copy-start.1 = (bf16[16,128,384]{2,1,0:T(8,128)(2,1)}, bf16[16,128,384]{2,1,0:T(8,128)(2,1)S(1)}, u32[]{:S(2)}) copy-start(bf16[16,128,384]{2,1,0:T(8,128)(2,1)S(1)} %collective-permute-done.3.refs_5_) | copy-start | bytes 4718596
  111.4 15.7 %all-to-all-start.2 = ((bf16[32,8,640]{2,1,0:T(8,128)(2,1)}), bf16[32,8,640]{2,1,0:T(8,128)(2,1)S(1)}, u32[]{:S(2)}, u32[]{:S(2)}) async-start(bf16[32,8,640]{2,1,0:T(8,128)(2,1)} %bitcast.21), calls=%async_computation.2 | async-start | bytes 655360 | tf_op jit(solution)/shard_map/all_to_all | solution.py:682
  144.4 5.1 %collective-permute-start.7 = (f32[8,640]{1,0:T(8,128)S(1)}, f32[8,640]{1,0:T(8,128)S(1)}, u32[]{:S(2)}, u32[]{:S(2)}) collective-permute-start(f32[8,640]{1,0:T(8,128)S(1)} %convert_reduce_fusion), channel_id=1, source_target_pairs={{0,16},{16,0},{32,48},{48,32},{64,80},{80,64},{96,112},{112,96},{1... | collective-permute-start | bytes 61448 | tf_op jit(solution)/shard_map/ppermute | solution.py:709
  149.7 0.6 copy-start.11

commit v7 on v6

--- a/solution.py
+++ b/solution.py
@@ -307,14 +307,22 @@
     for copy in outs:
         copy.start()
 
-    def velocity(u):
-        return dot_nt((u * row_norm(u) * fgain).astype(BF), wout_ref[...])
+    normed = [
+        (u * row_norm(u) * fgain).astype(BF)
+        for j in range(2)
+        for u in (adj_u[j], base_u[j])
+    ]
+    velocity = dot_nt(jnp.concatenate(normed, axis=0), wout_ref[...])
+    gaps = [
+        velocity[2 * j * tokens : (2 * j + 1) * tokens]
+        - velocity[(2 * j + 1) * tokens : (2 * j + 2) * tokens]
+        for j in range(2)
+    ]
 
     def regression(j, current):
         time = turn_time(step_ref, j)
         sigma = jnp.sqrt(2.0 * (1.0 - time) / time)
-        gap = velocity(adj_u[j]) - velocity(base_u[j])
-        residual = 2.0 / sigma * gap + sigma * current
+        residual = 2.0 / sigma * gaps[j] + sigma * current
         cotangent = 4.0 * residual / (sigma * sample_batch)
         grad = (tail_back(adj_u[j], cotangent, wout_ref, fgain) * gates[j]).astype(BF)
         adj_grad[turns[j], :] = grad

time: 151 us -> 152 us (level)
  no operation moved by 1% of the time
where the time goes in v7:
time: 152 us
  starting transfers between devices  42.5 us (28%)
  waiting for transfers between devices  36.5 us (24%)
  Pallas kernels  33.3 us (22%)
  blocking collectives  31.2 us (21%)
  local copies, waits for them, and re-layouts  3.77 us (2%)
  matrix products  1.7 us (1%)
  between operations  1.61 us (1%)
    all_to_all x1, waiting for transfers between devices, per_device(): home = lax.all_to_all(out, 'fsdp', 0, 0, tiled=True)  32.4 us
    pallas_call x1, Pallas kernels, step_pair_first(): pl.pallas_call(partial(first_kernel, sample_batch), out_shape=(jax.ShapeD...  19.9 us
    all_to_all x1, blocking collectives, per_device(): lax.all_to_all(jnp.broadcast_to(part[None], (chips,) + part.shape), 'dp',...  17.2 us
    ppermute x3, starting transfers between devices, gather_neighbours(): lax.ppermute(piece, ('dp', 'fsdp'), neighbours(*step))  16.6 us
    all_to_all x1, blocking collectives, per_device(): mods = lax.all_to_all(mods, 'fsdp', 0, 0, tiled=True)  14 us
    pallas_call x1, Pallas kernels, step_pair_second(): pl.pallas_call(second_kernel, out_shape=jax.ShapeDtypeStruct((chan, token...  10.8 us
    ppermute x4, starting transfers between devices, gather_neighbours(): return (own + [lax.ppermute(block, 'dp', swap) for block in own], mods)  8.83 us
    all_to_all x1, starting transfers between devices, per_device(): home = lax.all_to_all(out, 'fsdp', 0, 0, tiled=True)  8.83 us
  transfers between devices with their start and end apart: 10, of which 5 were waited for; matrix products, arithmetic and copies ran while one was open for 3% of the time, Pallas kernels for 7%

profile of v7, /device:TPU:1, one launch (start us, length us, event | category | flops | bytes accessed | tf_op | source)
XLA Modules:
  0.0 151.7 jit_solution(8794336820223181255)
XLA Ops:
  1.3 2.6 %shard_map.148 = bf16[16,128,384]{2,1,0:T(8,128)(2,1)} custom-call(s32[1]{0:T(128)S(6)} %copy.31.step_ref.refs_0_, bf16[96,2304]{1,0:T(8,128)(2,1)} %refs_0_.3, bf16[48,1536]{1,0:T(8,128)(2,1)} %refs_1_.1, bf16[16,4608]{1,0:T(8,128)(2,1)} %refs_2_.1, bf16[4,1536]{1,0:T(4,128)(2,1)} %refs_3_.1, bf16[48,64]{1,0:T(8,128)(2,1)} %refs_4_.1), custom_call_target="tpu_custom_call" | custom-call | tf_op jit(solution)/shard_map/pallas_call | solution.py:576
  3.9 0.0 copy-start.9
  3.9 0.0 copy-start.10
  3.9 0.0 copy-start.12
  3.9 0.0 copy-start.13
  3.9 0.0 copy-start.8
  3.9 8.8 %all-to-all-start = ((bf16[16,128,384]{2,1,0:T(8,128)(2,1)}), bf16[16,128,384]{2,1,0:T(8,128)(2,1)S(1)}, u32[]{:S(2)}, u32[]{:S(2)}) async-start(bf16[16,128,384]{2,1,0:T(8,128)(2,1)} %shard_map.148), calls=%async_computation | async-start | bytes 3145728 | tf_op jit(solution)/shard_map/all_to_all | solution.py:654
  12.7 0.0 copy-done.9
  12.8 0.0 copy-done.10
  12.8 0.6 broadcast_in_dim.6.refs_14_.refs_12_
  13.4 0.0 copy-done.12
  13.4 0.6 broadcast_in_dim_tile.6.refs_11_.refs_17_
  14.0 0.0 copy-done.13
  14.0 0.7 broadcast_in_dim_tile.7.refs_12_.refs_18_
  14.7 0.0 copy-done.8
  14.7 1.6 %fusion.refs_9_.refs_19_ = f32[256,1536]{1,0:T(8,128)} fusion(bf16[64,1536]{1,0:T(8,128)(2,1)S(1)} %copy-done.8, bf16[8,8,2,128]{3,2,1,0:T(2,128)(2,1)S(1)} %bitcast.24), kind=kOutput, calls=%fused_computation.1 | convolution fusion | flops 50331648 | bytes 1802240 | tf_op jit(solution)/shard_map/dot_general | solution.py:655
  16.2 32.4 %all-to-all-done.refs_1_ = bf16[16,128,384]{2,1,0:T(8,128)(2,1)S(1)} async-done(((bf16[16,128,384]{2,1,0:T(8,128)(2,1)}), bf16[16,128,384]{2,1,0:T(8,128)(2,1)S(1)}, u32[]{:S(2)}, u32[]{:S(2)}) %all-to-all-start) | async-done | bytes 1572896 | tf_op jit(solution)/shard_map/all_to_all | solution.py:654
  48.6 0.0 copy-start
  48.6 0.1 slice.39
  48.8 2.6 %collective-permute-start = (bf16[16,96,384]{2,1,0:T(8,128)(2,1)S(1)}, bf16[16,96,384]{2,1,0:T(8,128)(2,1)S(1)}, u32[]{:S(2)}, u32[]{:S(2)}) collective-permute-start(bf16[16,96,384]{2,1,0:T(8,128)(2,1)S(1)} %slice.39), channel_id=1, source_target_pairs={{8,0},{280,16},{40,32},{312,48},{72,64},{344,80},{104,96},{376,112... | collective-permute-start | bytes 3538952 | tf_op jit(solution)/shard_map/ppermute | solution.py:608
  51.4 2.7 %collective-permute-start.1 = (bf16[16,96,384]{2,1,0:T(8,128)(2,1)S(1)}, bf16[16,96,384]{2,1,0:T(8,128)(2,1)S(1)}, u32[]{:S(2)}, u32[]{:S(2)}) collective-permute-start(bf16[16,96,384]{2,1,0:T(8,128)(2,1)S(1)} %slice.39), channel_id=1, source_target_pairs={{1,0},{23,16},{33,32},{55,48},{65,64},{87,80},{97,96},{119,112},{1... | collective-permute-start | bytes 3538952 | tf_op jit(solution)/shard_map/ppermute | solution.py:608
  54.2 11.2 %collective-permute-start.2 = (bf16[16,96,384]{2,1,0:T(8,128)(2,1)S(1)}, bf16[16,96,384]{2,1,0:T(8,128)(2,1)S(1)}, u32[]{:S(2)}, u32[]{:S(2)}) collective-permute-start(bf16[16,96,384]{2,1,0:T(8,128)(2,1)S(1)} %slice.39), channel_id=1, source_target_pairs={{224,0},{48,16},{0,32},{80,48},{32,64},{112,80},{64,96},{144,112},... | collective-permute-start | bytes 3538952 | tf_op jit(solution)/shard_map/ppermute | solution.py:608
  65.4 0.3 add_reduce_fusion
  65.8 0.1 fusion.3
  65.9 0.1 fusion.5
  66.1 14.0 %all_to_all.20.refs_10_ = f32[16,2,384]{2,1,0:T(2,128)} all-to-all(f32[16,2,384]{2,1,0:T(2,128)S(1)} %copy.20), channel_id=1, replica_groups=mesh['dp'=32,'fsdp'=16] {'fsdp'}, dimensions={0} | all-to-all | bytes 98304 | tf_op jit(solution)/shard_map/all_to_all | solution.py:668
  80.1 0.0 collective-permute-done.refs_2_
  80.1 0.0 copy-start.2
  80.1 0.0 collective-permute-done.1.refs_3_
  80.1 0.0 copy-done
  80.1 0.0 copy-start.3
  80.1 1.9 %collective-permute-start.3 = (bf16[16,128,384]{2,1,0:T(8,128)(2,1)S(1)}, bf16[16,128,384]{2,1,0:T(8,128)(2,1)S(1)}, u32[]{:S(2)}, u32[]{:S(2)}) collective-permute-start(bf16[16,128,384]{2,1,0:T(8,128)(2,1)S(1)} %all-to-all-done.refs_1_), channel_id=1, source_target_pairs={{0,16},{16,0},{32,48},{48,32},{64,80},{80,64},{96,112},{112,96},{1... | collective-permute-start | bytes 4718600 | tf_op jit(solution)/shard_map/ppermute | solution.py:613
  82.0 2.4 %collective-permute-start.4 = (bf16[16,96,384]{2,1,0:T(8,128)(2,1)S(1)}, bf16[16,96,384]{2,1,0:T(8,128)(2,1)S(1)}, u32[]{:S(2)}, u32[]{:S(2)}) collective-permute-start(bf16[16,96,384]{2,1,0:T(8,128)(2,1)S(1)} %collective-permute-done.refs_2_), channel_id=1, source_target_pairs={{0,16},{16,0},{32,48},{48,32},{64,80},{80,64},{96,112},{112,96},{1... | collective-permute-start | bytes 3538952 | tf_op jit(solution)/shard_map/ppermute | solution.py:613
  84.5 1.9 %collective-permute-start.5 = (bf16[16,96,384]{2,1,0:T(8,128)(2,1)S(1)}, bf16[16,96,384]{2,1,0:T(8,128)(2,1)S(1)}, u32[]{:S(2)}, u32[]{:S(2)}) collective-permute-start(bf16[16,96,384]{2,1,0:T(8,128)(2,1)S(1)} %collective-permute-done.1.refs_3_), channel_id=1, source_target_pairs={{0,16},{16,0},{32,48},{48,32},{64,80},{80,64},{96,112},{112,96},{1... | collective-permute-start | bytes 3538952 | tf_op jit(solution)/shard_map/ppermute | solution.py:613
  86.4 0.0 collective-permute-done.2.refs_4_
  86.4 0.0 copy-start.4
  86.4 2.6 %collective-permute-start.6 = (bf16[16,96,384]{2,1,0:T(8,128)(2,1)S(1)}, bf16[16,96,384]{2,1,0:T(8,128)(2,1)S(1)}, u32[]{:S(2)}, u32[]{:S(2)}) collective-permute-start(bf16[16,96,384]{2,1,0:T(8,128)(2,1)S(1)} %collective-permute-done.2.refs_4_), channel_id=1, source_target_pairs={{0,16},{16,0},{32,48},{48,32},{64,80},{80,64},{96,112},{112,96},{1... | collective-permute-start | bytes 3538952 | tf_op jit(solution)/shard_map/ppermute | solution.py:613
  89.0 0.0 collective-permute-done.4.refs_6_
  89.0 0.0 copy-start.5
  89.0 0.2 collective-permute-done.5.refs_7_
  89.2 0.0 copy-start.6
  89.2 2.1 %collective-permute-done.6.refs_8_ = bf16[16,96,384]{2,1,0:T(8,128)(2,1)S(1)} collective-permute-done((bf16[16,96,384]{2,1,0:T(8,128)(2,1)S(1)}, bf16[16,96,384]{2,1,0:T(8,128)(2,1)S(1)}, u32[]{:S(2)}, u32[]{:S(2)}) %collective-permute-start.6) | collective-permute-done | bytes 1179680 | tf_op jit(solution)/shard_map/ppermute | solution.py:613
  91.3 0.0 copy-start.7
  91.3 0.0 collective-permute-done.3.refs_5_
  91.3 0.0 copy-done.2
  91.3 0.0 copy-start.1
  91.3 0.0 copy-done.3
  91.3 0.0 copy-done.4
  91.3 0.0 copy-done.5
  91.3 0.0 copy-done.6
  91.3 1.0 copy-done.7
  92.4 0.4 copy-done.1
  92.8 19.9 %shard_map.149 = (f32[128,64]{1,0:T(8,128)}, bf16[2,16,8,640]{3,2,1,0:T(8,128)(2,1)}, f32[128,1536]{1,0:T(8,128)}, f32[6,256,128]{2,1,0:T(8,128)}, f32[4,6,128,1...) custom-call(s32[1]{0:T(128)S(6)} %copy.31.step_ref.refs_0_, bf16[16,128,384]{2,1,0:T(8,128)(2,1)} %copy-done, ...), custom_call_target="tpu_custom_call" | custom-call | flops 5000000000 | bytes 20000000 | tf_op jit(solution)/shard_map/pallas_call | solution.py:466
  112.7 3.9 %all-to-all-start.2 = ((bf16[32,8,640]{2,1,0:T(8,128)(2,1)}), bf16[32,8,640]{2,1,0:T(8,128)(2,1)S(1)}, u32[]{:S(2)}, u32[]{:S(2)}) async-start(bf16[32,8,640]{2,1,0:T(8,128)(2,1)} %bitcast.21), calls=%async_computation.2 | async-start | bytes 655360 | tf_op jit(solution)/shard_map/all_to_all | solution.py:690
  116.6 10.8 %shard_map.150 = f32[64,128]{1,0:T(8,128)} custom-call(s32[1]{0:T(128)S(6)} %copy.31.step_ref.refs_0_, bf16[16,128,384]{2,1,0:T(8,128)(2,1)} %copy-done, bf16[16,96,384]{2,1,0:T(8,128)(2,1)} %copy-done.2, bf16[16,96,384]{2,1,0:T(8,128)(2,1)} %copy-done.3, bf16[16,96,384]{2,1,0:T(8,128)(2,1)} %copy-done.4, bf16[16,128,384]{2,1,0:T(8,128)(2,1)} %copy-done.1, ...), custom_call_target="tpu_custom_call" | custom-call | flops 3000000000 | bytes 20000000 | tf_op jit(solution)/shard_map/pallas_call | solution.py:510
  127.4 1.0 all-to-all-done.2
  128.5 0.1 reduce_sum.21
  128.6 17.2 %all_to_all.21 = bf16[16,8,640]{2,1,0:T(8,128)(2,1)S(1)} all-to-all(bf16[16,8,640]{2,1,0:T(8,128)(2,1)S(1)} %broadcast_in_dim.8), channel_id=1, replica_groups={{0,32,64,96,128,160,192,224,256,288,320,352,384,416,448,480},{16,48,80,..., dimensions={0} | all-to-all | bytes 327680 | tf_op jit(solution)/shard_map/all_to_all | solution.py:708
  145.8 4.3 %collective-permute-start.7 = (f32[8,640]{1,0:T(8,128)S(1)}, f32[8,640]{1,0:T(8,128)S(1)}, u32[]{:S(2)}, u32[]{:S(2)}) collective-permute-start(f32[8,640]{1,0:T(8,128)S(1)} %convert_reduce_fusion), channel_id=1, source_target_pairs={{0,16},{16,0},{32,48},{48,32},{64,80},{80,64},{96,112},{112,96},{1... | collective-permute-start | bytes 61448 | tf_op jit(solution)/shard_map/ppermute | solution.py:717
  150.1 0.8 collective-permute-done.7
  150.9 0.1 constant_dynamic-update-slice_fusion.4
  151.0 0.1 constant_dynamic-update-slice_fusion.1
  151.1 0.6 pad_maximum_fusion
  151.7 0.0 copy-done.11
  (16 shorter events, 0.2 us)
Async XLA Ops:
  3.9 8.9 %copy-start.9 = (bf16[1,2,128,64]{2,3,1,0:T(8,128)(2,1)S(1)}, bf16[1,2,128,64]{2,3,1,0:T(8,128)(2,1)}, u32[]{:S(2)}) copy-start(bf16[1,2,128,64]{2,3,1,0:T(8,128)(2,1)} %param.13) | copy-start | bytes 98308
  3.9 8.9 %copy-start.10 = (f32[1536]{0:T(1024)S(1)}, f32[1536]{0:T(1024)}, u32[]{:S(2)}) copy-start(f32[1536]{0:T(1024)} %param.24) | copy-start | bytes 18436
  3.9 9.5 %copy-start.12 = (f32[64]{0:T(128)S(1)}, f32[64]{0:T(128)}, u32[]{:S(2)}) copy-start(f32[64]{0:T(128)} %param.22) | copy-start | bytes 772
  3.9 10.1 %copy-start.13 = (f32[64]{0:T(128)S(1)}, f32[64]{0:T(128)}, u32[]{:S(2)}) copy-start(f32[64]{0:T(128)} %param.23) | copy-start | bytes 772
  3.9 10.8 %copy-start.8 = (bf16[64,1536]{1,0:T(8,128)(2,1)S(1)}, bf16[64,1536]{1,0:T(8,128)(2,1)}, u32[]{:S(2)}) copy-start(bf16[64,1536]{1,0:T(8,128)(2,1)} %refs_20_.1) | copy-start | bytes 589828
  3.9 44.7 %all-to-all-start = ((bf16[16,128,384]{2,1,0:T(8,128)(2,1)}), bf16[16,128,384]{2,1,0:T(8,128)(2,1)S(1)}, u32[]{:S(2)}, u32[]{:S(2)}) async-start(bf16[16,128,384]{2,1,0:T(8,128)(2,1)} %shard_map.148), calls=%async_computation | async-start | bytes 3145728 | tf_op jit(solution)/shard_map/all_to_all | solution.py:654
  48.6 31.5 %copy-start = (bf16[16,128,384]{2,1,0:T(8,128)(2,1)}, bf16[16,128,384]{2,1,0:T(8,128)(2,1)S(1)}, u32[]{:S(2)}) copy-start(bf16[16,128,384]{2,1,0:T(8,128)(2,1)S(1)} %all-to-all-done.refs_1_) | copy-start | bytes 4718596
  48.8 31.3 %collective-permute-start = (bf16[16,96,384]{2,1,0:T(8,128)(2,1)S(1)}, bf16[16,96,384]{2,1,0:T(8,128)(2,1)S(1)}, u32[]{:S(2)}, u32[]{:S(2)}) collective-permute-start(bf16[16,96,384]{2,1,0:T(8,128)(2,1)S(1)} %slice.39), channel_id=1, source_target_pairs={{8,0},{280,16},{40,32},{312,48},{72,64},{344,80},{104,96},{376,112... | collective-permute-start | bytes 3538952 | tf_op jit(solution)/shard_map/ppermute | solution.py:608
  51.4 28.7 %collective-permute-start.1 = (bf16[16,96,384]{2,1,0:T(8,128)(2,1)S(1)}, bf16[16,96,384]{2,1,0:T(8,128)(2,1)S(1)}, u32[]{:S(2)}, u32[]{:S(2)}) collective-permute-start(bf16[16,96,384]{2,1,0:T(8,128)(2,1)S(1)} %slice.39), channel_id=1, source_target_pairs={{1,0},{23,16},{33,32},{55,48},{65,64},{87,80},{97,96},{119,112},{1... | collective-permute-start | bytes 3538952 | tf_op jit(solution)/shard_map/ppermute | solution.py:608
  54.2 32.2 %collective-permute-start.2 = (bf16[16,96,384]{2,1,0:T(8,128)(2,1)S(1)}, bf16[16,96,384]{2,1,0:T(8,128)(2,1)S(1)}, u32[]{:S(2)}, u32[]{:S(2)}) collective-permute-start(bf16[16,96,384]{2,1,0:T(8,128)(2,1)S(1)} %slice.39), channel_id=1, source_target_pairs={{224,0},{48,16},{0,32},{80,48},{32,64},{112,80},{64,96},{144,112},... | collective-permute-start | bytes 3538952 | tf_op jit(solution)/shard_map/ppermute | solution.py:608
  80.1 11.2 %copy-start.2 = (bf16[16,96,384]{2,1,0:T(8,128)(2,1)}, bf16[16,96,384]{2,1,0:T(8,128)(2,1)S(1)}, u32[]{:S(2)}) copy-start(bf16[16,96,384]{2,1,0:T(8,128)(2,1)S(1)} %collective-permute-done.refs_2_) | copy-start | bytes 3538948
  80.1 11.2 %copy-start.3 = (bf16[16,96,384]{2,1,0:T(8,128)(2,1)}, bf16[16,96,384]{2,1,0:T(8,128)(2,1)S(1)}, u32[]{:S(2)}) copy-start(bf16[16,96,384]{2,1,0:T(8,128)(2,1)S(1)} %collective-permute-done.1.refs_3_) | copy-start | bytes 3538948
  80.1 11.2 %collective-permute-start.3 = (bf16[16,128,384]{2,1,0:T(8,128)(2,1)S(1)}, bf16[16,128,384]{2,1,0:T(8,128)(2,1)S(1)}, u32[]{:S(2)}, u32[]{:S(2)}) collective-permute-start(bf16[16,128,384]{2,1,0:T(8,128)(2,1)S(1)} %all-to-all-done.refs_1_), channel_id=1, source_target_pairs={{0,16},{16,0},{32,48},{48,32},{64,80},{80,64},{96,112},{112,96},{1... | collective-permute-start | bytes 4718600 | tf_op jit(solution)/shard_map/ppermute | solution.py:613
  82.0 7.0 %collective-permute-start.4 = (bf16[16,96,384]{2,1,0:T(8,128)(2,1)S(1)}, bf16[16,96,384]{2,1,0:T(8,128)(2,1)S(1)}, u32[]{:S(2)}, u32[]{:S(2)}) collective-permute-start(bf16[16,96,384]{2,1,0:T(8,128)(2,1)S(1)} %collective-permute-done.refs_2_), channel_id=1, source_target_pairs={{0,16},{16,0},{32,48},{48,32},{64,80},{80,64},{96,112},{112,96},{1... | collective-permute-start | bytes 3538952 | tf_op jit(solution)/shard_map/ppermute | solution.py:613
  84.5 4.7 %collective-permute-start.5 = (bf16[16,96,384]{2,1,0:T(8,128)(2,1)S(1)}, bf16[16,96,384]{2,1,0:T(8,128)(2,1)S(1)}, u32[]{:S(2)}, u32[]{:S(2)}) collective-permute-start(bf16[16,96,384]{2,1,0:T(8,128)(2,1)S(1)} %collective-permute-done.1.refs_3_), channel_id=1, source_target_pairs={{0,16},{16,0},{32,48},{48,32},{64,80},{80,64},{96,112},{112,96},{1... | collective-permute-start | bytes 3538952 | tf_op jit(solution)/shard_map/ppermute | solution.py:613
  86.4 4.9 %copy-start.4 = (bf16[16,96,384]{2,1,0:T(8,128)(2,1)}, bf16[16,96,384]{2,1,0:T(8,128)(2,1)S(1)}, u32[]{:S(2)}) copy-start(bf16[16,96,384]{2,1,0:T(8,128)(2,1)S(1)} %collective-permute-done.2.refs_4_) | copy-start | bytes 3538948
  86.4 4.9 %collective-permute-start.6 = (bf16[16,96,384]{2,1,0:T(8,128)(2,1)S(1)}, bf16[16,96,384]{2,1,0:T(8,128)(2,1)S(1)}, u32[]{:S(2)}, u32[]{:S(2)}) collective-permute-start(bf16[16,96,384]{2,1,0:T(8,128)(2,1)S(1)} %collective-permute-done.2.refs_4_), channel_id=1, source_target_pairs={{0,16},{16,0},{32,48},{48,32},{64,80},{80,64},{96,112},{112,96},{1... | collective-permute-start | bytes 3538952 | tf_op jit(solution)/shard_map/ppermute | solution.py:613
  89.0 2.3 %copy-start.5 = (bf16[16,96,384]{2,1,0:T(8,128)(2,1)}, bf16[16,96,384]{2,1,0:T(8,128)(2,1)S(1)}, u32[]{:S(2)}) copy-start(bf16[16,96,384]{2,1,0:T(8,128)(2,1)S(1)} %collective-permute-done.4.refs_6_) | copy-start | bytes 3538948
  89.2 2.1 %copy-start.6 = (bf16[16,96,384]{2,1,0:T(8,128)(2,1)}, bf16[16,96,384]{2,1,0:T(8,128)(2,1)S(1)}, u32[]{:S(2)}) copy-start(bf16[16,96,384]{2,1,0:T(8,128)(2,1)S(1)} %collective-permute-done.5.refs_7_) | copy-start | bytes 3538948
  91.3 1.1 copy-start.7
  91.3 1.5 copy-start.1
  112.7 15.7 %all-to-all-start.2 = ((bf16[32,8,640]{2,1,0:T(8,128)(2,1)}), bf16[32,8,640]{2,1,0:T(8,128)(2,1)S(1)}, u32[]{:S(2)}, u32[]{:S(2)}) async-start(bf16[32,8,640]{2,1,0:T(8,128)(2,1)} %bitcast.21), calls=%async_computation.2 | async-start | bytes 655360 | tf_op jit(solution)/shard_map/all_to_all | solution.py:690
  145.8 5.1 %collective-permute-start.7 = (f32[8,640]{1,0:T(8,128)S(1)}, f32[8,640]{1,0:T(8,128)S(1)}, u32[]{:S(2)}, u32[]{:S(2)}) collective-permute-start(f32[8,640]{1,0:T(8,128)S(1)} %convert_reduce_fusion), channel_id=1, source_target_pairs={{0,16},{16,0},{32,48},{48,32},{64,80},{80,64},{96,112},{112,96},{1... | collective-permute-start | bytes 61448 | tf_op jit(solution)/shard_map/ppermute | solution.py:717
  151.1 0.6 copy-start.11
